TPU v7x, 128 devices: a whole 4x4x4 slice. The times are simulated.
128 devices in a mesh: dp: 16 (over x, z_lo, core), proto: 8 (over z_hi, y).
Axes of the slice: x: 4, y: 4, z: 4 (z_hi: 2, z_lo: 2; z = z_hi * 2 + z_lo), core: 2. Of those that a mesh axis runs over, the one named last changes fastest.
Arguments:
- teacher_emb: bfloat16 [8192, 256], P('dp'), may hold values from -8 to 8
- student_emb: bfloat16 [8192, 256], P('dp'), may hold values from -8 to 8
- teacher_protos: bfloat16 [256, 65536], P(None, 'proto'), may hold values from -8 to 8
- student_protos: bfloat16 [256, 65536], P(None, 'proto'), may hold values from -8 to 8
Outputs:
- grad_embeddings: float32 [8192, 256], P(('dp', 'proto'))
- grad_prototypes: float32 [256, 65536], P('dp', 'proto')
- loss: float32 [], replicated
All inputs are finite; a program needn't handle non-finite values.
Results may differ from a plain program's by a relative error of at most 0.0068.
Values sent between devices are 32-bit elements; how exact they have to be, the bound alone decides.
No kernel may reach another device: no remote copies, remote signals or barrier semaphores. Data moves between devices by JAX's collectives and lax.ppermute only.
A program may use at most 128 MiB of HBM per device.

v0:
```python
import jax
import jax.numpy as jnp
from jax import lax
from jax.sharding import PartitionSpec as P

ITERS = 3


teacher_temp = 0.07
student_temp = 0.1
norm_eps = 1e-06


def unit_rows(values):
    wide = values.astype(jnp.float32)
    norms = jnp.sqrt(jnp.sum(wide * wide, axis=1, keepdims=True) + norm_eps)
    return (wide / norms, norms)


def unit_cols(values):
    wide = values.astype(jnp.float32)
    norms = jnp.sqrt(jnp.sum(wide * wide, axis=0, keepdims=True) + norm_eps)
    return (wide / norms, norms)


def column_total(partial_sum):
    return lax.psum(partial_sum, "dp")


def row_total(partial_sum):
    return lax.psum(partial_sum, "proto")


def on_device(teacher_emb, student_emb, teacher_protos, student_protos):
    row_count = teacher_emb.shape[0]
    local_protos = teacher_protos.shape[1]
    width = teacher_emb.shape[1]
    batch_total = row_count * lax.axis_size("dp")
    proto_total = local_protos * lax.axis_size("proto")
    t_unit, t_norm = unit_rows(teacher_emb)
    t_round = t_unit.astype(jnp.bfloat16)
    s_unit, s_norm = unit_rows(student_emb)
    s_round = s_unit.astype(jnp.bfloat16)
    t_dir, t_vnorm = unit_cols(teacher_protos)
    t_wn = t_dir.astype(jnp.bfloat16)
    s_dir, v_norm = unit_cols(student_protos)
    s_wn = s_dir.astype(jnp.bfloat16)
    s_wide = s_wn.astype(jnp.float32)
    teacher_exp = jnp.exp(jnp.dot(t_round, t_wn, preferred_element_type=jnp.float32) / teacher_temp)
    cosine = jnp.dot(s_round, s_wn, preferred_element_type=jnp.float32)
    logits = cosine / student_temp
    student_exp = jnp.exp(logits)
    student_part = jnp.sum(student_exp, axis=1)
    row_scale = jnp.ones((row_count,), jnp.float32)
    column_scale = jnp.zeros((local_protos,), jnp.float32)
    row_sum = jnp.ones((row_count,), jnp.float32)
    for sweep in range(ITERS):
        column_sum = column_total(jnp.sum(teacher_exp * row_scale[:, None], axis=0))
        column_scale = 1.0 / (proto_total * column_sum)
        row_part = jnp.sum(teacher_exp * column_scale[None, :], axis=1)
        row_sum = row_total(row_part)
        row_scale = 1.0 / (batch_total * row_sum)
    totals = lax.psum(student_part, "proto")
    targets = teacher_exp * column_scale[None, :] / row_sum[:, None]
    log_total = jnp.log(totals)
    loss_part = jnp.sum(targets * (log_total[:, None] - logits))
    loss = lax.psum(loss_part, ("dp", "proto")) / batch_total
    grad_logits = (student_exp / totals[:, None] - targets).astype(jnp.bfloat16)
    own_rows = row_count // lax.axis_size("proto")
    piece = grad_logits
    product = lax.dot_general(
        piece, s_wn, (((1,), (1,)), ((), ())), preferred_element_type=jnp.float32
    )
    grad_unit = lax.psum_scatter(product / student_temp, "proto", scatter_dimension=0, tiled=True)
    row_first = lax.axis_index("proto") * own_rows
    own_unit = lax.dynamic_slice_in_dim(s_unit, row_first, own_rows, 0)
    own_norm = lax.dynamic_slice_in_dim(s_norm, row_first, own_rows, 0)
    grad_embeddings = (
        grad_unit - own_unit * jnp.sum(own_unit * grad_unit, axis=1, keepdims=True)
    ) / own_norm
    own_width = width // lax.axis_size("dp")
    width_first = lax.axis_index("dp") * own_width
    dots_part = (
        jnp.sum(cosine * grad_logits.astype(jnp.float32), axis=0, keepdims=True) / student_temp
    )
    piece = s_round
    product = lax.dot_general(
        piece, grad_logits, (((0,), (0,)), ((), ())), preferred_element_type=jnp.float32
    )
    grad_rows = lax.psum_scatter(product / student_temp, "dp", scatter_dimension=0, tiled=True)
    dots = lax.psum(dots_part, "dp")
    own_dir = lax.dynamic_slice_in_dim(s_wide, width_first, own_width, 0)
    grad_prototypes = (grad_rows - own_dir * dots) / v_norm
    return (grad_embeddings, grad_prototypes, loss)


def solution(mesh):
    placed = (P("dp", None), P("dp", None), P(None, "proto"), P(None, "proto"))
    return jax.shard_map(
        on_device,
        mesh=mesh,
        in_specs=placed,
        out_specs=(P(("dp", "proto"), None), P("dp", "proto"), P()),
        check_vma=False,
    )
```

profile of v0, /device:TPU:1, one launch (start us, length us, event | category | flops | bytes accessed | tf_op | source)
XLA Modules:
  0.0 495.6 jit_solution(12219376132778684476)
XLA Ops:
  7.2 3.1 fusion.2
  10.3 1.1 fusion.7
  11.4 11.6 %fusion.14 = (f32[8192]{0:T(1024)S(1)}, f32[512,8192]{1,0:T(8,128)}) fusion(bf16[256,8192]{1,0:T(8,128)(2,1)} %param.6, f32[8192]{0:T(1024)S(1)} %add_sqrt_fusion, bf16[512,256]{1,0:T(8,128)(2,1)} %param.4, f32[512]{0:T(512)S(1)} %add_sqrt_fusion.2), kind=kOutput, calls=%fused_computation.46 | convolution fusion | flops 2162548736 | bytes 21301248 | tf_op jit(solution)/shard_map/dot_general | solution.py:49
  23.0 53.4 %psum.64 = f32[8192]{0:T(1024)S(1)} all-reduce(f32[8192]{0:T(1024)S(1)} %get-tuple-element.10), channel_id=1, replica_groups=mesh['dp'=16,'proto'=8] {'dp'}, use_global_device_ids=true, to_apply=%region_7.0 | all-reduce | flops 8192 | bytes 65536 | tf_op jit(solution)/shard_map/psum | solution.py:27
  76.4 7.3 %multiply_reduce_fusion.5 = f32[512]{0:T(512)S(1)} fusion(f32[512,8192]{1,0:T(8,128)} %get-tuple-element.11, f32[8192]{0:T(1024)S(1)} %multiply_divide_fusion.3), kind=kLoop, calls=%fused_computation.6 | loop fusion | flops 8388096 | bytes 16812032 | tf_op jit(solution)/shard_map/reduce_sum | solution.py:60
  83.7 21.2 %psum.65 = f32[512]{0:T(512)S(1)} all-reduce(f32[512]{0:T(512)S(1)} %multiply_reduce_fusion.5), channel_id=1, replica_groups=mesh['dp'=16,'proto'=8] {'proto'}, use_global_device_ids=true, to_apply=%region_9.0 | all-reduce | flops 512 | bytes 4096 | tf_op jit(solution)/shard_map/psum | solution.py:31
  104.9 8.3 %multiply_reduce_fusion.4 = f32[8192]{0:T(1024)S(1)} fusion(f32[512,8192]{1,0:T(8,128)} %get-tuple-element.11, f32[512]{0:T(512)S(1)} %multiply_divide_fusion.5), kind=kLoop, calls=%fused_computation.5 | loop fusion | flops 8380416 | bytes 16812032 | tf_op jit(solution)/shard_map/reduce_sum | solution.py:58
  113.2 56.7 %psum.66 = f32[8192]{0:T(1024)S(1)} all-reduce(f32[8192]{0:T(1024)S(1)} %multiply_reduce_fusion.4), channel_id=1, replica_groups=mesh['dp'=16,'proto'=8] {'dp'}, use_global_device_ids=true, to_apply=%region_11.0 | all-reduce | flops 8192 | bytes 65536 | tf_op jit(solution)/shard_map/psum | solution.py:27
  169.9 7.3 %multiply_reduce_fusion.3 = f32[512]{0:T(512)S(1)} fusion(f32[512,8192]{1,0:T(8,128)} %get-tuple-element.11, f32[8192]{0:T(1024)S(1)} %multiply_divide_fusion.2), kind=kLoop, calls=%fused_computation.4 | loop fusion | flops 8388096 | bytes 16812032 | tf_op jit(solution)/shard_map/reduce_sum | solution.py:60
  177.2 15.7 %psum.67 = f32[512]{0:T(512)S(1)} all-reduce(f32[512]{0:T(512)S(1)} %multiply_reduce_fusion.3), channel_id=1, replica_groups=mesh['dp'=16,'proto'=8] {'proto'}, use_global_device_ids=true, to_apply=%region_13.0 | all-reduce | flops 512 | bytes 4096 | tf_op jit(solution)/shard_map/psum | solution.py:31
  192.9 8.3 %multiply_reduce_fusion.2 = f32[8192]{0:T(1024)S(1)} fusion(f32[512,8192]{1,0:T(8,128)} %get-tuple-element.11, f32[512]{0:T(512)S(1)} %multiply_divide_fusion.4), kind=kLoop, calls=%fused_computation.3 | loop fusion | flops 8380416 | bytes 16812032 | tf_op jit(solution)/shard_map/reduce_sum | solution.py:58
  201.2 56.5 %psum.68 = f32[8192]{0:T(1024)S(1)} all-reduce(f32[8192]{0:T(1024)S(1)} %multiply_reduce_fusion.2), channel_id=1, replica_groups=mesh['dp'=16,'proto'=8] {'dp'}, use_global_device_ids=true, to_apply=%region_15.0 | all-reduce | flops 8192 | bytes 65536 | tf_op jit(solution)/shard_map/psum | solution.py:27
  257.7 7.4 %multiply_reduce_fusion.6 = f32[512]{0:T(512)S(1)} fusion(f32[512,8192]{1,0:T(8,128)} %get-tuple-element.11, f32[8192]{0:T(1024)S(1)} %multiply_divide_fusion.1), kind=kLoop, calls=%fused_computation.9 | loop fusion | flops 8388096 | bytes 16812032 | tf_op jit(solution)/shard_map/reduce_sum | solution.py:60
  265.1 0.9 fusion
  266.0 1.0 fusion.1
  267.0 0.1 fusion.6
  267.2 1.9 copy-done.1
  269.1 7.4 %exponential_reduce_fusion = (f32[512]{0:T(512)S(1)}, f32[512,8192]{1,0:T(8,128)}) fusion(bf16[256,8192]{1,0:T(8,128)(2,1)S(1)} %fusion.1, f32[512]{0:T(512)S(1)} %add_sqrt_fusion.3, bf16[512,256]{1,0:T(8,128)(2,1)S(1)} %copy-done.4), kind=kOutput, calls=%fused_computation.10 | convolution fusion | flops 2156264960 | bytes 21237760 | tf_op jit(solution)/shard_map/dot_general | solution.py:50
  276.5 17.4 %all-reduce = (f32[512]{0:T(512)S(1)}, f32[512]{0:T(512)S(1)}) all-reduce(f32[512]{0:T(512)S(1)} %get-tuple-element.8, f32[512]{0:T(512)S(1)} %multiply_reduce_fusion.6), channel_id=1, replica_groups=mesh['dp'=16,'proto'=8] {'proto'}, use_global_device_ids=true, to_apply=%region_3.0 | all-reduce | flops 1024 | bytes 8192 | tf_op jit(solution)/shard_map/psum | solution.py:63
  293.9 14.3 %multiply_reduce_fusion = (f32[]{:T(128)}, f32[8192]{0:T(1024)S(1)}, bf16[512,8192]{1,0:T(8,128)(2,1)S(1)}) fusion(f32[512,8192]{1,0:T(8,128)} %get-tuple-element.9, f32[512]{0:T(512)S(1)} %log.3, f32[512]{0:T(512)S(1)} %get-tuple-element.6, f32[512,8192]{1,0:T(8,128)} %get-tuple-element.11, f32[8192]{0:T(1024)S(1)} %multiply_divide_fusion.1, ...), kind=kLoop, calls=%fused_computation | loop fusion | flops 50323456 | bytes 42014724 | tf_op jit(solution)/shard_map/reduce_sum | solution.py:66
  308.2 3.2 copy-done
  311.4 3.2 convolution_multiply_fusion.1
  314.6 0.0 reduce-scatter.5.cloned.1.call-start
  314.6 9.1 %convolution_multiply_fusion = f32[256,8192]{1,0:T(8,128)} fusion(bf16[512,8192]{1,0:T(8,128)(2,1)} %copy-done, bf16[512,256]{1,0:T(8,128)(2,1)S(1)} %copy-done.4, f32[512]{0:T(512)S(1)} %add_sqrt_fusion.3), kind=kOutput, calls=%fused_computation.11 | convolution fusion | flops 2149974016 | bytes 17041408 | tf_op jit(solution)/shard_map/dot_general | solution.py:87
  323.8 70.3 %psum.71 = f32[]{:T(128)} all-reduce(f32[]{:T(128)} %get-tuple-element.3), channel_id=1, replica_groups=mesh['dp'=16,'proto'=8] {'dp','proto'}, use_global_device_ids=true, to_apply=%region_24.0 | all-reduce | flops 1 | bytes 8 | tf_op jit(solution)/shard_map/psum | solution.py:67
  394.0 0.1 dynamic-slice.3
  394.8 50.9 %psum.70 = f32[8192]{0:T(1024)S(1)} all-reduce(f32[8192]{0:T(1024)S(1)} %broadcast_multiply_fusion), channel_id=1, replica_groups=mesh['dp'=16,'proto'=8] {'dp'}, use_global_device_ids=true, to_apply=%region_22.0 | all-reduce | flops 8192 | bytes 65536 | tf_op jit(solution)/shard_map/psum | solution.py:91
  445.7 0.1 convert_divide_fusion.3
  445.8 1.0 multiply_reduce_fusion.7
  446.8 1.6 subtract_divide_fusion.1
  448.3 37.2 %reduce-scatter.5.cloned.1.call-done = f32[16,8192]{1,0:T(8,128)} async-done(((f32[256,8192]{1,0:T(8,128)}), f32[16,8192]{1,0:T(8,128)}) %reduce-scatter.5.cloned.1.call-update) | async-done | bytes 524304 | tf_op jit(solution)/shard_map/reduce_scatter | solution.py:90
  485.6 2.0 subtract_divide_fusion
  (23 shorter events, 0.2 us)
Async XLA Ops:
  7.2 438.7 %reduce-scatter.3.cloned.1.call-start = ((), (), s32[]{:S(2)}) async-start(), calls=%async_computation.2 | async-start | bytes 589824 | tf_op jit(solution)/shard_map/reduce_scatter | solution.py:74
  201.2 65.8 %copy-start.4 = (bf16[512,256]{1,0:T(8,128)(2,1)S(1)}, bf16[512,256]{1,0:T(8,128)(2,1)}, u32[]{:S(2)}) copy-start(bf16[512,256]{1,0:T(8,128)(2,1)} %param.5) | copy-start | bytes 786436
  257.7 7.4 %copy-start.3 = (bf16[256,8192]{1,0:T(8,128)(2,1)S(1)}, bf16[256,8192]{1,0:T(8,128)(2,1)}, u32[]{:S(2)}) copy-start(bf16[256,8192]{1,0:T(8,128)(2,1)} %param.7) | copy-start | bytes 12582916
  267.0 2.0 copy-start.1
  293.9 17.5 %copy-start.2 = (bf16[256,8192]{1,0:T(8,128)(2,1)S(1)}, bf16[256,8192]{1,0:T(8,128)(2,1)}, u32[]{:S(2)}) copy-start(bf16[256,8192]{1,0:T(8,128)(2,1)} %copy-done.1) | copy-start | bytes 12582916
  308.2 3.2 copy-start
  314.6 171.0 %reduce-scatter.5.cloned.1.call-start = ((), (), s32[]{:S(2)}) async-start(), calls=%async_computation.3 | async-start | bytes 8912896 | tf_op jit(solution)/shard_map/reduce_scatter | solution.py:90
Sparse Core Ops, SparseCore 0:
  314.7 69.8 reduce-scatter.2
  387.1 98.4 reduce-scatter.4
where the time goes:
time: 497 us; the launch traced here: 496 us
  blocking collectives  342 us (69%)
  other arithmetic  63.8 us (13%)
  waiting for transfers between devices  37.3 us (8%)
  matrix products  31.3 us (6%)
  between operations  16 us (3%)
  local copies, waits for them, and re-layouts  5.18 us (1%)
    psum x3, blocking collectives, column_total(): return lax.psum(partial_sum, 'dp')  167 us
    psum x1, blocking collectives, on_device(): loss = lax.psum(loss_part, ('dp', 'proto')) / batch_total  70.3 us
    psum x1, blocking collectives, on_device(): dots = lax.psum(dots_part, 'dp')  50.9 us
    reduce_scatter x1, waiting for transfers between devices, on_device(): lax.psum_scatter(product / student_temp, 'dp', scatter_dimension=0, tiled...  37.2 us
    psum x2, blocking collectives, row_total(): return lax.psum(partial_sum, 'proto')  36.9 us
    reduce_sum x3, other arithmetic, on_device(): row_part = jnp.sum(teacher_exp * column_scale[None, :], axis=1)  22 us
    psum x1, blocking collectives, on_device(): totals = lax.psum(student_part, 'proto')  17.4 us
    reduce_sum x2, other arithmetic, on_device(): column_sum = column_total(jnp.sum(teacher_exp * row_scale[:, None], axis=0))  16.6 us
  transfers between devices with their start and end apart: 2, of which 1 were waited for; matrix products, arithmetic and copies ran while one was open for 2% of the time, Pallas kernels for 0%

commit v1 on v0

v1 whole, which is shorter than its diff:
```python
import math

import jax
import jax.numpy as jnp
from jax import lax
from jax.experimental import pallas as pl
from jax.experimental.pallas import tpu as pltpu
from jax.sharding import Mesh
from jax.sharding import PartitionSpec as P

teacher_temp = 0.07
student_temp = 0.1
norm_eps = 1e-06
log2_e = math.log2(math.e)
teacher_rate = log2_e / teacher_temp
student_rate = log2_e / student_temp

BF16 = jnp.bfloat16
F32 = jnp.float32
LANES = 128
MIB = 1 << 20


def params(mib):
    return pltpu.CompilerParams(vmem_limit_bytes=mib * MIB)


def unit_rows(wide):
    norms = jnp.sqrt(jnp.sum(wide * wide, axis=1, keepdims=True) + norm_eps)
    return wide / norms, norms


def unit_cols(wide):
    norms = jnp.sqrt(jnp.sum(wide * wide, axis=0, keepdims=True) + norm_eps)
    return (wide * (1.0 / norms)).astype(BF16), norms


def dot_rows(left, right):
    return lax.dot_general(left, right, (((1,), (1,)), ((), ())), preferred_element_type=F32)


def dot_cols(left, right):
    return lax.dot_general(left, right, (((0,), (0,)), ((), ())), preferred_element_type=F32)


def dot(left, right):
    return jnp.dot(left, right, preferred_element_type=F32)


def fold_lanes(values):
    total = values[:, :LANES]
    for first in range(LANES, values.shape[1], LANES):
        total = total + values[:, first : first + LANES]
    return total


def row_to_lanes(values):
    return jnp.sum(values.T, axis=0, keepdims=True)


def lanes_to_rows(values):
    return jnp.broadcast_to(values, (LANES, values.shape[1])).T


def place_pair(scratch, core, own, other):
    rows = own.shape[0]
    scratch[pl.ds(pl.multiple_of(core * rows, rows), rows), :] = own
    scratch[pl.ds(pl.multiple_of((1 - core) * rows, rows), rows), :] = other


def teacher_kernel(place, own, other, protos, expo, col_part, unit):
    @pl.when(pl.program_id(0) == 0)
    def _():
        first = unit_rows(own[...].astype(F32))[0].astype(BF16)
        second = unit_rows(other[...])[0].astype(BF16)
        place_pair(unit, place[0], first, second)

    directions, _ = unit_cols(protos[...].astype(F32))
    values = jnp.exp2(dot(unit[...], directions) * teacher_rate)
    expo[...] = values.astype(BF16)
    total = jnp.sum(values, axis=0, keepdims=True)
    col_part[...] = jnp.broadcast_to(total[None], col_part.shape)


def teacher_call(place, own, both, protos, copies, blocks=8):
    rows, width = own.shape
    cols = protos.shape[1] // 2
    step = cols // blocks
    return pl.pallas_call(
        teacher_kernel,
        grid_spec=pltpu.PrefetchScalarGridSpec(
            num_scalar_prefetch=1,
            grid=(blocks,),
            in_specs=[
                pl.BlockSpec((rows, width), lambda j, place: (0, 0)),
                pl.BlockSpec((rows, width), lambda j, place: (0, 0)),
                pl.BlockSpec((width, step), lambda j, place: (0, place[0] * blocks + j)),
            ],
            out_specs=[
                pl.BlockSpec((2 * rows, step), lambda j, place: (0, j)),
                pl.BlockSpec((copies, 1, step), lambda j, place: (0, 0, j)),
            ],
            scratch_shapes=[pltpu.VMEM((2 * rows, width), BF16)],
        ),
        out_shape=[
            jax.ShapeDtypeStruct((2 * rows, cols), BF16),
            jax.ShapeDtypeStruct((copies, 1, cols), F32),
        ],
        compiler_params=params(40),
        cost_estimate=pl.CostEstimate(
            flops=4 * rows * cols * width,
            bytes_accessed=2 * 2 * rows * cols + 2 * width * cols,
            transcendentals=2 * rows * cols,
        ),
        name="teacher_expo",
    )(place, own, both, protos)


def student_kernel(place, own, other, protos, mixed, total_part, dirs, round_out, unit, sums):
    step = pl.program_id(0)

    @pl.when(step == 0)
    def _():
        first = unit_rows(own[...].astype(F32))[0].astype(BF16)
        second = unit_rows(other[...])[0].astype(BF16)
        place_pair(unit, place[0], first, second)
        round_out[...] = unit[...]
        sums[...] = jnp.zeros_like(sums)
        mixed[...] = jnp.zeros_like(mixed)

    directions, _ = unit_cols(protos[...].astype(F32))
    dirs[...] = directions
    values = jnp.exp2(dot(unit[...], directions) * student_rate)
    sums[...] += fold_lanes(values)
    mixed[...] += dot_rows(values.astype(BF16), directions)

    @pl.when(step == pl.num_programs(0) - 1)
    def _():
        total_part[...] = row_to_lanes(sums[...])


def student_call(place, own, both, protos, blocks=8):
    rows, width = own.shape
    cols = protos.shape[1] // 2
    step = cols // blocks
    return pl.pallas_call(
        student_kernel,
        grid_spec=pltpu.PrefetchScalarGridSpec(
            num_scalar_prefetch=1,
            grid=(blocks,),
            in_specs=[
                pl.BlockSpec((rows, width), lambda j, place: (0, 0)),
                pl.BlockSpec((rows, width), lambda j, place: (0, 1)),
                pl.BlockSpec((width, step), lambda j, place: (0, place[0] * blocks + j)),
            ],
            out_specs=[
                pl.BlockSpec((2 * rows, width), lambda j, place: (0, 0)),
                pl.BlockSpec((1, 2 * rows), lambda j, place: (0, 0)),
                pl.BlockSpec((width, step), lambda j, place: (0, j)),
                pl.BlockSpec((2 * rows, width), lambda j, place: (0, 0)),
            ],
            scratch_shapes=[
                pltpu.VMEM((2 * rows, width), BF16),
                pltpu.VMEM((2 * rows, LANES), F32),
            ],
        ),
        out_shape=[
            jax.ShapeDtypeStruct((2 * rows, width), F32),
            jax.ShapeDtypeStruct((1, 2 * rows), F32),
            jax.ShapeDtypeStruct((width, cols), BF16),
            jax.ShapeDtypeStruct((2 * rows, width), BF16),
        ],
        compiler_params=params(40),
        cost_estimate=pl.CostEstimate(
            flops=8 * rows * cols * width,
            bytes_accessed=4 * width * cols + 8 * rows * width,
            transcendentals=2 * rows * cols,
        ),
        name="student_totals",
    )(place, own, both, protos)


def row_sweep_kernel(proto_total, col_parts, expo, row_part):
    scale = 1.0 / (proto_total * jnp.sum(col_parts[...], axis=0))
    rows, cols = expo.shape
    for first in range(0, rows, LANES):
        total = jnp.zeros((LANES, LANES), F32)
        for at in range(0, cols, LANES):
            block = expo[first : first + LANES, at : at + LANES].astype(F32)
            total = total + block * scale[:, at : at + LANES]
        sums = row_to_lanes(total)
        row_part[:, :, first : first + LANES] = jnp.broadcast_to(
            sums[None], (row_part.shape[0], 1, LANES)
        )


def row_sweep(proto_total, col_parts, expo, copies, blocks=4):
    rows, cols = expo.shape
    step = rows // blocks
    return pl.pallas_call(
        lambda *refs: row_sweep_kernel(proto_total, *refs),
        grid=(blocks,),
        in_specs=[
            pl.BlockSpec(col_parts.shape, lambda i: (0, 0, 0)),
            pl.BlockSpec((step, cols), lambda i: (i, 0)),
        ],
        out_specs=pl.BlockSpec((copies, 1, step), lambda i: (0, 0, i)),
        out_shape=jax.ShapeDtypeStruct((copies, 1, rows), F32),
        compiler_params=params(32),
        cost_estimate=pl.CostEstimate(
            flops=2 * rows * cols, bytes_accessed=2 * rows * cols, transcendentals=0
        ),
        name="row_sweep",
    )(col_parts, expo)


def col_sweep_kernel(batch_total, row_parts, expo, col_part, scale):
    @pl.when(pl.program_id(0) == 0)
    def _():
        sums = jnp.sum(row_parts[...], axis=0)
        scale[...] = lanes_to_rows(1.0 / (batch_total * sums))

    rows, cols = expo.shape
    for at in range(0, cols, LANES):
        block = expo[:, at : at + LANES].astype(F32) * scale[...]
        total = jnp.sum(block, axis=0, keepdims=True)
        col_part[:, :, at : at + LANES] = jnp.broadcast_to(
            total[None], (col_part.shape[0], 1, LANES)
        )


def col_sweep(batch_total, row_parts, expo, copies, blocks=4):
    rows, cols = expo.shape
    step = cols // blocks
    return pl.pallas_call(
        lambda *refs: col_sweep_kernel(batch_total, *refs),
        grid=(blocks,),
        in_specs=[
            pl.BlockSpec((row_parts.shape[0], 1, rows), lambda j: (0, 0, 0)),
            pl.BlockSpec((rows, step), lambda j: (0, j)),
        ],
        out_specs=pl.BlockSpec((copies, 1, step), lambda j: (0, 0, j)),
        out_shape=jax.ShapeDtypeStruct((copies, 1, cols), F32),
        scratch_shapes=[pltpu.VMEM((rows, LANES), F32)],
        compiler_params=params(32),
        cost_estimate=pl.CostEstimate(
            flops=2 * rows * cols, bytes_accessed=2 * rows * cols, transcendentals=0
        ),
        name="col_sweep",
    )(row_parts, expo)


def last_sweep_kernel(proto_total, col_parts, expo, dirs, unit, row_part, mixed, scale_out, scaled):
    scale = 1.0 / (proto_total * jnp.sum(col_parts[...], axis=0))

    @pl.when(pl.program_id(0) == 0)
    def _():
        scale_out[...] = scale
        scaled[...] = (dirs[...].astype(F32) * scale).astype(BF16)

    rows, cols = expo.shape
    copies = row_part.shape[0]
    product = dot_rows(expo[...], scaled[...])
    mixed[...] = product
    meet = fold_lanes(product * unit[...].astype(F32))
    row_part[:, 1:2, :] = jnp.broadcast_to(row_to_lanes(meet)[None], (copies, 1, rows))
    for first in range(0, rows, LANES):
        total = jnp.zeros((LANES, LANES), F32)
        for at in range(0, cols, LANES):
            block = expo[first : first + LANES, at : at + LANES].astype(F32)
            total = total + block * scale[:, at : at + LANES]
        sums = row_to_lanes(total)
        row_part[:, 0:1, first : first + LANES] = jnp.broadcast_to(
            sums[None], (copies, 1, LANES)
        )


def last_sweep(proto_total, col_parts, expo, dirs, unit, copies, blocks=4):
    rows, cols = expo.shape
    width = dirs.shape[0]
    step = rows // blocks
    return pl.pallas_call(
        lambda *refs: last_sweep_kernel(proto_total, *refs),
        grid=(blocks,),
        in_specs=[
            pl.BlockSpec((col_parts.shape[0], 1, cols), lambda i: (0, 0, 0)),
            pl.BlockSpec((step, cols), lambda i: (i, 0)),
            pl.BlockSpec((width, cols), lambda i: (0, 0)),
            pl.BlockSpec((step, width), lambda i: (i, 0)),
        ],
        out_specs=[
            pl.BlockSpec((copies, 2, step), lambda i: (0, 0, i)),
            pl.BlockSpec((step, width), lambda i: (i, 0)),
            pl.BlockSpec((1, cols), lambda i: (0, 0)),
        ],
        out_shape=[
            jax.ShapeDtypeStruct((copies, 2, rows), F32),
            jax.ShapeDtypeStruct((rows, width), F32),
            jax.ShapeDtypeStruct((1, cols), F32),
        ],
        scratch_shapes=[pltpu.VMEM((width, cols), BF16)],
        compiler_params=params(40),
        cost_estimate=pl.CostEstimate(
            flops=2 * rows * cols * (width + 1),
            bytes_accessed=2 * rows * cols + 2 * width * cols,
            transcendentals=0,
        ),
        name="last_sweep",
    )(col_parts, expo, dirs, unit)


def wide_kernel(
    place, both, totals, t_protos, s_protos, expo, rounded, dirs, col_norm, mixed, t_dirs
):
    step = pl.program_id(0)

    @pl.when(step == 0)
    def _():
        t_dirs[...] = unit_cols(t_protos[...].astype(F32))[0]
        dirs[...], col_norm[...] = unit_cols(s_protos[...].astype(F32))
        mixed[...] = jnp.zeros_like(mixed)

    width = t_dirs.shape[0]
    t_unit = unit_rows(both[:, :width])[0].astype(BF16)
    expo[...] = jnp.exp2(dot(t_unit, t_dirs[...]) * teacher_rate).astype(BF16)
    s_unit = unit_rows(both[:, width:])[0].astype(BF16)
    rounded[...] = s_unit
    log_total = lanes_to_rows(jnp.log2(totals[0]))
    shift = jnp.concatenate([log_total] * (dirs.shape[1] // LANES), axis=1)
    chance = jnp.exp2(dot(s_unit, dirs[...]) * student_rate - shift).astype(BF16)
    mixed[...] += dot_cols(s_unit, chance)


def wide_call(place, both, totals, t_protos, s_protos, parts):
    crops, double = both.shape
    width = double // 2
    rows = crops // parts
    cols = t_protos.shape[1] // parts
    whole = lambda i, place: (0, 0)
    return pl.pallas_call(
        wide_kernel,
        grid_spec=pltpu.PrefetchScalarGridSpec(
            num_scalar_prefetch=1,
            grid=(parts,),
            in_specs=[
                pl.BlockSpec((rows, double), lambda i, place: (i, 0)),
                pl.BlockSpec((1, 1, rows), lambda i, place: (i, 0, 0)),
                pl.BlockSpec((width, cols), lambda i, place: (0, place[1])),
                pl.BlockSpec((width, cols), lambda i, place: (0, place[1])),
            ],
            out_specs=[
                pl.BlockSpec((rows, cols), lambda i, place: (i, 0)),
                pl.BlockSpec((rows, width), lambda i, place: (i, 0)),
                pl.BlockSpec((width, cols), whole),
                pl.BlockSpec((1, cols), whole),
                pl.BlockSpec((width, cols), whole),
            ],
            scratch_shapes=[pltpu.VMEM((width, cols), BF16)],
        ),
        out_shape=[
            jax.ShapeDtypeStruct((crops, cols), BF16),
            jax.ShapeDtypeStruct((crops, width), BF16),
            jax.ShapeDtypeStruct((width, cols), BF16),
            jax.ShapeDtypeStruct((1, cols), F32),
            jax.ShapeDtypeStruct((width, cols), F32),
        ],
        compiler_params=params(40),
        cost_estimate=pl.CostEstimate(
            flops=6 * crops * cols * width,
            bytes_accessed=4 * crops * double + 2 * crops * cols,
            transcendentals=2 * crops * cols,
        ),
        name="wide_products",
    )(place, both, totals, t_protos, s_protos)


def finish_kernel(place, row_sums, expo, rounded, scale, dirs, mixed, keep, send, dots, total):
    step = pl.program_id(0)

    @pl.when(step == 0)
    def _():
        total[...] = jnp.zeros_like(total)

    per = row_sums.shape[2]
    parts = []
    for k in range(row_sums.shape[0]):
        inverse = lanes_to_rows(1.0 / row_sums[k])
        inverse = jnp.concatenate([inverse] * (rounded.shape[1] // LANES), axis=1)
        parts.append((rounded[k * per : (k + 1) * per, :].astype(F32) * inverse).astype(BF16))
    total[...] += dot_cols(jnp.concatenate(parts, axis=0), expo[...])

    @pl.when(step == pl.num_programs(0) - 1)
    def _():
        grad = (mixed[...] - scale[...] * total[...]) * (1.0 / student_temp)
        dots[...] = jnp.sum(grad * dirs[...].astype(F32), axis=0, keepdims=True)
        total[...] = grad
        chunks, rows = keep.shape[0], keep.shape[1]
        for k in range(chunks):
            first = pl.multiple_of((2 * k + place[0]) * rows, rows)
            other = pl.multiple_of((2 * k + 1 - place[0]) * rows, rows)
            keep[k] = total[pl.ds(first, rows), :]
            send[k] = total[pl.ds(other, rows), :]


def finish_call(place, row_sums, expo, rounded, scale, dirs, mixed, blocks=4):
    crops, cols = expo.shape
    width = dirs.shape[0]
    parts = row_sums.shape[0]
    rows = crops // blocks
    whole = lambda i, place: (0, 0)
    chunk = (parts, width // (2 * parts), cols)
    return pl.pallas_call(
        finish_kernel,
        grid_spec=pltpu.PrefetchScalarGridSpec(
            num_scalar_prefetch=1,
            grid=(blocks,),
            in_specs=[
                pl.BlockSpec((parts // blocks, 1, crops // parts), lambda i, place: (i, 0, 0)),
                pl.BlockSpec((rows, cols), lambda i, place: (i, 0)),
                pl.BlockSpec((rows, width), lambda i, place: (i, 0)),
                pl.BlockSpec((1, cols), whole),
                pl.BlockSpec((width, cols), whole),
                pl.BlockSpec((width, cols), whole),
            ],
            out_specs=[
                pl.BlockSpec(chunk, lambda i, place: (0, 0, 0)),
                pl.BlockSpec(chunk, lambda i, place: (0, 0, 0)),
                pl.BlockSpec((1, cols), whole),
            ],
            scratch_shapes=[pltpu.VMEM((width, cols), F32)],
        ),
        out_shape=[
            jax.ShapeDtypeStruct(chunk, F32),
            jax.ShapeDtypeStruct(chunk, F32),
            jax.ShapeDtypeStruct((1, cols), F32),
        ],
        compiler_params=params(40),
        cost_estimate=pl.CostEstimate(
            flops=2 * crops * cols * width,
            bytes_accessed=2 * crops * cols + 2 * crops * width,
            transcendentals=0,
        ),
        name="finish_protos",
    )(place, row_sums, expo, rounded, scale, dirs, mixed)


COL_AXES = ("x", "zl")
ROW_AXES = ("c", "zh", "y")
SWAP = [(0, 1), (1, 0)]


def exchange(values, axes):
    return lax.all_to_all(values, axes, 0, 0, tiled=True)


def swap_cores(values):
    return lax.ppermute(values, "c", SWAP)


def in_core_order(core, own, other, axis):
    first = jnp.where(core == 0, own, other)
    second = jnp.where(core == 0, other, own)
    return jnp.concatenate([first, second], axis=axis)


def on_device(teacher_emb, student_emb, teacher_protos, student_protos):
    core = lax.axis_index("c")
    chip = lax.axis_index(COL_AXES)
    group = lax.axis_index(("zh", "y"))
    chips = lax.axis_size(COL_AXES)
    groups = lax.axis_size(("zh", "y"))
    row_copies = 2 * groups
    crops, width = teacher_emb.shape
    batch_total = crops * chips * 2
    proto_total = teacher_protos.shape[1] * groups
    place = jnp.stack([core, chip]).astype(jnp.int32)

    both = jnp.concatenate([teacher_emb, student_emb], axis=1).astype(F32)
    other = swap_cores(both)
    gathered = lax.all_gather(both, COL_AXES, axis=0, tiled=True)

    expo, col_part = teacher_call(place, teacher_emb, other, teacher_protos, chips)
    student_mixed, total_part, dirs, unit = student_call(
        place, student_emb, other, student_protos
    )

    row_parts = exchange(row_sweep(proto_total, exchange(col_part, COL_AXES), expo, row_copies), ROW_AXES)
    col_parts = exchange(col_sweep(batch_total, row_parts, expo, chips), COL_AXES)
    row_part = row_sweep(proto_total, col_parts, expo, row_copies)
    total_copies = jnp.broadcast_to(total_part[None], row_part.shape)
    row_parts = exchange(jnp.concatenate([row_part, total_copies], axis=2), ROW_AXES)
    totals = jnp.sum(row_parts[:, 0, 2 * crops :], axis=0)
    col_part = col_sweep(batch_total, row_parts, expo, chips)
    own_totals = lax.dynamic_slice_in_dim(totals, core * crops, crops, 0)
    total_copies = jnp.broadcast_to(own_totals[None, None], (chips, 1, crops))
    col_parts = exchange(jnp.concatenate([col_part, total_copies], axis=2), COL_AXES)
    all_totals = col_parts[:, :, col_part.shape[2] :]
    row_part, teacher_mixed, scale = last_sweep(
        proto_total, col_parts, expo, dirs, unit, row_copies
    )
    row_parts = jnp.sum(exchange(row_part, ROW_AXES), axis=0)
    row_sum = row_parts[0]
    loss_part = jnp.sum(jnp.log(totals) - row_parts[1] / (student_temp * row_sum))

    own_sums = lax.dynamic_slice_in_dim(row_sum, core * crops, crops, 0)
    message = jnp.concatenate([own_sums, jnp.full((LANES,), loss_part, F32)])
    message = exchange(jnp.broadcast_to(message, (chips, 1, crops + LANES)), COL_AXES)
    loss = jnp.sum(message[:, 0, crops]) / batch_total

    wide_expo, wide_round, wide_dirs, wide_norm, wide_mixed = wide_call(
        place, gathered, all_totals, teacher_protos, student_protos, chips
    )
    cols = wide_expo.shape[1]
    full_scale = in_core_order(core, scale, swap_cores(scale), 1)
    wide_scale = lax.dynamic_slice_in_dim(full_scale, chip * cols, cols, 1)
    keep, send, dots_part = finish_call(
        place, message[:, :, :crops], wide_expo, wide_round, wide_scale, wide_dirs, wide_mixed
    )
    grad_rows = keep + swap_cores(send)
    dots = dots_part + swap_cores(dots_part)
    own_dirs = lax.dynamic_index_in_dim(
        wide_dirs.reshape(chips, 2, width // (2 * chips), cols), core, 1, keepdims=False
    )
    grad_rows = (grad_rows - own_dirs.astype(F32) * dots) / wide_norm
    grad_rows = exchange(grad_rows, COL_AXES)
    grad_prototypes = jnp.swapaxes(grad_rows, 0, 1).reshape(grad_rows.shape[1], chips * cols)

    crop_part = (student_mixed / totals[:, None] - teacher_mixed / row_sum[:, None]) / student_temp
    own_part = lax.dynamic_slice_in_dim(crop_part, core * crops, crops, 0)
    other_part = lax.dynamic_slice_in_dim(crop_part, (1 - core) * crops, crops, 0)
    own_part = own_part + swap_cores(other_part)
    rows = crops // groups
    parts = exchange(own_part.reshape(groups, rows, width), ("zh", "y"))
    grad_unit = jnp.sum(parts, axis=0)
    own_emb = lax.dynamic_slice_in_dim(student_emb, group * rows, rows, 0)
    s_unit, s_norm = unit_rows(own_emb.astype(F32))
    along = jnp.sum(s_unit * grad_unit, axis=1, keepdims=True)
    grad_embeddings = (grad_unit - s_unit * along) / s_norm
    return (grad_embeddings, grad_prototypes, loss)


def solution(mesh):
    fine = Mesh(mesh.devices.reshape(4, 2, 2, 2, 4), ("x", "zl", "c", "zh", "y"))
    crops, protos = ("x", "zl", "c"), ("zh", "y")
    return jax.shard_map(
        on_device,
        mesh=fine,
        in_specs=(P(crops, None), P(crops, None), P(None, protos), P(None, protos)),
        out_specs=(P(crops + protos, None), P(crops, protos), P()),
        check_vma=False,
    )
```

time: 497 us -> 262 us (0.53)
  blocking collectives: 342 us -> 46.6 us
  other arithmetic: 63.8 us -> 11.4 us
  Pallas kernels: 0 us -> 48.9 us
  waiting for transfers between devices: 37.3 us -> 72.5 us
  starting transfers between devices: 0.08 us -> 34.3 us
  matrix products: 31.3 us -> 0 us
  local copies, waits for them, and re-layouts: 5.18 us -> 30.7 us
    psum x8 -> x0, blocking collectives: 342 us -> none  [the longest x3 167 us: column_total(): return lax.psum(partial_sum, 'dp')]
    reduce_sum x9 -> x6, other arithmetic: 57.8 us -> 2.23 us  [the longest x1 1.3 us: on_device(): jnp.sum(jnp.log(totals) - row_parts[1] / (student_temp * row_sum))]
    pallas_call x0 -> x9, Pallas kernels: none -> 48.9 us  [the longest x1 13 us: wide_call(): pl.pallas_call(wide_kernel, grid_spec=pltpu.PrefetchScalarGridSpec(num_sc...]
    all_to_all x0 -> x3, blocking collectives: none -> 46.6 us  [exchange(): return lax.all_to_all(values, axes, 0, 0, tiled=True)]
    reduce_scatter x2 -> x0, waiting for transfers between devices: 37.3 us -> none  [the longest x1 37.2 us: on_device(): lax.psum_scatter(product / student_temp, 'dp', scatter_dimension=0, tiled...]
    all_gather x0 -> x1, waiting for transfers between devices: none -> 35.8 us  [on_device(): gathered = lax.all_gather(both, COL_AXES, axis=0, tiled=True)]
    all_to_all x0 -> x6, waiting for transfers between devices: none -> 33.5 us  [exchange(): return lax.all_to_all(values, axes, 0, 0, tiled=True)]
    dot_general x4 -> x0, matrix products: 31.3 us -> none  [the longest x1 11.6 us: on_device(): jnp.dot(t_round, t_wn, preferred_element_type=jnp.float32) / teacher_temp]
  transfers between devices with their start and end apart: 2 -> 12, of which waited for: 1 -> 8; matrix products, arithmetic and copies ran while one was open for 2% -> 4% of each run, Pallas kernels for 0% -> 19%
where the time goes in v1:
time: 262 us; the launch traced here: 261 us
  waiting for transfers between devices  72.5 us (28%)
  Pallas kernels  48.9 us (19%)
  blocking collectives  46.6 us (18%)
  starting transfers between devices  34.3 us (13%)
  local copies, waits for them, and re-layouts  30.7 us (12%)
  between operations  16 us (6%)
  other arithmetic  11.4 us (4%)
    all_to_all x3, blocking collectives, exchange(): return lax.all_to_all(values, axes, 0, 0, tiled=True)  46.6 us
    all_gather x1, waiting for transfers between devices, on_device(): gathered = lax.all_gather(both, COL_AXES, axis=0, tiled=True)  35.8 us
    all_to_all x6, waiting for transfers between devices, exchange(): return lax.all_to_all(values, axes, 0, 0, tiled=True)  33.5 us
    all_to_all x6, starting transfers between devices, exchange(): return lax.all_to_all(values, axes, 0, 0, tiled=True)  30 us
    unnamed x40, local copies, waits for them, and re-layouts  27.7 us
    pallas_call x1, Pallas kernels, wide_call(): pl.pallas_call(wide_kernel, grid_spec=pltpu.PrefetchScalarGridSpec(num_sc...  13 us
    pallas_call x1, Pallas kernels, student_call(): pl.pallas_call(student_kernel, grid_spec=pltpu.PrefetchScalarGridSpec(num...  8.02 us
    pallas_call x2, Pallas kernels, col_sweep(): pl.pallas_call(lambda *refs: col_sweep_kernel(batch_total, *refs), grid=(...  6.52 us
  transfers between devices with their start and end apart: 12, of which 8 were waited for; matrix products, arithmetic and copies ran while one was open for 4% of the time, Pallas kernels for 19%

profile of v1, /device:TPU:1, one launch (start us, length us, event | category | flops | bytes accessed | tf_op | source)
XLA Modules:
  0.0 260.6 jit_solution(16893962272640807501)
XLA Ops:
  11.0 2.4 collective-permute-done.other
  14.4 2.2 copy-done.13
  16.5 5.9 %teacher_expo.1 = (bf16[1024,4096]{1,0:T(8,128)(2,1)S(1)}, f32[8,1,4096]{2,1,0:T(1,128)S(1)}) custom-call(s32[2]{0:T(128)S(1)} %pad_add_fusion.place, bf16[512,256]{1,0:T(8,128)(2,1)S(1)} %copy-done.9, f32[512,512]{1,0:T(8,128)S(1)} %collective-permute-done.other, bf16[256,8192]{1,0:T(8,128)(2,1)S(1)} %copy-done.13), custom_call_target="tpu_custom_call" | custom-call | flops 2147483648 | bytes 10485760 | tf_op jit(solution)/shard_map/teacher_expo/pallas_call | solution.py:89
  22.5 16.5 %all_to_all.45.refs_0_ = f32[8,1,4096]{2,1,0:T(1,128)S(1)} all-to-all(f32[8,1,4096]{2,1,0:T(1,128)S(1)} %get-tuple-element.21), channel_id=1, replica_groups=mesh['x'=4,'zl'=2,'c'=2,'zh'=2,'y'=4] {'x','zl'}, dimensions={0} | all-to-all | bytes 262144 | tf_op jit(solution)/shard_map/all_to_all | solution.py:453
  39.0 2.4 row_sweep.2
  41.4 14.9 %all_to_all.46.refs_0_ = f32[16,1,1024]{2,1,0:T(1,128)S(1)} all-to-all(f32[16,1,1024]{2,1,0:T(1,128)S(1)} %row_sweep.2), channel_id=1, replica_groups=mesh['x'=4,'zl'=2,'c'=2,'zh'=2,'y'=4] {'c','zh','y'}, dimensions={0} | all-to-all | bytes 131072 | tf_op jit(solution)/shard_map/all_to_all | solution.py:453
  56.3 3.5 %col_sweep.2 = f32[8,1,4096]{2,1,0:T(1,128)} custom-call(f32[16,1,1024]{2,1,0:T(1,128)S(1)} %all_to_all.46.refs_0_, bf16[1024,4096]{1,0:T(8,128)(2,1)S(1)} %get-tuple-element.22.refs_1_), custom_call_target="tpu_custom_call" | custom-call | flops 8388608 | bytes 8388608 | tf_op jit(solution)/shard_map/col_sweep/pallas_call | solution.py:235
  59.9 3.4 %all-to-all-start.2 = ((f32[8,1,4096]{2,1,0:T(1,128)}), f32[8,1,4096]{2,1,0:T(1,128)S(1)}, u32[]{:S(2)}, u32[]{:S(2)}) async-start(f32[8,1,4096]{2,1,0:T(1,128)} %col_sweep.2), calls=%async_computation.2 | async-start | bytes 262144 | tf_op jit(solution)/shard_map/all_to_all | solution.py:453
  63.3 2.2 copy-done.15
  66.7 8.0 %student_totals.1 = (f32[1024,256]{1,0:T(8,128)S(1)}, f32[1,1024]{1,0:T(1,128)S(1)}, bf16[256,4096]{1,0:T(8,128)(2,1)S(1)}, bf16[1024,256]{1,0:T(8,128)(2,1)S(1)}) custom-call(s32[2]{0:T(128)S(1)} %pad_add_fusion.place, bf16[512,256]{1,0:T(8,128)(2,1)S(1)} %copy-done.8, f32[512,512]{1,0:T(8,128)S(1)} %copy-done.18, bf16[256,8192]{1,0:T(8,128)(2,1)S(1)} %copy-done.15), custom_call_target="tpu_custom_call" | custom-call | flops 4294967296 | bytes 5242880 | tf_op jit(solution)/shard_map/student_totals/pallas_call | solution.py:146
  75.5 3.4 %copy-done.1 = bf16[1024,4096]{1,0:T(8,128)(2,1)S(1)} copy-done((bf16[1024,4096]{1,0:T(8,128)(2,1)S(1)}, bf16[1024,4096]{1,0:T(8,128)(2,1)}, u32[]{:S(2)}) %copy-start.1) | copy-done | bytes 8388632
  79.0 2.4 row_sweep.3
  82.1 5.1 %all-to-all-start.3 = ((f32[16,1,2048]{2,1,0:T(1,128)}), f32[16,1,2048]{2,1,0:T(1,128)S(1)}, u32[]{:S(2)}, u32[]{:S(2)}) async-start(f32[16,1,2048]{2,1,0:T(1,128)} %pad_maximum_fusion.1), calls=%async_computation.3 | async-start | bytes 262144 | tf_op jit(solution)/shard_map/all_to_all | solution.py:453
  87.2 8.8 %all-to-all-done.3.refs_0_ = f32[16,1,2048]{2,1,0:T(1,128)S(1)} async-done(((f32[16,1,2048]{2,1,0:T(1,128)}), f32[16,1,2048]{2,1,0:T(1,128)S(1)}, u32[]{:S(2)}, u32[]{:S(2)}) %all-to-all-start.3) | async-done | bytes 131104 | tf_op jit(solution)/shard_map/all_to_all | solution.py:453
  96.6 3.4 %copy-done.2 = bf16[1024,4096]{1,0:T(8,128)(2,1)S(1)} copy-done((bf16[1024,4096]{1,0:T(8,128)(2,1)S(1)}, bf16[1024,4096]{1,0:T(8,128)(2,1)}, u32[]{:S(2)}) %copy-start.2) | copy-done | bytes 8388632
  100.0 3.0 %col_sweep.3 = f32[8,1,4096]{2,1,0:T(1,128)S(1)} custom-call(f32[16,1,2048]{2,1,0:T(1,128)S(1)} %all-to-all-done.3.refs_0_, bf16[1024,4096]{1,0:T(8,128)(2,1)S(1)} %copy-done.2), custom_call_target="tpu_custom_call" | custom-call | flops 8388608 | bytes 8388608 | tf_op jit(solution)/shard_map/col_sweep/pallas_call | solution.py:235
  103.2 15.2 %all_to_all.47.refs_0_ = f32[8,1,4608]{2,1,0:T(1,128)S(1)} all-to-all(f32[8,1,4608]{2,1,0:T(1,128)S(1)} %pad_maximum_fusion), channel_id=1, replica_groups=mesh['x'=4,'zl'=2,'c'=2,'zh'=2,'y'=4] {'x','zl'}, dimensions={0} | all-to-all | bytes 294912 | tf_op jit(solution)/shard_map/all_to_all | solution.py:453
  118.3 3.4 %copy-done.3 = bf16[1024,4096]{1,0:T(8,128)(2,1)S(1)} copy-done((bf16[1024,4096]{1,0:T(8,128)(2,1)S(1)}, bf16[1024,4096]{1,0:T(8,128)(2,1)}, u32[]{:S(2)}) %copy-start.3) | copy-done | bytes 8388632
  121.8 6.0 %last_sweep.1 = (f32[16,2,1024]{2,1,0:T(2,128)S(1)}, f32[1024,256]{1,0:T(8,128)S(1)}, f32[1,4096]{1,0:T(1,128)}) custom-call(f32[8,1,4608]{2,1,0:T(1,128)S(1)} %all_to_all.47.refs_0_, bf16[1024,4096]{1,0:T(8,128)(2,1)S(1)} %copy-done.3, bf16[256,4096]{1,0:T(8,128)(2,1)S(1)} %get-tuple-element.24.refs_2_, bf16[1024,256]{1,0:T(8,128)(2,1)S(1)} %copy-done.7), custom_call_target="tpu_custom_call" | custom-call | flops 2155872256 | bytes 10485760 | tf_op jit(solution)/shard_map/last_sweep/pallas_call | solution.py:282
  130.1 3.4 %all-to-all-start.5 = ((f32[16,2,1024]{2,1,0:T(2,128)}), f32[16,2,1024]{2,1,0:T(2,128)S(1)}, u32[]{:S(2)}, u32[]{:S(2)}) async-start(f32[16,2,1024]{2,1,0:T(2,128)} %copy-done.10), calls=%async_computation.5 | async-start | bytes 262144 | tf_op jit(solution)/shard_map/all_to_all | solution.py:453
  134.3 7.6 %all-to-all-done.5 = f32[16,2,1024]{2,1,0:T(2,128)S(1)} async-done(((f32[16,2,1024]{2,1,0:T(2,128)}), f32[16,2,1024]{2,1,0:T(2,128)S(1)}, u32[]{:S(2)}, u32[]{:S(2)}) %all-to-all-start.5) | async-done | bytes 131104 | tf_op jit(solution)/shard_map/all_to_all | solution.py:453
  144.5 3.5 %all-to-all-start.7 = ((f32[8,1,640]{2,1,0:T(1,128)}), f32[8,1,640]{2,1,0:T(1,128)S(1)}, u32[]{:S(2)}, u32[]{:S(2)}) async-start(f32[8,1,640]{2,1,0:T(1,128)} %broadcast_in_dim.11), calls=%async_computation.7 | async-start | bytes 40960 | tf_op jit(solution)/shard_map/all_to_all | solution.py:453
  153.6 35.8 %all-gather.2.cloned.1.call-done.both = f32[4096,512]{1,0:T(8,128)} async-done(((f32[512,512]{1,0:T(8,128)}), f32[4096,512]{1,0:T(8,128)}) %all-gather.2.cloned.1.call-update) | async-done | bytes 8388624 | tf_op jit(solution)/shard_map/all_gather | solution.py:480
  189.4 2.2 copy-done.14
  191.6 2.2 copy-done.16
  193.8 13.0 %wide_products.1 = (bf16[4096,1024]{1,0:T(8,128)(2,1)}, bf16[4096,256]{1,0:T(8,128)(2,1)S(1)}, bf16[256,1024]{1,0:T(8,128)(2,1)S(1)}, f32[1,1024]{1,0:T(1,128)S(1)}, f32[256,1024]{1,0:T(8,128)S(1)}) custom-call(s32[2]{0:T(128)S(1)} %copy-done.12, f32[4096,512]{1,0:T(8,128)} %all-gather.2.cloned.1.call-done.both, f32[8,1,512]{2,1,0:T(1,128)S(1)} %slice.28.totals, ...), custom_call_target="tpu_custom_call" | custom-call | flops 6442450944 | bytes 16777216 | tf_op jit(solution)/shard_map/wide_products/pallas_call | solution.py:340
  206.8 3.4 %copy-done.4 = bf16[4096,1024]{1,0:T(8,128)(2,1)S(1)} copy-done((bf16[4096,1024]{1,0:T(8,128)(2,1)S(1)}, bf16[4096,1024]{1,0:T(8,128)(2,1)}, u32[]{:S(2)}) %copy-start.4) | copy-done | bytes 8388632
  210.2 4.7 %finish_protos.1 = (f32[8,16,1024]{2,1,0:T(8,128)S(1)}, f32[8,16,1024]{2,1,0:T(8,128)S(1)}, f32[1,1024]{1,0:T(1,128)S(1)}) custom-call(s32[2]{0:T(128)S(1)} %copy-done.12, f32[8,1,512]{2,1,0:T(1,128)S(1)} %slice.27.row_sums, bf16[4096,1024]{1,0:T(8,128)(2,1)S(1)} %copy-done.4, bf16[4096,256]{1,0:T(8,128)(2,1)S(1)} %get-tuple-element.29.rounded, ...), custom_call_target="tpu_custom_call" | custom-call | flops 2147483648 | bytes 10485760 | tf_op jit(solution)/shard_map/finish_protos/pallas_call | solution.py:412
  216.6 6.3 %all-to-all-start.6 = ((f32[8,64,256]{2,1,0:T(8,128)}), f32[8,64,256]{2,1,0:T(8,128)S(1)}, u32[]{:S(2)}, u32[]{:S(2)}) async-start(f32[8,64,256]{2,1,0:T(8,128)} %bitcast.4), calls=%async_computation.6 | async-start | bytes 1048576 | tf_op jit(solution)/shard_map/all_to_all | solution.py:453
  226.1 8.6 %all-to-all-done.6 = f32[8,64,256]{2,1,0:T(8,128)S(1)} async-done(((f32[8,64,256]{2,1,0:T(8,128)}), f32[8,64,256]{2,1,0:T(8,128)S(1)}, u32[]{:S(2)}, u32[]{:S(2)}) %all-to-all-start.6) | async-done | bytes 524320 | tf_op jit(solution)/shard_map/all_to_all | solution.py:453
  234.7 8.4 %all-to-all-start.8 = ((f32[8,16,1024]{2,1,0:T(8,128)}), f32[8,16,1024]{2,1,0:T(8,128)S(1)}, u32[]{:S(2)}, u32[]{:S(2)}) async-start(f32[8,16,1024]{2,1,0:T(8,128)} %fusion.1), calls=%async_computation.8 | async-start | bytes 1048576 | tf_op jit(solution)/shard_map/all_to_all | solution.py:453
  245.3 6.5 %all-to-all-done.8 = f32[8,16,1024]{2,1,0:T(8,128)S(1)} async-done(((f32[8,16,1024]{2,1,0:T(8,128)}), f32[8,16,1024]{2,1,0:T(8,128)S(1)}, u32[]{:S(2)}, u32[]{:S(2)}) %all-to-all-start.8) | async-done | bytes 524320 | tf_op jit(solution)/shard_map/all_to_all | solution.py:453
  (75 shorter events, 26.9 us)
Async XLA Ops:
  7.2 182.2 %all-gather.2.cloned.1.call-start = ((), (), s32[]{:S(2)}) async-start(), calls=%async_computation.9 | async-start | bytes 9437184 | tf_op jit(solution)/shard_map/all_gather | solution.py:480
  9.4 4.0 %collective-permute-start = (f32[512,512]{1,0:T(8,128)}, f32[512,512]{1,0:T(8,128)S(1)}, u32[]{:S(2)}, u32[]{:S(2)}) collective-permute-start(f32[512,512]{1,0:T(8,128)} %maximum_convert_fusion), channel_id=1, source_target_pairs={{0,8},{8,0},{1,9},{9,1},{2,10},{10,2},{3,11},{11,3},{4,12},{12,4},... | collective-permute-start | bytes 3145736 | tf_op jit(solution)/shard_map/ppermute | solution.py:457
  11.0 52.3 %copy-start.11 = (s32[2]{0:T(128)}, s32[2]{0:T(128)S(1)}, u32[]{:S(2)}) copy-start(s32[2]{0:T(128)S(1)} %pad_add_fusion.place) | copy-start | bytes 28
  13.4 0.9 copy-start.9
  14.4 2.2 copy-start.13
  16.5 24.8 %copy-start.17 = (f32[512,512]{1,0:T(8,128)}, f32[512,512]{1,0:T(8,128)S(1)}, u32[]{:S(2)}) copy-start(f32[512,512]{1,0:T(8,128)S(1)} %collective-permute-done.other) | copy-start | bytes 3145732
  22.5 33.9 %copy-start = (bf16[1024,4096]{1,0:T(8,128)(2,1)}, bf16[1024,4096]{1,0:T(8,128)(2,1)S(1)}, u32[]{:S(2)}) copy-start(bf16[1024,4096]{1,0:T(8,128)(2,1)S(1)} %get-tuple-element.22.refs_1_) | copy-start | bytes 25165828
  56.3 6.9 %copy-start.8 = (bf16[512,256]{1,0:T(8,128)(2,1)S(1)}, bf16[512,256]{1,0:T(8,128)(2,1)}, u32[]{:S(2)}) copy-start(bf16[512,256]{1,0:T(8,128)(2,1)} %own.2) | copy-start | bytes 786436
  59.9 15.7 %all-to-all-start.2 = ((f32[8,1,4096]{2,1,0:T(1,128)}), f32[8,1,4096]{2,1,0:T(1,128)S(1)}, u32[]{:S(2)}, u32[]{:S(2)}) async-start(f32[8,1,4096]{2,1,0:T(1,128)} %col_sweep.2), calls=%async_computation.2 | async-start | bytes 262144 | tf_op jit(solution)/shard_map/all_to_all | solution.py:453
  63.3 2.2 copy-start.15
  65.5 1.2 copy-start.18
  74.7 0.8 copy-start.6
  75.5 3.4 %copy-start.1 = (bf16[1024,4096]{1,0:T(8,128)(2,1)S(1)}, bf16[1024,4096]{1,0:T(8,128)(2,1)}, u32[]{:S(2)}) copy-start(bf16[1024,4096]{1,0:T(8,128)(2,1)} %copy-done) | copy-start | bytes 25165828
  82.1 13.8 %all-to-all-start.3 = ((f32[16,1,2048]{2,1,0:T(1,128)}), f32[16,1,2048]{2,1,0:T(1,128)S(1)}, u32[]{:S(2)}, u32[]{:S(2)}) async-start(f32[16,1,2048]{2,1,0:T(1,128)} %pad_maximum_fusion.1), calls=%async_computation.3 | async-start | bytes 262144 | tf_op jit(solution)/shard_map/all_to_all | solution.py:453
  96.0 0.6 copy-start.19
  96.6 3.5 %copy-start.2 = (bf16[1024,4096]{1,0:T(8,128)(2,1)S(1)}, bf16[1024,4096]{1,0:T(8,128)(2,1)}, u32[]{:S(2)}) copy-start(bf16[1024,4096]{1,0:T(8,128)(2,1)} %copy-done) | copy-start | bytes 25165828
  100.0 18.3 %copy-start.7 = (bf16[1024,256]{1,0:T(8,128)(2,1)S(1)}, bf16[1024,256]{1,0:T(8,128)(2,1)}, u32[]{:S(2)}) copy-start(bf16[1024,256]{1,0:T(8,128)(2,1)} %copy-done.6) | copy-start | bytes 1572868
  118.3 3.4 %copy-start.3 = (bf16[1024,4096]{1,0:T(8,128)(2,1)S(1)}, bf16[1024,4096]{1,0:T(8,128)(2,1)}, u32[]{:S(2)}) copy-start(bf16[1024,4096]{1,0:T(8,128)(2,1)} %copy-done) | copy-start | bytes 25165828
  127.8 1.1 copy-start.5
  128.8 0.7 copy-start.10
  129.5 59.9 %copy-start.12 = (s32[2]{0:T(128)S(1)}, s32[2]{0:T(128)}, u32[]{:S(2)}) copy-start(s32[2]{0:T(128)} %copy-done.11) | copy-start | bytes 28
  129.5 4.0 %collective-permute-start.2 = (f32[1,4096]{1,0:T(1,128)}, f32[1,4096]{1,0:T(1,128)S(1)}, u32[]{:S(2)}, u32[]{:S(2)}) collective-permute-start(f32[1,4096]{1,0:T(1,128)} %get-tuple-element.30), channel_id=1, source_target_pairs={{0,8},{8,0},{1,9},{9,1},{2,10},{10,2},{3,11},{11,3},{4,12},{12,4},... | collective-permute-start | bytes 49160 | tf_op jit(solution)/shard_map/ppermute | solution.py:457
  130.1 11.8 %all-to-all-start.5 = ((f32[16,2,1024]{2,1,0:T(2,128)}), f32[16,2,1024]{2,1,0:T(2,128)S(1)}, u32[]{:S(2)}, u32[]{:S(2)}) async-start(f32[16,2,1024]{2,1,0:T(2,128)} %copy-done.10), calls=%async_computation.5 | async-start | bytes 262144 | tf_op jit(solution)/shard_map/all_to_all | solution.py:453
  144.5 9.1 %all-to-all-start.7 = ((f32[8,1,640]{2,1,0:T(1,128)}), f32[8,1,640]{2,1,0:T(1,128)S(1)}, u32[]{:S(2)}, u32[]{:S(2)}) async-start(f32[8,1,640]{2,1,0:T(1,128)} %broadcast_in_dim.11), calls=%async_computation.7 | async-start | bytes 40960 | tf_op jit(solution)/shard_map/all_to_all | solution.py:453
  150.4 65.3 %collective-permute-start.1 = (f32[512,256]{1,0:T(8,128)}, f32[512,256]{1,0:T(8,128)S(1)}, u32[]{:S(2)}, u32[]{:S(2)}) collective-permute-start(f32[512,256]{1,0:T(8,128)} %constant_dynamic-slice_fusion.1), channel_id=1, source_target_pairs={{0,8},{8,0},{1,9},{9,1},{2,10},{10,2},{3,11},{11,3},{4,12},{12,4},... | collective-permute-start | bytes 1572872 | tf_op jit(solution)/shard_map/ppermute | solution.py:457
  189.4 2.2 copy-start.14
  191.6 2.2 copy-start.16
  206.8 3.4 %copy-start.4 = (bf16[4096,1024]{1,0:T(8,128)(2,1)S(1)}, bf16[4096,1024]{1,0:T(8,128)(2,1)}, u32[]{:S(2)}) copy-start(bf16[4096,1024]{1,0:T(8,128)(2,1)} %get-tuple-element.28.expo) | copy-start | bytes 25165828
  214.9 9.2 %collective-permute-start.3 = (f32[8,16,1024]{2,1,0:T(8,128)S(1)}, f32[8,16,1024]{2,1,0:T(8,128)}, u32[]{:S(2)}, u32[]{:S(2)}) collective-permute-start(f32[8,16,1024]{2,1,0:T(8,128)S(1)} %get-tuple-element.34), channel_id=1, source_target_pairs={{0,8},{8,0},{1,9},{9,1},{2,10},{10,2},{3,11},{11,3},{4,12},{12,4},... | collective-permute-start | bytes 1572872 | tf_op jit(solution)/shard_map/ppermute | solution.py:457
  216.6 18.1 %all-to-all-start.6 = ((f32[8,64,256]{2,1,0:T(8,128)}), f32[8,64,256]{2,1,0:T(8,128)S(1)}, u32[]{:S(2)}, u32[]{:S(2)}) async-start(f32[8,64,256]{2,1,0:T(8,128)} %bitcast.4), calls=%async_computation.6 | async-start | bytes 1048576 | tf_op jit(solution)/shard_map/all_to_all | solution.py:453
  222.9 1.2 collective-permute-start.4
  234.7 17.0 %all-to-all-start.8 = ((f32[8,16,1024]{2,1,0:T(8,128)}), f32[8,16,1024]{2,1,0:T(8,128)S(1)}, u32[]{:S(2)}, u32[]{:S(2)}) async-start(f32[8,16,1024]{2,1,0:T(8,128)} %fusion.1), calls=%async_computation.8 | async-start | bytes 1048576 | tf_op jit(solution)/shard_map/all_to_all | solution.py:453
Sparse Core Ops, SparseCore 0:
  9.6 179.7 all-gather.1

commit v2 on v0

v2 whole, which is shorter than its diff:
```python
import math

import jax
import jax.numpy as jnp
from jax import lax
from jax.experimental import pallas as pl
from jax.experimental.pallas import tpu as pltpu
from jax.sharding import Mesh
from jax.sharding import PartitionSpec as P

teacher_temp = 0.07
student_temp = 0.1
norm_eps = 1e-06
log2_e = math.log2(math.e)
teacher_rate = log2_e / teacher_temp
student_rate = log2_e / student_temp

BF16 = jnp.bfloat16
F32 = jnp.float32
LANES = 128
BLOCK = 512
MIB = 1 << 20


def params(mib):
    return pltpu.CompilerParams(vmem_limit_bytes=mib * MIB)


def unit_rows(wide):
    norms = jnp.sqrt(jnp.sum(wide * wide, axis=1, keepdims=True) + norm_eps)
    return wide / norms, norms


def unit_cols(wide):
    norms = jnp.sqrt(jnp.sum(wide * wide, axis=0, keepdims=True) + norm_eps)
    return (wide * (1.0 / norms)).astype(BF16), norms


def dot_rows(left, right):
    return lax.dot_general(left, right, (((1,), (1,)), ((), ())), preferred_element_type=F32)


def dot_cols(left, right):
    return lax.dot_general(left, right, (((0,), (0,)), ((), ())), preferred_element_type=F32)


def dot(left, right):
    return jnp.dot(left, right, preferred_element_type=F32)


def fold_lanes(values):
    total = values[:, :LANES]
    for first in range(LANES, values.shape[1], LANES):
        total = total + values[:, first : first + LANES]
    return total


def row_to_lanes(values):
    return jnp.sum(values.T, axis=0, keepdims=True)


def lanes_to_rows(values):
    return jnp.broadcast_to(values, (LANES, values.shape[1])).T


def place_pair(scratch, core, own, other):
    rows = own.shape[0]
    scratch[pl.ds(pl.multiple_of(core * rows, rows), rows), :] = own
    scratch[pl.ds(pl.multiple_of((1 - core) * rows, rows), rows), :] = other

VMEM = pl.BlockSpec(memory_space=pltpu.VMEM)
SMEM = pl.BlockSpec(memory_space=pltpu.SMEM)


def tall(values, copies):
    return jnp.broadcast_to(values[None], (copies,) + values.shape)


def teacher_kernel(place, own, other, protos, expo, col_part, unit):
    core = place[0]
    first = unit_rows(own[...].astype(F32))[0].astype(BF16)
    second = unit_rows(other[...])[0].astype(BF16)
    place_pair(unit, core, first, second)
    half = expo.shape[1]
    copies = col_part.shape[0]

    def block(j, carry):
        here = pl.ds(pl.multiple_of(j * BLOCK, BLOCK), BLOCK)
        there = pl.ds(pl.multiple_of(core * half + j * BLOCK, BLOCK), BLOCK)
        directions, _ = unit_cols(protos[:, there].astype(F32))
        values = jnp.exp2(dot(unit[...], directions) * teacher_rate)
        expo[:, here] = values.astype(BF16)
        col_part[:, :, here] = tall(jnp.sum(values, axis=0, keepdims=True), copies)
        return carry

    lax.fori_loop(0, half // BLOCK, block, 0)


def teacher_call(place, own, other, protos, copies):
    rows, width = own.shape
    cols = protos.shape[1] // 2
    return pl.pallas_call(
        teacher_kernel,
        in_specs=[SMEM, VMEM, VMEM, VMEM],
        out_specs=[VMEM, VMEM],
        out_shape=[
            jax.ShapeDtypeStruct((2 * rows, cols), BF16),
            jax.ShapeDtypeStruct((copies, 1, cols), F32),
        ],
        scratch_shapes=[pltpu.VMEM((2 * rows, width), BF16)],
        compiler_params=params(16),
        cost_estimate=pl.CostEstimate(
            flops=4 * rows * cols * width,
            bytes_accessed=2 * 2 * rows * cols + 2 * width * cols,
            transcendentals=2 * rows * cols,
        ),
        name="teacher_expo",
    )(place, own, other, protos)


def student_kernel(place, own, other, protos, mixed, total_part, dirs, unit, sums):
    core = place[0]
    first = unit_rows(own[...].astype(F32))[0].astype(BF16)
    second = unit_rows(other[...])[0].astype(BF16)
    place_pair(unit, core, first, second)
    sums[...] = jnp.zeros_like(sums)
    mixed[...] = jnp.zeros_like(mixed)
    half = dirs.shape[1]

    def block(j, carry):
        here = pl.ds(pl.multiple_of(j * BLOCK, BLOCK), BLOCK)
        there = pl.ds(pl.multiple_of(core * half + j * BLOCK, BLOCK), BLOCK)
        directions, _ = unit_cols(protos[:, there].astype(F32))
        dirs[:, here] = directions
        values = jnp.exp2(dot(unit[...], directions) * student_rate)
        sums[...] += fold_lanes(values)
        mixed[...] += dot_rows(values.astype(BF16), directions)
        return carry

    lax.fori_loop(0, half // BLOCK, block, 0)
    total_part[...] = row_to_lanes(sums[...])


def student_call(place, own, other, protos):
    rows, width = own.shape
    cols = protos.shape[1] // 2
    return pl.pallas_call(
        student_kernel,
        in_specs=[SMEM, VMEM, VMEM, VMEM],
        out_specs=[VMEM] * 4,
        out_shape=[
            jax.ShapeDtypeStruct((2 * rows, width), F32),
            jax.ShapeDtypeStruct((1, 2 * rows), F32),
            jax.ShapeDtypeStruct((width, cols), BF16),
            jax.ShapeDtypeStruct((2 * rows, width), BF16),
        ],
        scratch_shapes=[pltpu.VMEM((2 * rows, LANES), F32)],
        compiler_params=params(16),
        cost_estimate=pl.CostEstimate(
            flops=8 * rows * cols * width,
            bytes_accessed=4 * width * cols + 8 * rows * width,
            transcendentals=2 * rows * cols,
        ),
        name="student_totals",
    )(place, own, other, protos)


def row_sweep_kernel(proto_total, col_parts, expo, *rest):
    row_part, scale = rest[-2:]
    copies = row_part.shape[0]
    cols = expo.shape[1]
    sums = jnp.sum(col_parts[:, :, :cols], axis=0)
    scale[...] = jnp.broadcast_to(1.0 / (proto_total * sums), scale.shape)
    for first in range(0, expo.shape[0], LANES):
        here = slice(first, first + LANES)
        total = jnp.zeros((LANES, LANES), F32)
        for at in range(0, cols, LANES):
            wide = jnp.concatenate([scale[:, at : at + LANES]] * (LANES // 8), axis=0)
            total = total + expo[here, at : at + LANES].astype(F32) * wide
        row_part[:, 0:1, here] = tall(row_to_lanes(total), copies)
    if len(rest) > 2:
        row_part[:, 1:2, :] = tall(rest[0][...], copies)


def row_sweep(proto_total, col_parts, expo, copies, extra=()):
    rows, cols = expo.shape
    return pl.pallas_call(
        lambda *refs: row_sweep_kernel(proto_total, *refs),
        in_specs=[VMEM] * (2 + len(extra)),
        out_specs=VMEM,
        out_shape=jax.ShapeDtypeStruct((copies, 1 + len(extra), rows), F32),
        scratch_shapes=[pltpu.VMEM((8, cols), F32)],
        compiler_params=params(16),
        cost_estimate=pl.CostEstimate(
            flops=2 * rows * cols, bytes_accessed=2 * rows * cols, transcendentals=0
        ),
        name="row_sweep",
    )(col_parts, expo, *extra)


def col_sweep_kernel(batch_total, row_parts, expo, col_part, scale):
    sums = jnp.sum(row_parts[...], axis=0)
    scale[...] = lanes_to_rows(1.0 / (batch_total * sums[0:1]))
    copies = col_part.shape[0]
    cols = expo.shape[1]
    for at in range(0, cols, LANES):
        block = expo[:, at : at + LANES].astype(F32) * scale[...]
        col_part[:, :, at : at + LANES] = tall(jnp.sum(block, axis=0, keepdims=True), copies)
    if sums.shape[0] > 1:
        col_part[:, :, cols:] = tall(sums[1:2], copies)


def col_sweep(batch_total, row_parts, expo, copies):
    rows, cols = expo.shape
    extra = rows * (row_parts.shape[1] - 1)
    return pl.pallas_call(
        lambda *refs: col_sweep_kernel(batch_total, *refs),
        in_specs=[VMEM] * 2,
        out_specs=VMEM,
        out_shape=jax.ShapeDtypeStruct((copies, 1, cols + extra), F32),
        scratch_shapes=[pltpu.VMEM((rows, LANES), F32)],
        compiler_params=params(16),
        cost_estimate=pl.CostEstimate(
            flops=2 * rows * cols, bytes_accessed=2 * rows * cols, transcendentals=0
        ),
        name="col_sweep",
    )(row_parts, expo)


def last_sweep_kernel(proto_total, col_parts, expo, dirs, unit, row_part, mixed, scale_out, scaled):
    rows, cols = expo.shape
    copies = row_part.shape[0]
    scale = 1.0 / (proto_total * jnp.sum(col_parts[:, :, :cols], axis=0))
    scale_out[...] = jnp.broadcast_to(scale, scale_out.shape)
    scaled[...] = (dirs[...].astype(F32) * scale).astype(BF16)
    step = 2 * LANES

    def block(i, carry):
        here = pl.ds(pl.multiple_of(i * step, step), step)
        values = expo[here, :]
        product = dot_rows(values, scaled[...])
        mixed[here, :] = product
        meet = fold_lanes(product * unit[here, :].astype(F32))
        total = jnp.zeros((step, LANES), F32)
        for at in range(0, cols, LANES):
            wide = jnp.concatenate([scale_out[:, at : at + LANES]] * (step // 8), axis=0)
            total = total + values[:, at : at + LANES].astype(F32) * wide
        row_part[:, 0:1, here] = tall(row_to_lanes(total), copies)
        row_part[:, 1:2, here] = tall(row_to_lanes(meet), copies)
        return carry

    lax.fori_loop(0, rows // step, block, 0)


def last_sweep(proto_total, col_parts, expo, dirs, unit, copies):
    rows, cols = expo.shape
    width = dirs.shape[0]
    return pl.pallas_call(
        lambda *refs: last_sweep_kernel(proto_total, *refs),
        in_specs=[VMEM] * 4,
        out_specs=[VMEM] * 3,
        out_shape=[
            jax.ShapeDtypeStruct((copies, 2, rows), F32),
            jax.ShapeDtypeStruct((rows, width), F32),
            jax.ShapeDtypeStruct((8, cols), F32),
        ],
        scratch_shapes=[pltpu.VMEM((width, cols), BF16)],
        compiler_params=params(16),
        cost_estimate=pl.CostEstimate(
            flops=2 * rows * cols * (width + 1),
            bytes_accessed=2 * rows * cols + 2 * width * cols,
            transcendentals=0,
        ),
        name="last_sweep",
    )(col_parts, expo, dirs, unit)


def message_kernel(place, row_parts, col_parts, message):
    rows = row_parts.shape[2]
    sums = jnp.sum(row_parts[...], axis=0)
    cols = col_parts.shape[2] - rows
    totals = col_parts[place[1], :, cols:]
    inverse = 1.0 / sums[0:1]
    terms = jnp.log(totals) - sums[1:2] * inverse * (1.0 / student_temp)
    loss = jnp.sum(terms, axis=1, keepdims=True)
    message[:, :, :rows] = tall(sums[0:1], message.shape[0])
    message[:, :, rows:] = jnp.broadcast_to(loss[None], (message.shape[0], 1, LANES))


def message_call(place, row_parts, col_parts, copies):
    rows = row_parts.shape[2]
    return pl.pallas_call(
        message_kernel,
        in_specs=[SMEM, VMEM, VMEM],
        out_specs=VMEM,
        out_shape=jax.ShapeDtypeStruct((copies, 1, rows + LANES), F32),
        compiler_params=params(16),
        name="row_message",
    )(place, row_parts, col_parts)


def crop_kernel(place, row_parts, col_parts, student, teacher, own, other):
    rows, width = student.shape
    sums = jnp.sum(row_parts[:, 0:1, :], axis=0)
    totals = col_parts[place[1], :, col_parts.shape[2] - rows :]
    half = rows // 2
    factor = 1.0 / student_temp
    a = lanes_to_rows(factor / totals)
    b = lanes_to_rows(factor / sums)
    a = jnp.concatenate([a] * (width // LANES), axis=1)
    b = jnp.concatenate([b] * (width // LANES), axis=1)
    full = student[...] * a - teacher[...] * b
    swap = place[0] == 1
    own[...] = jnp.where(swap, full[half:], full[:half])
    other[...] = jnp.where(swap, full[:half], full[half:])


def crop_call(place, row_parts, col_parts, student, teacher):
    rows, width = student.shape
    return pl.pallas_call(
        crop_kernel,
        in_specs=[SMEM] + [VMEM] * 4,
        out_specs=[VMEM] * 2,
        out_shape=[jax.ShapeDtypeStruct((rows // 2, width), F32)] * 2,
        compiler_params=params(16),
        cost_estimate=pl.CostEstimate(
            flops=4 * rows * width, bytes_accessed=12 * rows * width, transcendentals=0
        ),
        name="crop_gradients",
    )(place, row_parts, col_parts, student, teacher)


def wide_kernel(place, crops, totals, protos, rounded, dirs, col_norm, mixed):
    @pl.when(pl.program_id(0) == 0)
    def _():
        dirs[...], col_norm[...] = unit_cols(protos[...].astype(F32))
        mixed[...] = jnp.zeros_like(mixed)

    unit = unit_rows(crops[...])[0].astype(BF16)
    rounded[...] = unit
    log_total = lanes_to_rows(jnp.log2(totals[0]))
    shift = jnp.concatenate([log_total] * (dirs.shape[1] // LANES), axis=1)
    chance = jnp.exp2(dot(unit, dirs[...]) * student_rate - shift).astype(BF16)
    mixed[...] += dot_cols(unit, chance)


def wide_call(place, gathered, col_parts, protos, shares):
    crops, width = gathered.shape
    chips = col_parts.shape[0]
    rows = crops // chips
    cols = protos.shape[1] // shares
    last = col_parts.shape[2] // rows - 1
    whole = lambda i, place: (0, 0)
    return pl.pallas_call(
        wide_kernel,
        grid_spec=pltpu.PrefetchScalarGridSpec(
            num_scalar_prefetch=1,
            grid=(chips,),
            in_specs=[
                pl.BlockSpec((rows, width), lambda i, place: (i, 0)),
                pl.BlockSpec((1, 1, rows), lambda i, place: (i, 0, last)),
                pl.BlockSpec((width, cols), lambda i, place: (0, place[2])),
            ],
            out_specs=[
                pl.BlockSpec((rows, width), lambda i, place: (i, 0)),
                pl.BlockSpec((width, cols), whole),
                pl.BlockSpec((1, cols), whole),
                pl.BlockSpec((width, cols), whole),
            ],
        ),
        out_shape=[
            jax.ShapeDtypeStruct((crops, width), BF16),
            jax.ShapeDtypeStruct((width, cols), BF16),
            jax.ShapeDtypeStruct((1, cols), F32),
            jax.ShapeDtypeStruct((width, cols), F32),
        ],
        compiler_params=params(48),
        cost_estimate=pl.CostEstimate(
            flops=4 * crops * cols * width,
            bytes_accessed=6 * crops * width,
            transcendentals=crops * cols,
        ),
        name="wide_products",
    )(place, gathered, col_parts, protos)


def finish_kernel(place, crops, row_sums, protos, rounded, scale, dirs, col_norm, mixed, grad, t_dirs, total):
    step = pl.program_id(0)

    @pl.when(step == 0)
    def _():
        t_dirs[...] = unit_cols(protos[...].astype(F32))[0]
        total[...] = jnp.zeros_like(total)

    unit = unit_rows(crops[...])[0].astype(BF16)
    expo = jnp.exp2(dot(unit, t_dirs[...]) * teacher_rate).astype(BF16)
    inverse = lanes_to_rows(1.0 / row_sums[0])
    inverse = jnp.concatenate([inverse] * (rounded.shape[1] // LANES), axis=1)
    weighted = (rounded[...].astype(F32) * inverse).astype(BF16)
    total[...] += dot_cols(weighted, expo)

    @pl.when(step == pl.num_programs(0) - 1)
    def _():
        values = (mixed[...] - scale[0:1] * total[...]) * (1.0 / student_temp)
        wide = dirs[...].astype(F32)
        dots = jnp.sum(values * wide, axis=0, keepdims=True)
        values = (values - wide * dots) / col_norm[...]
        grad[...] = values.reshape(grad.shape)


def finish_call(place, gathered, message, protos, rounded, scale, dirs, col_norm, mixed, shares):
    crops, width = gathered.shape
    chips = message.shape[0]
    rows = crops // chips
    cols = dirs.shape[1]
    whole = lambda i, place: (0, 0)
    return pl.pallas_call(
        finish_kernel,
        grid_spec=pltpu.PrefetchScalarGridSpec(
            num_scalar_prefetch=1,
            grid=(chips,),
            in_specs=[
                pl.BlockSpec((rows, width), lambda i, place: (i, 0)),
                pl.BlockSpec((1, 1, rows), lambda i, place: (i, 0, 0)),
                pl.BlockSpec((width, cols), lambda i, place: (0, place[2])),
                pl.BlockSpec((rows, width), lambda i, place: (i, 0)),
                pl.BlockSpec((8, cols), lambda i, place: (0, place[3])),
                pl.BlockSpec((width, cols), whole),
                pl.BlockSpec((1, cols), whole),
                pl.BlockSpec((width, cols), whole),
            ],
            out_specs=pl.BlockSpec((shares, width // shares, cols), lambda i, place: (0, 0, 0)),
            scratch_shapes=[pltpu.VMEM((width, cols), BF16), pltpu.VMEM((width, cols), F32)],
        ),
        out_shape=jax.ShapeDtypeStruct((shares, width // shares, cols), F32),
        compiler_params=params(58),
        cost_estimate=pl.CostEstimate(
            flops=4 * crops * cols * width,
            bytes_accessed=6 * crops * width,
            transcendentals=crops * cols,
        ),
        name="finish_protos",
    )(place, gathered, message, protos, rounded, scale, dirs, col_norm, mixed)


COL_AXES = ("x", "zl")
ROW_AXES = ("c", "zh", "y")
CROP_AXES = ("x", "zl", "c")
SWAP = [(0, 1), (1, 0)]


def exchange(values, axes):
    return lax.all_to_all(values, axes, 0, 0, tiled=True)


def swap_cores(values):
    return lax.ppermute(values, "c", SWAP)


def on_device(teacher_emb, student_emb, teacher_protos, student_protos):
    core = lax.axis_index("c")
    chip = lax.axis_index(COL_AXES)
    group = lax.axis_index(("zh", "y"))
    chips = lax.axis_size(COL_AXES)
    groups = lax.axis_size(("zh", "y"))
    row_copies = 2 * groups
    shares = 2 * chips
    crops, width = teacher_emb.shape
    batch_total = crops * shares
    proto_total = teacher_protos.shape[1] * groups
    share = 2 * chip + core
    place = jnp.stack([core, chip, share, share % chips]).astype(jnp.int32)

    teacher_wide = teacher_emb.astype(F32)
    teacher_other = swap_cores(teacher_wide)
    student_wide = student_emb.astype(F32)
    student_other = swap_cores(student_wide)
    student_all = lax.all_gather(student_wide, CROP_AXES, axis=0, tiled=True)
    teacher_all = lax.all_gather(teacher_wide, CROP_AXES, axis=0, tiled=True)

    expo, col_part = teacher_call(place, teacher_emb, teacher_other, teacher_protos, chips)
    student_mixed, total_part, dirs, unit = student_call(
        place, student_emb, student_other, student_protos
    )

    col_parts = exchange(col_part, COL_AXES)
    row_part = row_sweep(proto_total, col_parts, expo, row_copies)
    row_parts = exchange(row_part, ROW_AXES)
    col_part = col_sweep(batch_total, row_parts, expo, chips)
    col_parts = exchange(col_part, COL_AXES)
    row_part = row_sweep(proto_total, col_parts, expo, row_copies, (total_part,))
    row_parts = exchange(row_part, ROW_AXES)
    col_part = col_sweep(batch_total, row_parts, expo, chips)
    col_parts = exchange(col_part, COL_AXES)
    row_part, teacher_mixed, scale = last_sweep(
        proto_total, col_parts, expo, dirs, unit, row_copies
    )
    row_parts = exchange(row_part, ROW_AXES)

    message = exchange(message_call(place, row_parts, col_parts, chips), COL_AXES)
    loss = jnp.sum(message[:, 0, 2 * crops]) / batch_total

    own_part, other_part = crop_call(place, row_parts, col_parts, student_mixed, teacher_mixed)
    own_part = own_part + swap_cores(other_part)
    rows = crops // groups
    parts = exchange(own_part.reshape(groups, rows, width), ("zh", "y"))
    grad_unit = jnp.sum(parts, axis=0)
    own_emb = lax.dynamic_slice_in_dim(student_emb, group * rows, rows, 0)
    s_unit, s_norm = unit_rows(own_emb.astype(F32))
    along = jnp.sum(s_unit * grad_unit, axis=1, keepdims=True)
    grad_embeddings = (grad_unit - s_unit * along) / s_norm

    rounded, wide_dirs, wide_norm, wide_mixed = wide_call(
        place, student_all, col_parts, student_protos, shares
    )
    other_scale = swap_cores(scale)
    own_half = share // chips == core
    wide_scale = jnp.where(own_half, scale, other_scale)
    grad_rows = finish_call(
        place, teacher_all, message, teacher_protos, rounded, wide_scale,
        wide_dirs, wide_norm, wide_mixed, shares,
    )
    grad_rows = exchange(grad_rows, CROP_AXES)
    grad_prototypes = jnp.swapaxes(grad_rows, 0, 1).reshape(grad_rows.shape[1], -1)
    return (grad_embeddings, grad_prototypes, loss)


def solution(mesh):
    fine = Mesh(mesh.devices.reshape(4, 2, 2, 2, 4), ("x", "zl", "c", "zh", "y"))
    crops, protos = ("x", "zl", "c"), ("zh", "y")
    return jax.shard_map(
        on_device,
        mesh=fine,
        in_specs=(P(crops, None), P(crops, None), P(None, protos), P(None, protos)),
        out_specs=(P(crops + protos, None), P(crops, protos), P()),
        check_vma=False,
    )
```

time: 497 us -> 189 us (0.38)
  blocking collectives: 342 us -> 51.5 us
  other arithmetic: 63.8 us -> 9.9 us
  Pallas kernels: 0 us -> 51.3 us
  matrix products: 31.3 us -> 0 us
  starting transfers between devices: 0.08 us -> 23.1 us
  waiting for transfers between devices: 37.3 us -> 14.9 us
  local copies, waits for them, and re-layouts: 5.18 us -> 20.2 us
    psum x8 -> x0, blocking collectives: 342 us -> none  [the longest x3 167 us: column_total(): return lax.psum(partial_sum, 'dp')]
    reduce_sum x9 -> x3, other arithmetic: 57.8 us -> 2.29 us  [the longest x1 1.3 us: on_device(): loss = jnp.sum(message[:, 0, 2 * crops]) / batch_total]
    all_to_all x0 -> x4, blocking collectives: none -> 51.5 us  [exchange(): return lax.all_to_all(values, axes, 0, 0, tiled=True)]
    pallas_call x0 -> x11, Pallas kernels: none -> 51.3 us  [the longest x1 13.5 us: finish_call(): pl.pallas_call(finish_kernel, grid_spec=pltpu.PrefetchScalarGridSpec(num_...]
    reduce_scatter x2 -> x0, waiting for transfers between devices: 37.3 us -> none  [the longest x1 37.2 us: on_device(): lax.psum_scatter(product / student_temp, 'dp', scatter_dimension=0, tiled...]
    dot_general x4 -> x0, matrix products: 31.3 us -> none  [the longest x1 11.6 us: on_device(): jnp.dot(t_round, t_wn, preferred_element_type=jnp.float32) / teacher_temp]
    all_to_all x0 -> x5, starting transfers between devices: none -> 19.5 us  [exchange(): return lax.all_to_all(values, axes, 0, 0, tiled=True)]
    unnamed x10 -> x38, local copies, waits for them, and re-layouts: 5.09 us -> 19.4 us
  transfers between devices with their start and end apart: 2 -> 11, of which waited for: 1 -> 4; matrix products, arithmetic and copies ran while one was open for 2% -> 4% of each run, Pallas kernels for 0% -> 27%
where the time goes in v2:
time: 189 us; the launch traced here: 187 us
  blocking collectives  51.5 us (27%)
  Pallas kernels  51.3 us (27%)
  starting transfers between devices  23.1 us (12%)
  local copies, waits for them, and re-layouts  20.2 us (11%)
  between operations  16 us (8%)
  waiting for transfers between devices  14.9 us (8%)
  other arithmetic  9.9 us (5%)
    all_to_all x4, blocking collectives, exchange(): return lax.all_to_all(values, axes, 0, 0, tiled=True)  51.5 us
    all_to_all x5, starting transfers between devices, exchange(): return lax.all_to_all(values, axes, 0, 0, tiled=True)  19.5 us
    unnamed x38, local copies, waits for them, and re-layouts  19.4 us
    pallas_call x1, Pallas kernels, finish_call(): pl.pallas_call(finish_kernel, grid_spec=pltpu.PrefetchScalarGridSpec(num_...  13.5 us
    all_to_all x5, waiting for transfers between devices, exchange(): return lax.all_to_all(values, axes, 0, 0, tiled=True)  12.2 us
    pallas_call x1, Pallas kernels, wide_call(): pl.pallas_call(wide_kernel, grid_spec=pltpu.PrefetchScalarGridSpec(num_sc...  10.9 us
    pallas_call x1, Pallas kernels, student_call(): pl.pallas_call(student_kernel, in_specs=[SMEM, VMEM, VMEM, VMEM], out_spe...  7.46 us
    pallas_call x1, Pallas kernels, teacher_call(): pl.pallas_call(teacher_kernel, in_specs=[SMEM, VMEM, VMEM, VMEM], out_spe...  4.89 us
  transfers between devices with their start and end apart: 11, of which 4 were waited for; matrix products, arithmetic and copies ran while one was open for 4% of the time, Pallas kernels for 27%

profile of v2, /device:TPU:1, one launch (start us, length us, event | category | flops | bytes accessed | tf_op | source)
XLA Modules:
  0.0 186.8 jit_solution(7037735802625964980)
XLA Ops:
  7.2 1.9 convert_element_type.10
  9.1 1.8 convert_element_type.9
  10.9 1.5 collective-permute-start
  12.6 1.6 collective-permute-done.other
  14.2 2.2 %copy-done.2 = bf16[256,8192]{1,0:T(8,128)(2,1)S(1)} copy-done((bf16[256,8192]{1,0:T(8,128)(2,1)S(1)}, bf16[256,8192]{1,0:T(8,128)(2,1)}, u32[]{:S(2)}) %copy-start.2) | copy-done | bytes 4194328
  17.3 4.9 %teacher_expo.1 = (bf16[1024,4096]{1,0:T(8,128)(2,1)S(1)}, f32[8,1,4096]{2,1,0:T(1,128)S(1)}) custom-call(s32[4]{0:T(128)S(1)} %pad_add_fusion.place, bf16[512,256]{1,0:T(8,128)(2,1)S(1)} %copy-done.11, f32[512,256]{1,0:T(8,128)S(1)} %collective-permute-done.other, bf16[256,8192]{1,0:T(8,128)(2,1)S(1)} %copy-done.2), custom_call_target="tpu_custom_call" | custom-call | flops 2147483648 | bytes 10485760 | tf_op jit(solution)/shard_map/teacher_expo/pallas_call | solution.py:102
  22.2 12.1 %all_to_all.45.refs_0_ = f32[8,1,4096]{2,1,0:T(1,128)S(1)} all-to-all(f32[8,1,4096]{2,1,0:T(1,128)S(1)} %get-tuple-element.18), channel_id=1, replica_groups=mesh['x'=4,'zl'=2,'c'=2,'zh'=2,'y'=4] {'x','zl'}, dimensions={0} | all-to-all | bytes 262144 | tf_op jit(solution)/shard_map/all_to_all | solution.py:453
  34.3 1.8 row_sweep.2
  36.1 16.2 %all_to_all.46.refs_0_ = f32[16,1,1024]{2,1,0:T(1,128)S(1)} all-to-all(f32[16,1,1024]{2,1,0:T(1,128)S(1)} %row_sweep.2), channel_id=1, replica_groups=mesh['x'=4,'zl'=2,'c'=2,'zh'=2,'y'=4] {'c','zh','y'}, dimensions={0} | all-to-all | bytes 131072 | tf_op jit(solution)/shard_map/all_to_all | solution.py:453
  52.3 2.7 %col_sweep.2 = f32[8,1,4096]{2,1,0:T(1,128)} custom-call(f32[16,1,1024]{2,1,0:T(1,128)S(1)} %all_to_all.46.refs_0_, bf16[1024,4096]{1,0:T(8,128)(2,1)S(1)} %get-tuple-element.19.refs_1_), custom_call_target="tpu_custom_call" | custom-call | flops 8388608 | bytes 8388608 | tf_op jit(solution)/shard_map/col_sweep/pallas_call | solution.py:216
  55.0 3.4 %all-to-all-start.2 = ((f32[8,1,4096]{2,1,0:T(1,128)}), f32[8,1,4096]{2,1,0:T(1,128)S(1)}, u32[]{:S(2)}, u32[]{:S(2)}) async-start(f32[8,1,4096]{2,1,0:T(1,128)} %col_sweep.2), calls=%async_computation.2 | async-start | bytes 262144 | tf_op jit(solution)/shard_map/all_to_all | solution.py:453
  60.1 2.3 %copy-done.15 = bf16[256,8192]{1,0:T(8,128)(2,1)S(1)} copy-done((bf16[256,8192]{1,0:T(8,128)(2,1)S(1)}, bf16[256,8192]{1,0:T(8,128)(2,1)}, u32[]{:S(2)}) %copy-start.15) | copy-done | bytes 4194328
  63.4 7.5 %student_totals.1 = (f32[1024,256]{1,0:T(8,128)S(1)}, f32[1,1024]{1,0:T(1,128)S(1)}, bf16[256,4096]{1,0:T(8,128)(2,1)S(1)}, bf16[1024,256]{1,0:T(8,128)(2,1)S(1)}) custom-call(s32[4]{0:T(128)S(1)} %pad_add_fusion.place, bf16[512,256]{1,0:T(8,128)(2,1)S(1)} %copy-done.9, f32[512,256]{1,0:T(8,128)S(1)} %copy-done.17, bf16[256,8192]{1,0:T(8,128)(2,1)S(1)} %copy-done.15), custom_call_target="tpu_custom_call" | custom-call | flops 4294967296 | bytes 5242880 | tf_op jit(solution)/shard_map/student_totals/pallas_call | solution.py:147
  71.7 3.4 %copy-done.1 = bf16[1024,4096]{1,0:T(8,128)(2,1)S(1)} copy-done((bf16[1024,4096]{1,0:T(8,128)(2,1)S(1)}, bf16[1024,4096]{1,0:T(8,128)(2,1)}, u32[]{:S(2)}) %copy-start.1) | copy-done | bytes 8388632
  75.1 1.8 row_sweep.3
  76.8 10.8 %all_to_all.47.refs_0_ = f32[16,2,1024]{2,1,0:T(2,128)S(1)} all-to-all(f32[16,2,1024]{2,1,0:T(2,128)S(1)} %row_sweep.3), channel_id=1, replica_groups=mesh['x'=4,'zl'=2,'c'=2,'zh'=2,'y'=4] {'c','zh','y'}, dimensions={0} | all-to-all | bytes 262144 | tf_op jit(solution)/shard_map/all_to_all | solution.py:453
  87.6 2.1 %col_sweep.3 = f32[8,1,5120]{2,1,0:T(1,128)S(1)} custom-call(f32[16,2,1024]{2,1,0:T(2,128)S(1)} %all_to_all.47.refs_0_, bf16[1024,4096]{1,0:T(8,128)(2,1)S(1)} %copy-done.1), custom_call_target="tpu_custom_call" | custom-call | flops 8388608 | bytes 8388608 | tf_op jit(solution)/shard_map/col_sweep/pallas_call | solution.py:216
  89.7 12.5 %all_to_all.48.refs_0_.col_parts.totals = f32[8,1,5120]{2,1,0:T(1,128)S(1)} all-to-all(f32[8,1,5120]{2,1,0:T(1,128)S(1)} %col_sweep.3), channel_id=1, replica_groups=mesh['x'=4,'zl'=2,'c'=2,'zh'=2,'y'=4] {'x','zl'}, dimensions={0} | all-to-all | bytes 327680 | tf_op jit(solution)/shard_map/all_to_all | solution.py:453
  102.2 3.9 %last_sweep.1 = (f32[16,2,1024]{2,1,0:T(2,128)S(1)}, f32[1024,256]{1,0:T(8,128)S(1)}, f32[8,4096]{1,0:T(8,128)S(1)}) custom-call(f32[8,1,5120]{2,1,0:T(1,128)S(1)} %all_to_all.48.refs_0_.col_parts.totals, bf16[1024,4096]{1,0:T(8,128)(2,1)S(1)} %copy-done.1, bf16[256,4096]{1,0:T(8,128)(2,1)S(1)} %get-tuple-element.21.refs_2_, bf16[1024,256]{1,0:T(8,128)(2,1)S(1)} %copy-done.7), custom_call_target="tpu_custom_call" | custom-call | flops 2155872256 | bytes 10485760 | tf_op jit(solution)/shard_map/last_sweep/pallas_call | solution.py:258
  107.7 1.7 collective-permute-start.3
  109.4 3.5 %all-to-all-start.5 = ((f32[16,2,1024]{2,1,0:T(2,128)}), f32[16,2,1024]{2,1,0:T(2,128)S(1)}, u32[]{:S(2)}, u32[]{:S(2)}) async-start(f32[16,2,1024]{2,1,0:T(2,128)} %copy-done.12), calls=%async_computation.5 | async-start | bytes 262144 | tf_op jit(solution)/shard_map/all_to_all | solution.py:453
  113.7 7.0 %all-to-all-done.5.row_parts = f32[16,2,1024]{2,1,0:T(2,128)S(1)} async-done(((f32[16,2,1024]{2,1,0:T(2,128)}), f32[16,2,1024]{2,1,0:T(2,128)S(1)}, u32[]{:S(2)}, u32[]{:S(2)}) %all-to-all-start.5) | async-done | bytes 131104 | tf_op jit(solution)/shard_map/all_to_all | solution.py:453
  120.7 1.3 row_message.1
  122.0 3.3 %all-to-all-start.7 = ((f32[8,1,1152]{2,1,0:T(1,128)}), f32[8,1,1152]{2,1,0:T(1,128)S(1)}, u32[]{:S(2)}, u32[]{:S(2)}) async-start(f32[8,1,1152]{2,1,0:T(1,128)} %row_message.1), calls=%async_computation.7 | async-start | bytes 73728 | tf_op jit(solution)/shard_map/all_to_all | solution.py:453
  130.5 3.5 %all-to-all-start.6 = ((f32[8,64,256]{2,1,0:T(8,128)}), f32[8,64,256]{2,1,0:T(8,128)S(1)}, u32[]{:S(2)}, u32[]{:S(2)}) async-start(f32[8,64,256]{2,1,0:T(8,128)} %bitcast.4), calls=%async_computation.6 | async-start | bytes 1048576 | tf_op jit(solution)/shard_map/all_to_all | solution.py:453
  134.0 10.9 %wide_products.1 = (bf16[8192,256]{1,0:T(8,128)(2,1)S(1)}, bf16[256,512]{1,0:T(8,128)(2,1)S(1)}, f32[1,512]{1,0:T(1,128)S(1)}, f32[256,512]{1,0:T(8,128)S(1)}) custom-call(s32[4]{0:T(128)S(1)} %pad_add_fusion.place, f32[8192,256]{1,0:T(8,128)} %all-gather.5.cloned.1.call-done.crops, f32[8,1,5120]{2,1,0:T(1,128)S(1)} %all_to_all.48.refs_0_.col_parts.totals, ...), custom_call_target="tpu_custom_call" | custom-call | flops 4294967296 | bytes 12582912 | tf_op jit(solution)/shard_map/wide_products/pallas_call | solution.py:354
  144.9 2.0 %copy-done.3 = bf16[8192,256]{1,0:T(8,128)(2,1)} copy-done((bf16[8192,256]{1,0:T(8,128)(2,1)}, bf16[8192,256]{1,0:T(8,128)(2,1)S(1)}, u32[]{:S(2)}) %copy-start.3) | copy-done | bytes 4194328
  149.0 13.5 %finish_protos.1 = f32[16,16,512]{2,1,0:T(8,128)} custom-call(s32[4]{0:T(128)} %copy-done.13, f32[8192,256]{1,0:T(8,128)} %all-gather.3.cloned.1.call-done.crops, f32[8,1,1152]{2,1,0:T(1,128)} %copy-done.18, bf16[256,8192]{1,0:T(8,128)(2,1)} %protos.7, bf16[8192,256]{1,0:T(8,128)(2,1)} %copy-done.3, f32[8,4096]{1,0:T(8,128)} %broadcast_select_fusion.scale, ...), custom_call_target="tpu_custom_call" | custom-call | flops 4294967296 | bytes 12582912 | tf_op jit(solution)/shard_map/finish_protos/pallas_call | solution.py:417
  162.6 5.8 %all-to-all-start.8 = ((f32[16,16,512]{2,1,0:T(8,128)}), f32[16,16,512]{2,1,0:T(8,128)S(1)}, u32[]{:S(2)}, u32[]{:S(2)}) async-start(f32[16,16,512]{2,1,0:T(8,128)} %finish_protos.1), calls=%async_computation.8 | async-start | bytes 1048576 | tf_op jit(solution)/shard_map/all_to_all | solution.py:453
  168.4 1.3 slice_reduce_fusion
  171.4 1.5 subtract_divide_fusion
  172.8 5.2 %all-to-all-done.8 = f32[16,16,512]{2,1,0:T(8,128)S(1)} async-done(((f32[16,16,512]{2,1,0:T(8,128)}), f32[16,16,512]{2,1,0:T(8,128)S(1)}, u32[]{:S(2)}, u32[]{:S(2)}) %all-to-all-start.8) | async-done | bytes 524320 | tf_op jit(solution)/shard_map/all_to_all | solution.py:453
  (57 shorter events, 16.4 us)
Async XLA Ops:
  7.2 126.9 %all-gather.5.cloned.1.call-start = ((), (), s32[]{:S(2)}) async-start(), calls=%async_computation.10 | async-start | bytes 8912896 | tf_op jit(solution)/shard_map/all_gather | solution.py:478
  9.1 139.4 %all-gather.3.cloned.1.call-start = ((), (), s32[]{:S(2)}) async-start(), calls=%async_computation.9 | async-start | bytes 8912896 | tf_op jit(solution)/shard_map/all_gather | solution.py:479
  10.9 3.2 %collective-permute-start = (f32[512,256]{1,0:T(8,128)}, f32[512,256]{1,0:T(8,128)S(1)}, u32[]{:S(2)}, u32[]{:S(2)}) collective-permute-start(f32[512,256]{1,0:T(8,128)} %convert_element_type.9), channel_id=1, source_target_pairs={{0,8},{8,0},{1,9},{9,1},{2,10},{10,2},{3,11},{11,3},{4,12},{12,4},... | collective-permute-start | bytes 1572872 | tf_op jit(solution)/shard_map/ppermute | solution.py:457
  12.4 45.9 %collective-permute-start.1 = (f32[512,256]{1,0:T(8,128)}, f32[512,256]{1,0:T(8,128)S(1)}, u32[]{:S(2)}, u32[]{:S(2)}) collective-permute-start(f32[512,256]{1,0:T(8,128)} %convert_element_type.10), channel_id=1, source_target_pairs={{0,8},{8,0},{1,9},{9,1},{2,10},{10,2},{3,11},{11,3},{4,12},{12,4},... | collective-permute-start | bytes 1572872 | tf_op jit(solution)/shard_map/ppermute | solution.py:457
  12.6 121.4 %copy-start.13 = (s32[4]{0:T(128)}, s32[4]{0:T(128)S(1)}, u32[]{:S(2)}) copy-start(s32[4]{0:T(128)S(1)} %pad_add_fusion.place) | copy-start | bytes 52
  14.2 2.2 %copy-start.2 = (bf16[256,8192]{1,0:T(8,128)(2,1)S(1)}, bf16[256,8192]{1,0:T(8,128)(2,1)}, u32[]{:S(2)}) copy-start(bf16[256,8192]{1,0:T(8,128)(2,1)} %protos.7) | copy-start | bytes 12582916
  16.4 0.9 copy-start.11
  22.2 30.0 %copy-start = (bf16[1024,4096]{1,0:T(8,128)(2,1)}, bf16[1024,4096]{1,0:T(8,128)(2,1)S(1)}, u32[]{:S(2)}) copy-start(bf16[1024,4096]{1,0:T(8,128)(2,1)S(1)} %get-tuple-element.19.refs_1_) | copy-start | bytes 25165828
  55.0 16.7 %all-to-all-start.2 = ((f32[8,1,4096]{2,1,0:T(1,128)}), f32[8,1,4096]{2,1,0:T(1,128)S(1)}, u32[]{:S(2)}, u32[]{:S(2)}) async-start(f32[8,1,4096]{2,1,0:T(1,128)} %col_sweep.2), calls=%async_computation.2 | async-start | bytes 262144 | tf_op jit(solution)/shard_map/all_to_all | solution.py:453
  58.3 0.8 copy-start.16
  59.1 1.0 copy-start.9
  60.1 2.3 %copy-start.15 = (bf16[256,8192]{1,0:T(8,128)(2,1)S(1)}, bf16[256,8192]{1,0:T(8,128)(2,1)}, u32[]{:S(2)}) copy-start(bf16[256,8192]{1,0:T(8,128)(2,1)} %protos.6) | copy-start | bytes 12582916
  62.4 1.0 copy-start.17
  70.9 0.8 copy-start.6
  71.7 3.4 %copy-start.1 = (bf16[1024,4096]{1,0:T(8,128)(2,1)S(1)}, bf16[1024,4096]{1,0:T(8,128)(2,1)}, u32[]{:S(2)}) copy-start(bf16[1024,4096]{1,0:T(8,128)(2,1)} %copy-done) | copy-start | bytes 25165828
  87.6 14.5 %copy-start.7 = (bf16[1024,256]{1,0:T(8,128)(2,1)S(1)}, bf16[1024,256]{1,0:T(8,128)(2,1)}, u32[]{:S(2)}) copy-start(bf16[1024,256]{1,0:T(8,128)(2,1)} %copy-done.6) | copy-start | bytes 1572868
  106.1 1.0 copy-start.4
  107.1 0.6 copy-start.12
  107.7 20.2 %collective-permute-start.3 = (f32[8,4096]{1,0:T(8,128)S(1)}, f32[8,4096]{1,0:T(8,128)S(1)}, u32[]{:S(2)}, u32[]{:S(2)}) collective-permute-start(f32[8,4096]{1,0:T(8,128)S(1)} %get-tuple-element.29), channel_id=1, source_target_pairs={{0,8},{8,0},{1,9},{9,1},{2,10},{10,2},{3,11},{11,3},{4,12},{12,4},... | collective-permute-start | bytes 393224 | tf_op jit(solution)/shard_map/ppermute | solution.py:457
  109.4 11.3 %all-to-all-start.5 = ((f32[16,2,1024]{2,1,0:T(2,128)}), f32[16,2,1024]{2,1,0:T(2,128)S(1)}, u32[]{:S(2)}, u32[]{:S(2)}) async-start(f32[16,2,1024]{2,1,0:T(2,128)} %copy-done.12), calls=%async_computation.5 | async-start | bytes 262144 | tf_op jit(solution)/shard_map/all_to_all | solution.py:453
  122.0 8.5 %all-to-all-start.7 = ((f32[8,1,1152]{2,1,0:T(1,128)}), f32[8,1,1152]{2,1,0:T(1,128)S(1)}, u32[]{:S(2)}, u32[]{:S(2)}) async-start(f32[8,1,1152]{2,1,0:T(1,128)} %row_message.1), calls=%async_computation.7 | async-start | bytes 73728 | tf_op jit(solution)/shard_map/all_to_all | solution.py:453
  125.4 1.3 copy-start.5
  127.6 2.0 %collective-permute-start.2 = (f32[512,256]{1,0:T(8,128)S(1)}, f32[512,256]{1,0:T(8,128)S(1)}, u32[]{:S(2)}, u32[]{:S(2)}) collective-permute-start(f32[512,256]{1,0:T(8,128)S(1)} %get-tuple-element.27), channel_id=1, source_target_pairs={{0,8},{8,0},{1,9},{9,1},{2,10},{10,2},{3,11},{11,3},{4,12},{12,4},... | collective-permute-start | bytes 1572872 | tf_op jit(solution)/shard_map/ppermute | solution.py:457
  130.5 14.4 %copy-start.18 = (f32[8,1,1152]{2,1,0:T(1,128)}, f32[8,1,1152]{2,1,0:T(1,128)S(1)}, u32[]{:S(2)}) copy-start(f32[8,1,1152]{2,1,0:T(1,128)S(1)} %all-to-all-done.7.row_sums) | copy-start | bytes 110596
  130.5 32.1 %all-to-all-start.6 = ((f32[8,64,256]{2,1,0:T(8,128)}), f32[8,64,256]{2,1,0:T(8,128)S(1)}, u32[]{:S(2)}, u32[]{:S(2)}) async-start(f32[8,64,256]{2,1,0:T(8,128)} %bitcast.4), calls=%async_computation.6 | async-start | bytes 1048576 | tf_op jit(solution)/shard_map/all_to_all | solution.py:453
  144.9 2.0 %copy-start.3 = (bf16[8192,256]{1,0:T(8,128)(2,1)}, bf16[8192,256]{1,0:T(8,128)(2,1)S(1)}, u32[]{:S(2)}) copy-start(bf16[8192,256]{1,0:T(8,128)(2,1)S(1)} %get-tuple-element.28.rounded) | copy-start | bytes 12582916
  146.9 0.8 copy-start.8
  147.8 0.7 copy-start.10
  148.5 0.6 copy-start.14
  162.6 15.4 %all-to-all-start.8 = ((f32[16,16,512]{2,1,0:T(8,128)}), f32[16,16,512]{2,1,0:T(8,128)S(1)}, u32[]{:S(2)}, u32[]{:S(2)}) async-start(f32[16,16,512]{2,1,0:T(8,128)} %finish_protos.1), calls=%async_computation.8 | async-start | bytes 1048576 | tf_op jit(solution)/shard_map/all_to_all | solution.py:453
Sparse Core Ops, SparseCore 0:
  9.7 59.2 all-gather.4
  71.3 57.1 all-gather.2

commit v3 on v0

v3 whole, which is shorter than its diff:
```python
import math

import jax
import jax.numpy as jnp
from jax import lax
from jax.experimental import pallas as pl
from jax.experimental.pallas import tpu as pltpu
from jax.sharding import Mesh
from jax.sharding import PartitionSpec as P

teacher_temp = 0.07
student_temp = 0.1
norm_eps = 1e-06
log2_e = math.log2(math.e)
teacher_rate = log2_e / teacher_temp
student_rate = log2_e / student_temp

BF16 = jnp.bfloat16
F32 = jnp.float32
LANES = 128
BLOCK = 512
MIB = 1 << 20


PARAMS = pltpu.CompilerParams(vmem_limit_bytes=61 * MIB)
HELD = pltpu.CompilerParams(vmem_limit_bytes=20 * MIB)


def unit_rows(wide):
    norms = jnp.sqrt(jnp.sum(wide * wide, axis=1, keepdims=True) + norm_eps)
    return wide * (1.0 / norms), norms


def unit_cols(wide):
    norms = jnp.sqrt(jnp.sum(wide * wide, axis=0, keepdims=True) + norm_eps)
    return (wide * (1.0 / norms)).astype(BF16), norms


def dot_rows(left, right):
    return lax.dot_general(left, right, (((1,), (1,)), ((), ())), preferred_element_type=F32)


def dot_cols(left, right):
    return lax.dot_general(left, right, (((0,), (0,)), ((), ())), preferred_element_type=F32)


def dot(left, right):
    return jnp.dot(left, right, preferred_element_type=F32)


def fold_lanes(values):
    total = values[:, :LANES]
    for first in range(LANES, values.shape[1], LANES):
        total = total + values[:, first : first + LANES]
    return total


def row_to_lanes(values):
    return jnp.sum(values.T, axis=0, keepdims=True)


def lanes_to_rows(values):
    return jnp.broadcast_to(values, (LANES, values.shape[1])).T


VMEM = pl.BlockSpec(memory_space=pltpu.VMEM)
SMEM = pl.BlockSpec(memory_space=pltpu.SMEM)
HBM = pl.BlockSpec(memory_space=pltpu.HBM)
TOKEN = (8, LANES)


def whole(shape):
    return pl.BlockSpec(shape, lambda *_: (0,) * len(shape))


def tall(values, copies):
    return jnp.broadcast_to(values[None], (copies,) + values.shape)


def unit_kernel(teacher, student, teacher_unit, student_unit, both, place):
    width = teacher.shape[1]
    first = unit_rows(teacher[...].astype(F32))[0].astype(BF16).astype(F32)
    second = unit_rows(student[...].astype(F32))[0].astype(BF16).astype(F32)
    teacher_unit[...] = first
    student_unit[...] = second
    both[:, :width] = first
    both[:, width:] = second
    core, x, near = (lax.axis_index(axis) for axis in ("c", "x", "zl"))
    share = 2 * x + core
    here = (share // 4 == core).astype(jnp.int32)
    for i, value in enumerate((core, 2 * x + near, share, share % 4, near, x, here)):
        place[i] = value.astype(jnp.int32)


def unit_call(teacher, student):
    rows, width = teacher.shape
    return pl.pallas_call(
        unit_kernel,
        grid=(1,),
        in_specs=[whole((rows, width))] * 2,
        out_specs=[whole((rows, width))] * 2 + [whole((rows, 2 * width)), SMEM],
        out_shape=[
            jax.ShapeDtypeStruct((rows, width), F32),
            jax.ShapeDtypeStruct((rows, width), F32),
            jax.ShapeDtypeStruct((rows, 2 * width), F32),
            jax.ShapeDtypeStruct((7,), jnp.int32),
        ],
        compiler_params=HELD,
        name="unit_rows",
    )(teacher, student)


def pair_rows(core, own, other):
    swap = core == 1
    first = jnp.where(swap, other, own).astype(BF16)
    second = jnp.where(swap, own, other).astype(BF16)
    return jnp.concatenate([first, second], axis=0)


def teacher_kernel(place, own, other, protos, expo, col_part, unit):
    unit[...] = pair_rows(place[0], own[...], other[...])
    for first in range(0, protos.shape[1], BLOCK):
        here = slice(first, first + BLOCK)
        directions, _ = unit_cols(protos[:, here].astype(F32))
        values = jnp.exp2(dot(unit[...], directions) * teacher_rate)
        expo[:, here] = values.astype(BF16)
        col_part[:, :, here] = tall(jnp.sum(values, axis=0, keepdims=True), col_part.shape[0])


def teacher_call(place, own, other, protos, copies):
    rows, width = own.shape
    cols = protos.shape[1]
    return pl.pallas_call(
        teacher_kernel,
        in_specs=[SMEM, VMEM, VMEM, VMEM],
        out_specs=[VMEM, VMEM],
        out_shape=[
            jax.ShapeDtypeStruct((2 * rows, cols), BF16),
            jax.ShapeDtypeStruct((copies, 1, cols), F32),
        ],
        scratch_shapes=[pltpu.VMEM((2 * rows, width), BF16)],
        compiler_params=HELD,
        cost_estimate=pl.CostEstimate(
            flops=4 * rows * cols * width,
            bytes_accessed=2 * 2 * rows * cols + 2 * width * cols,
            transcendentals=2 * rows * cols,
        ),
        name="teacher_expo",
    )(place, own, other, protos)


def student_kernel(
    place, own, other, protos, mixed, total_part, dirs, unit, own_v, other_v, store, dirs_v, unit_v, sums, in_sems, out_sems
):
    half = store.shape[1]
    pair = [
        pltpu.make_async_copy(own, own_v, in_sems.at[0]),
        pltpu.make_async_copy(other, other_v, in_sems.at[1]),
    ]
    incoming, outgoing = [], []
    for j in range(half // BLOCK):
        there = pl.ds(pl.multiple_of(place[0] * half + j * BLOCK, BLOCK), BLOCK)
        here = pl.ds(j * BLOCK, BLOCK)
        incoming.append(
            pltpu.make_async_copy(protos.at[:, there], store.at[:, here], in_sems.at[2 + j])
        )
        outgoing.append(
            pltpu.make_async_copy(dirs_v.at[:, here], dirs.at[:, here], out_sems.at[1 + j])
        )
    for copy in pair + incoming:
        copy.start()
    for copy in pair:
        copy.wait()
    unit_v[...] = pair_rows(place[0], own_v[...], other_v[...])
    unit_out = pltpu.make_async_copy(unit_v, unit, out_sems.at[0])
    unit_out.start()
    for j in range(half // BLOCK):
        here = slice(j * BLOCK, (j + 1) * BLOCK)
        incoming[j].wait()
        directions, _ = unit_cols(store[:, here].astype(F32))
        dirs_v[:, here] = directions
        outgoing[j].start()
        values = jnp.exp2(dot(unit_v[...], directions) * student_rate)
        part = fold_lanes(values)
        product = dot_rows(values.astype(BF16), directions)
        sums[...] = part if j == 0 else sums[...] + part
        mixed[...] = product if j == 0 else mixed[...] + product
    total_part[...] = row_to_lanes(sums[...])
    for copy in [unit_out] + outgoing:
        copy.wait()


def student_call(place, own, other, protos):
    rows, width = own.shape
    cols = protos.shape[1] // 2
    return pl.pallas_call(
        student_kernel,
        in_specs=[SMEM, HBM, HBM, HBM],
        out_specs=[VMEM, VMEM, HBM, HBM],
        out_shape=[
            jax.ShapeDtypeStruct((2 * rows, width), F32),
            jax.ShapeDtypeStruct((1, 2 * rows), F32),
            jax.ShapeDtypeStruct((width, cols), BF16),
            jax.ShapeDtypeStruct((2 * rows, width), BF16),
        ],
        scratch_shapes=[
            pltpu.VMEM((rows, width), F32),
            pltpu.VMEM((rows, width), F32),
            pltpu.VMEM((width, cols), BF16),
            pltpu.VMEM((width, cols), BF16),
            pltpu.VMEM((2 * rows, width), BF16),
            pltpu.VMEM((2 * rows, LANES), F32),
            pltpu.SemaphoreType.DMA((2 + cols // BLOCK,)),
            pltpu.SemaphoreType.DMA((1 + cols // BLOCK,)),
        ],
        compiler_params=PARAMS,
        cost_estimate=pl.CostEstimate(
            flops=8 * rows * cols * width,
            bytes_accessed=4 * width * cols + 8 * rows * width,
            transcendentals=2 * rows * cols,
        ),
        name="student_totals",
    )(place, own, other, protos)


def row_slices(expo):
    return [slice(first, first + LANES) for first in range(0, expo.shape[0], LANES)]


class Stream:
    def __init__(self, expo, scratch):
        self.rows = row_slices(expo)
        self.values, self.copies = expo, []
        if scratch:
            self.values, sems = scratch
            for i, here in enumerate(self.rows):
                copy = pltpu.make_async_copy(expo.at[here, :], self.values.at[here, :], sems.at[i])
                copy.start()
                self.copies.append(copy)

    def __iter__(self):
        for i, here in enumerate(self.rows):
            if self.copies:
                self.copies[i].wait()
            yield here


def stream_scratch(expo, held):
    if held:
        return []
    return [pltpu.VMEM(expo.shape, BF16), pltpu.SemaphoreType.DMA((expo.shape[0] // LANES,))]


def scaled_row_sums(values, here, scale):
    total = jnp.zeros((LANES, LANES), F32)
    for at in range(0, values.shape[1], LANES):
        wide = jnp.concatenate([scale[:, at : at + LANES]] * (LANES // 8), axis=0)
        total = total + values[here, at : at + LANES].astype(F32) * wide
    return row_to_lanes(total)


def row_sweep_kernel(proto_total, extra, col_parts, expo, *rest):
    row_part, scale = rest[extra], rest[extra + 1]
    stream = Stream(expo, rest[extra + 2 :])
    copies = row_part.shape[0]
    sums = jnp.sum(col_parts[...], axis=0)
    scale[...] = jnp.broadcast_to(1.0 / (proto_total * sums), scale.shape)
    if extra:
        row_part[:, 1:2, :] = tall(rest[0][...], copies)
    for here in stream:
        row_part[:, 0:1, here] = tall(scaled_row_sums(stream.values, here, scale), copies)


def row_sweep(proto_total, col_parts, expo, copies, held, extra=()):
    rows, cols = expo.shape
    kinds = 1 + len(extra)
    return pl.pallas_call(
        lambda *refs: row_sweep_kernel(proto_total, len(extra), *refs),
        in_specs=[VMEM, VMEM if held else HBM] + [VMEM] * len(extra),
        out_specs=VMEM,
        out_shape=jax.ShapeDtypeStruct((copies, kinds, rows), F32),
        scratch_shapes=[pltpu.VMEM((8, cols), F32)] + stream_scratch(expo, held),
        compiler_params=HELD if held else PARAMS,
        cost_estimate=pl.CostEstimate(
            flops=2 * rows * cols, bytes_accessed=2 * rows * cols, transcendentals=0
        ),
        name="row_sweep",
    )(col_parts, expo, *extra)


def col_sweep_kernel(batch_total, row_parts, expo, col_part, scale, *scratch):
    stream = Stream(expo, scratch)
    copies = col_part.shape[0]
    cols = expo.shape[1]
    sums = jnp.sum(row_parts[...], axis=0)
    scale[...] = lanes_to_rows(1.0 / (batch_total * sums[0:1]))
    if sums.shape[0] > 1:
        col_part[:, :, cols:] = tall(sums[1:2], copies)
    if stream.copies:
        total = [jnp.zeros((8, LANES), F32)] * (cols // LANES)
        for here in stream:
            for j in range(cols // LANES):
                block = stream.values[here, j * LANES : (j + 1) * LANES].astype(F32) * scale[here, :]
                total[j] = total[j] + jnp.sum(block.reshape(LANES // 8, 8, LANES), axis=0)
        for j, part in enumerate(total):
            part = jnp.sum(part, axis=0, keepdims=True)
            col_part[:, :, j * LANES : (j + 1) * LANES] = tall(part, copies)
    else:
        for at in range(0, cols, LANES):
            block = expo[:, at : at + LANES].astype(F32) * scale[...]
            col_part[:, :, at : at + LANES] = tall(jnp.sum(block, axis=0, keepdims=True), copies)


def col_sweep(batch_total, row_parts, expo, copies, held):
    rows, cols = expo.shape
    extra = row_parts.shape[1] - 1
    return pl.pallas_call(
        lambda *refs: col_sweep_kernel(batch_total, *refs),
        in_specs=[VMEM, VMEM if held else HBM],
        out_specs=VMEM,
        out_shape=jax.ShapeDtypeStruct((copies, 1, cols + extra * rows), F32),
        scratch_shapes=[pltpu.VMEM((rows, LANES), F32)] + stream_scratch(expo, held),
        compiler_params=HELD if held else PARAMS,
        cost_estimate=pl.CostEstimate(
            flops=2 * rows * cols, bytes_accessed=2 * rows * cols, transcendentals=0
        ),
        name="col_sweep",
    )(row_parts, expo)


def last_sweep_kernel(
    proto_total, place, col_parts, expo, dirs, unit, student, row_part, own, other, scale, scaled
):
    rows, cols = expo.shape
    width = dirs.shape[0]
    copies = row_part.shape[0]
    half = rows // 2
    wide = 1.0 / (proto_total * jnp.sum(col_parts[:, :, :cols], axis=0))
    scale[...] = jnp.broadcast_to(wide, scale.shape)
    scaled[...] = (dirs[...].astype(F32) * wide).astype(BF16)
    second = place[0] == 1
    products = []
    for first in range(0, rows, half):
        here = slice(first, first + half)
        product = dot_rows(expo[here, :], scaled[...])
        products.append(product)
        meet = fold_lanes(product * unit[here, :].astype(F32))
        row_part[:, 1:2, here] = tall(row_to_lanes(meet), copies)
    for here in row_slices(expo):
        row_part[:, 0:1, here] = tall(scaled_row_sums(expo, here, scale), copies)
    own[:, :width] = jnp.where(second, student[half:, :], student[:half, :])
    other[:, :width] = jnp.where(second, student[:half, :], student[half:, :])
    own[:, width:] = jnp.where(second, products[1], products[0])
    other[:, width:] = jnp.where(second, products[0], products[1])


def last_sweep(proto_total, place, col_parts, expo, dirs, unit, student, copies):
    rows, cols = expo.shape
    width = dirs.shape[0]
    half = (rows // 2, 2 * width)
    return pl.pallas_call(
        lambda *refs: last_sweep_kernel(proto_total, *refs),
        in_specs=[SMEM] + [VMEM] * 5,
        out_specs=[VMEM] * 4,
        out_shape=[
            jax.ShapeDtypeStruct((copies, 2, rows), F32),
            jax.ShapeDtypeStruct(half, F32),
            jax.ShapeDtypeStruct(half, F32),
            jax.ShapeDtypeStruct((8, cols), F32),
        ],
        scratch_shapes=[pltpu.VMEM((width, cols), BF16)],
        compiler_params=HELD,
        cost_estimate=pl.CostEstimate(
            flops=2 * rows * cols * (width + 1),
            bytes_accessed=2 * rows * cols + 2 * width * cols,
            transcendentals=0,
        ),
        name="last_sweep",
    )(place, col_parts, expo, dirs, unit, student)


def wide_kernel(
    place, both, totals, t_protos, s_protos, after, expo, turned, dirs, inverse, mixed, t_dirs
):
    @pl.when(pl.program_id(0) == 0)
    def _():
        t_dirs[...] = unit_cols(t_protos[...].astype(F32))[0]
        dirs[...], norms = unit_cols(s_protos[...].astype(F32))
        inverse[...] = 1.0 / norms
        mixed[...] = jnp.zeros_like(mixed)

    width, cols = dirs.shape
    teacher = both[:, :width].astype(BF16)
    student = both[:, width:].astype(BF16)
    across = student.T
    turned[...] = across
    log_total = lanes_to_rows(jnp.log2(totals[0]))
    shift = jnp.concatenate([log_total] * (BLOCK // LANES), axis=1)
    for first in range(0, cols, BLOCK):
        here = slice(first, first + BLOCK)
        expo[:, here] = jnp.exp2(dot(teacher, t_dirs[:, here]) * teacher_rate).astype(BF16)
        chance = jnp.exp2(dot(student, dirs[:, here]) * student_rate - shift).astype(BF16)
        mixed[:, here] += dot(across, chance)


def wide_call(place, gathered, col_parts, t_protos, s_protos, after, shares, blocks):
    crops, double = gathered.shape
    width = double // 2
    rows = crops // blocks
    cols = t_protos.shape[1] // shares
    last = col_parts.shape[2] // rows - 1
    return pl.pallas_call(
        wide_kernel,
        grid_spec=pltpu.PrefetchScalarGridSpec(
            num_scalar_prefetch=1,
            grid=(blocks,),
            in_specs=[
                pl.BlockSpec((rows, double), lambda i, place: (i, 0)),
                pl.BlockSpec((1, 1, rows), lambda i, place: (2 * i + place[4], 0, last)),
                pl.BlockSpec((width, cols), lambda i, place: (0, place[2])),
                pl.BlockSpec((width, cols), lambda i, place: (0, place[2])),
                whole(TOKEN),
            ],
            out_specs=[
                pl.BlockSpec((rows, cols), lambda i, place: (i, 0)),
                pl.BlockSpec((width, rows), lambda i, place: (0, i)),
                whole((width, cols)),
                whole((1, cols)),
                whole((width, cols)),
            ],
            scratch_shapes=[pltpu.VMEM((width, cols), BF16)],
        ),
        out_shape=[
            jax.ShapeDtypeStruct((crops, cols), BF16),
            jax.ShapeDtypeStruct((width, crops), BF16),
            jax.ShapeDtypeStruct((width, cols), BF16),
            jax.ShapeDtypeStruct((1, cols), F32),
            jax.ShapeDtypeStruct((width, cols), F32),
        ],
        compiler_params=PARAMS,
        cost_estimate=pl.CostEstimate(
            flops=6 * crops * cols * width,
            bytes_accessed=4 * crops * double + 2 * crops * cols,
            transcendentals=2 * crops * cols,
        ),
        name="wide_products",
    )(place, gathered, col_parts, t_protos, s_protos, after)


def finish_kernel(
    place, row_parts, totals, turned, expo, scale, far_scale, dirs, inverse, mixed, grad, loss, *scratch
):
    across, store, total, dirs_v, mixed_v, sems = scratch
    rows = totals.shape[2]
    copies = []
    late = [
        pltpu.make_async_copy(dirs, dirs_v, sems.at[0, across.shape[1] // BLOCK]),
        pltpu.make_async_copy(mixed, mixed_v, sems.at[1, across.shape[1] // BLOCK]),
    ]
    for i in range(totals.shape[0] // 2):
        for first in range(i * rows, (i + 1) * rows, BLOCK):
            here = slice(first, first + BLOCK)
            k = first // BLOCK
            copies.append(
                (
                    here,
                    pltpu.make_async_copy(turned.at[:, here], across.at[:, here], sems.at[0, k]),
                    pltpu.make_async_copy(expo.at[here, :], store.at[here, :], sems.at[1, k]),
                )
            )
    for _, one, two in copies:
        one.start()
        two.start()
    for copy in late:
        copy.start()
    sources = row_parts.shape[0] // (totals.shape[0] // 2)
    terms = jnp.zeros((1, rows), F32)
    done = 0
    for i in range(totals.shape[0] // 2):
        sums = jnp.sum(row_parts[i * sources : (i + 1) * sources], axis=0)
        reciprocal = 1.0 / sums[0:1]
        meet = sums[1:2] * reciprocal * (1.0 / student_temp)
        terms = terms + jnp.log(totals[2 * i + place[4]]) - meet
        for first in range(0, rows, BLOCK):
            here, one, two = copies[done]
            one.wait()
            two.wait()
            factor = reciprocal[:, first : first + BLOCK]
            weighted = (across[:, here].astype(F32) * factor).astype(BF16)
            product = dot(weighted, store[here, :])
            total[...] = product if done == 0 else total[...] + product
            done += 1
    for copy in late:
        copy.wait()
    factor = jnp.where(place[6] == 1, scale[0:1], far_scale[0:1])
    values = mixed_v[...] - factor * total[...]
    wide = dirs_v[...].astype(F32)
    dots = jnp.sum(values * wide, axis=0, keepdims=True)
    values = (values - wide * dots) * (inverse[...] * (1.0 / student_temp))
    grad[...] = values.reshape(grad.shape)
    loss[...] = jnp.broadcast_to(jnp.sum(terms, axis=1, keepdims=True), loss.shape)


def finish_call(
    place, row_parts, col_parts, turned, expo, scale, far_scale, dirs, inverse, mixed, pieces
):
    crops, cols = expo.shape
    width = dirs.shape[0]
    chips = col_parts.shape[0]
    rows = 2 * crops // chips
    last = col_parts.shape[2] // rows - 1
    out = (pieces, width // pieces, cols)
    return pl.pallas_call(
        finish_kernel,
        grid_spec=pltpu.PrefetchScalarGridSpec(
            num_scalar_prefetch=1,
            grid=(1,),
            in_specs=[
                whole(row_parts.shape),
                pl.BlockSpec((chips, 1, rows), lambda i, place: (0, 0, last)),
                HBM,
                HBM,
                pl.BlockSpec((8, cols), lambda i, place: (0, place[3])),
                pl.BlockSpec((8, cols), lambda i, place: (0, place[3])),
                HBM,
                whole((1, cols)),
                HBM,
            ],
            out_specs=[whole(out), whole((1, LANES))],
            scratch_shapes=[
                pltpu.VMEM((width, crops), BF16),
                pltpu.VMEM((crops, cols), BF16),
                pltpu.VMEM((width, cols), F32),
                pltpu.VMEM((width, cols), BF16),
                pltpu.VMEM((width, cols), F32),
                pltpu.SemaphoreType.DMA((2, 1 + crops // BLOCK)),
            ],
        ),
        out_shape=[
            jax.ShapeDtypeStruct(out, F32),
            jax.ShapeDtypeStruct((1, LANES), F32),
        ],
        compiler_params=PARAMS,
        cost_estimate=pl.CostEstimate(
            flops=2 * crops * cols * width,
            bytes_accessed=2 * crops * width + 2 * crops * cols,
            transcendentals=0,
        ),
        name="finish_protos",
    )(place, row_parts, col_parts, turned, expo, scale, far_scale, dirs, inverse, mixed)


COL_AXES = ("x", "zl")
ROW_AXES = ("c", "zh", "y")
CROP_AXES = ("x", "zl", "c")
GATHER_AXES = ("x", "c")
LAST_AXES = ("x", "c", "zh", "y")
SWAP = [(0, 1), (1, 0)]


def exchange(values, axes):
    return lax.all_to_all(values, axes, 0, 0, tiled=True)


def swap(values, axis):
    return lax.ppermute(values, axis, SWAP)


def pick(values, index):
    return lax.dynamic_index_in_dim(values, index, 0, keepdims=False)


def sum_scatter(values):
    near, along = lax.axis_index("zh"), lax.axis_index("y")
    count = values.shape[1]
    half = pick(values, near) + swap(pick(values, 1 - near), "zh")
    total = pick(half, along)
    for step in range(1, count):
        ring = [(i, (i + step) % count) for i in range(count)]
        total = total + lax.ppermute(pick(half, (along + step) % count), "y", ring)
    return total


def on_device(teacher_emb, student_emb, teacher_protos, student_protos):
    core = lax.axis_index("c")
    chip = lax.axis_index(COL_AXES)
    group = lax.axis_index(("zh", "y"))
    chips = lax.axis_size(COL_AXES)
    groups = lax.axis_size(("zh", "y"))
    row_copies = 2 * groups
    shares = lax.axis_size(GATHER_AXES)
    blocks = lax.axis_size("x")
    crops, width = teacher_emb.shape
    batch_total = crops * chips * 2
    proto_total = teacher_protos.shape[1] * groups
    share = lax.axis_index(GATHER_AXES)

    teacher_unit, student_unit, both, place = unit_call(teacher_emb, student_emb)
    teacher_other = swap(teacher_unit, "c")
    gathered = lax.all_gather(both, GATHER_AXES, axis=0, tiled=True)
    student_other = swap(student_unit, "c")
    half = teacher_protos.shape[1] // 2
    half_protos = lax.dynamic_slice_in_dim(teacher_protos, core * half, half, 1)

    expo, col_part = teacher_call(place, teacher_unit, teacher_other, half_protos, chips)
    student_mixed, total_part, dirs, unit = student_call(
        place, student_unit, student_other, student_protos
    )

    col_parts = exchange(col_part, COL_AXES)
    row_part = row_sweep(proto_total, col_parts, expo, row_copies, True)
    row_parts = exchange(row_part, ROW_AXES)
    col_part = col_sweep(batch_total, row_parts, expo, chips, True)
    col_parts = exchange(col_part, COL_AXES)
    row_part = row_sweep(proto_total, col_parts, expo, row_copies, True, (total_part,))
    row_parts = exchange(row_part, ROW_AXES)
    col_part = col_sweep(batch_total, row_parts, expo, chips, True)
    col_parts = exchange(col_part, COL_AXES)
    row_part, own_part, other_part, scale = last_sweep(
        proto_total, place, col_parts, expo, dirs, unit, student_mixed, blocks * row_copies
    )
    row_parts = exchange(row_part, LAST_AXES)
    wide_expo, turned, wide_dirs, inverse, wide_mixed = wide_call(
        place, gathered, col_parts, teacher_protos, student_protos, scale, shares, blocks
    )
    far_scale = swap(scale, "c")

    grad_rows, terms = finish_call(
        place, row_parts, col_parts, turned, wide_expo, scale, far_scale, wide_dirs, inverse,
        wide_mixed, 2 * chips,
    )
    loss = (terms + swap(terms, "zl"))[0, 0] / batch_total
    grad_rows = exchange(grad_rows, CROP_AXES)
    own_rows, cols = grad_rows.shape[1:]
    grad_rows = grad_rows.reshape(blocks, 2, 2, own_rows, cols)
    grad_rows = grad_rows[:, 0] + grad_rows[:, 1]
    grad_prototypes = jnp.moveaxis(grad_rows, 2, 0).reshape(own_rows, shares * cols)

    rows = crops // groups
    far_part, wide_mixed = lax.optimization_barrier((swap(other_part, "c"), wide_mixed))
    summed = sum_scatter(
        (own_part + far_part).reshape(
            lax.axis_size("zh"), lax.axis_size("y"), rows, 2 * width
        )
    )
    first = core * crops + group * rows
    sources = lax.dynamic_slice(
        row_parts, (lax.axis_index("x") * row_copies, 0, first), (row_copies, 1, rows)
    )
    row_sum = jnp.sum(sources, axis=(0, 1))
    total = lax.dynamic_slice(
        col_parts, (chip, 0, col_parts.shape[2] - 2 * crops + first), (1, 1, rows)
    ).reshape(rows)
    grad_unit = summed[:, :width] / total[:, None] - summed[:, width:] / row_sum[:, None]
    grad_unit = grad_unit / student_temp
    own_emb = lax.dynamic_slice_in_dim(student_emb, group * rows, rows, 0)
    s_unit, s_norm = unit_rows(own_emb.astype(F32))
    along = jnp.sum(s_unit * grad_unit, axis=1, keepdims=True)
    grad_embeddings = (grad_unit - s_unit * along) / s_norm
    return (grad_embeddings, grad_prototypes, loss)


def solution(mesh):
    fine = Mesh(mesh.devices.reshape(4, 2, 2, 2, 4), ("x", "zl", "c", "zh", "y"))
    crops, protos = ("x", "zl", "c"), ("zh", "y")
    return jax.shard_map(
        on_device,
        mesh=fine,
        in_specs=(P(crops, None), P(crops, None), P(None, protos), P(None, protos)),
        out_specs=(P(crops + protos, None), P(crops, protos), P()),
        check_vma=False,
    )
```

time: 497 us -> 165 us (0.33)
  blocking collectives: 342 us -> 49 us
  other arithmetic: 63.8 us -> 6.83 us
  Pallas kernels: 0 us -> 48.7 us
  waiting for transfers between devices: 37.3 us -> 4.4 us
  matrix products: 31.3 us -> 0 us
  starting transfers between devices: 0.08 us -> 26.2 us
  local copies, waits for them, and re-layouts: 5.18 us -> 13.4 us
    psum x8 -> x0, blocking collectives: 342 us -> none  [the longest x3 167 us: column_total(): return lax.psum(partial_sum, 'dp')]
    reduce_sum x9 -> x2, other arithmetic: 57.8 us -> 1.78 us  [the longest x1 0.96 us: on_device(): along = jnp.sum(s_unit * grad_unit, axis=1, keepdims=True)]
    all_to_all x0 -> x4, blocking collectives: none -> 49 us  [exchange(): return lax.all_to_all(values, axes, 0, 0, tiled=True)]
    pallas_call x0 -> x10, Pallas kernels: none -> 48.7 us  [the longest x1 11.9 us: wide_call(): pl.pallas_call(wide_kernel, grid_spec=pltpu.PrefetchScalarGridSpec(num_sc...]
    reduce_scatter x2 -> x0, waiting for transfers between devices: 37.3 us -> none  [the longest x1 37.2 us: on_device(): lax.psum_scatter(product / student_temp, 'dp', scatter_dimension=0, tiled...]
    dot_general x4 -> x0, matrix products: 31.3 us -> none  [the longest x1 11.6 us: on_device(): jnp.dot(t_round, t_wn, preferred_element_type=jnp.float32) / teacher_temp]
    all_to_all x0 -> x3, starting transfers between devices: none -> 13.2 us  [exchange(): return lax.all_to_all(values, axes, 0, 0, tiled=True)]
    ppermute x0 -> x9, starting transfers between devices: none -> 13 us  [the longest x6 8.14 us: swap(): return lax.ppermute(values, axis, SWAP)]
  transfers between devices with their start and end apart: 2 -> 13, of which waited for: 1 -> 4; matrix products, arithmetic and copies ran while one was open for 2% -> 6% of each run, Pallas kernels for 0% -> 29%
where the time goes in v3:
time: 165 us; the launch traced here: 164 us
  blocking collectives  49 us (30%)
  Pallas kernels  48.7 us (30%)
  starting transfers between devices  26.2 us (16%)
  between operations  15.5 us (9%)
  local copies, waits for them, and re-layouts  13.4 us (8%)
  other arithmetic  6.83 us (4%)
  waiting for transfers between devices  4.4 us (3%)
    all_to_all x4, blocking collectives, exchange(): return lax.all_to_all(values, axes, 0, 0, tiled=True)  49 us
    all_to_all x3, starting transfers between devices, exchange(): return lax.all_to_all(values, axes, 0, 0, tiled=True)  13.2 us
    pallas_call x1, Pallas kernels, wide_call(): pl.pallas_call(wide_kernel, grid_spec=pltpu.PrefetchScalarGridSpec(num_sc...  11.9 us
    pallas_call x1, Pallas kernels, student_call(): pl.pallas_call(student_kernel, in_specs=[SMEM, HBM, HBM, HBM], out_specs=...  9.5 us
    unnamed x40, local copies, waits for them, and re-layouts  8.41 us
    ppermute x6, starting transfers between devices, swap(): return lax.ppermute(values, axis, SWAP)  8.14 us
    pallas_call x1, Pallas kernels, finish_call(): pl.pallas_call(finish_kernel, grid_spec=pltpu.PrefetchScalarGridSpec(num_...  7.89 us
    pallas_call x1, Pallas kernels, last_sweep(): pl.pallas_call(lambda *refs: last_sweep_kernel(proto_total, *refs), in_sp...  5.59 us
  transfers between devices with their start and end apart: 13, of which 4 were waited for; matrix products, arithmetic and copies ran while one was open for 6% of the time, Pallas kernels for 29%

profile of v3, /device:TPU:1, one launch (start us, length us, event | category | flops | bytes accessed | tf_op | source)
XLA Modules:
  0.0 164.0 jit_solution(5748673757083787568)
XLA Ops:
  9.1 1.4 unit_rows.1
  10.5 1.5 collective-permute-start
  12.1 1.8 %constant_dynamic-slice_fusion.1.protos = bf16[256,4096]{1,0:T(8,128)(2,1)S(1)} fusion(bf16[256,8192]{1,0:T(8,128)(2,1)} %t_protos.1, s32[]{:T(128)S(6)} %select_n.53), kind=kLoop, calls=%fused_computation.24 | loop fusion | bytes 4194308 | tf_op jit(solution)/shard_map/dynamic_slice | solution.py:603
  13.9 3.7 %teacher_expo.1 = (bf16[1024,4096]{1,0:T(8,128)(2,1)S(1)}, f32[8,1,4096]{2,1,0:T(1,128)S(1)}) custom-call(s32[7]{0:T(128)S(1)} %get-tuple-element.25.place.refs_0_, f32[512,256]{1,0:T(8,128)S(1)} %get-tuple-element.26.own, f32[512,256]{1,0:T(8,128)S(1)} %collective-permute-done.other, bf16[256,4096]{1,0:T(8,128)(2,1)S(1)} %constant_dynamic-slice_fusion.1.protos), custom_call_target="tpu_custom_call" | custom-call | flops 2147483648 | bytes 10485760 | tf_op jit(solution)/shard_map/teacher_expo/pallas_call | solution.py:133
  17.6 10.7 %all_to_all.35.refs_0_ = f32[8,1,4096]{2,1,0:T(1,128)S(1)} all-to-all(f32[8,1,4096]{2,1,0:T(1,128)S(1)} %get-tuple-element.27), channel_id=1, replica_groups=mesh['x'=4,'zl'=2,'c'=2,'zh'=2,'y'=4] {'x','zl'}, dimensions={0} | all-to-all | bytes 262144 | tf_op jit(solution)/shard_map/all_to_all | solution.py:562
  28.3 1.8 %row_sweep.2 = f32[16,1,1024]{2,1,0:T(1,128)S(1)} custom-call(f32[8,1,4096]{2,1,0:T(1,128)S(1)} %all_to_all.35.refs_0_, bf16[1024,4096]{1,0:T(8,128)(2,1)S(1)} %get-tuple-element.28.refs_1_.refs_2_), custom_call_target="tpu_custom_call" | custom-call | flops 8388608 | bytes 8388608 | tf_op jit(solution)/shard_map/row_sweep/pallas_call | solution.py:277
  30.1 17.1 %all_to_all.36.refs_0_ = f32[16,1,1024]{2,1,0:T(1,128)S(1)} all-to-all(f32[16,1,1024]{2,1,0:T(1,128)S(1)} %row_sweep.2), channel_id=1, replica_groups=mesh['x'=4,'zl'=2,'c'=2,'zh'=2,'y'=4] {'c','zh','y'}, dimensions={0} | all-to-all | bytes 131072 | tf_op jit(solution)/shard_map/all_to_all | solution.py:562
  47.1 2.7 %col_sweep.2 = f32[8,1,4096]{2,1,0:T(1,128)} custom-call(f32[16,1,1024]{2,1,0:T(1,128)S(1)} %all_to_all.36.refs_0_, bf16[1024,4096]{1,0:T(8,128)(2,1)S(1)} %get-tuple-element.28.refs_1_.refs_2_), custom_call_target="tpu_custom_call" | custom-call | flops 8388608 | bytes 8388608 | tf_op jit(solution)/shard_map/col_sweep/pallas_call | solution.py:317
  49.9 3.6 %all-to-all-start.2 = ((f32[8,1,4096]{2,1,0:T(1,128)}), f32[8,1,4096]{2,1,0:T(1,128)S(1)}, u32[]{:S(2)}, u32[]{:S(2)}) async-start(f32[8,1,4096]{2,1,0:T(1,128)} %col_sweep.2), calls=%async_computation.2 | async-start | bytes 262144 | tf_op jit(solution)/shard_map/all_to_all | solution.py:562
  54.3 9.5 %student_totals.1 = (f32[1024,256]{1,0:T(8,128)}, f32[1,1024]{1,0:T(1,128)}, bf16[256,4096]{1,0:T(8,128)(2,1)}, bf16[1024,256]{1,0:T(8,128)(2,1)}) custom-call(s32[7]{0:T(128)} %copy-done.11, f32[512,256]{1,0:T(8,128)} %copy-done.13, f32[512,256]{1,0:T(8,128)} %copy-done.16, bf16[256,8192]{1,0:T(8,128)(2,1)} %s_protos.1), custom_call_target="tpu_custom_call" | custom-call | flops 4294967296 | bytes 5242880 | tf_op jit(solution)/shard_map/student_totals/pallas_call | solution.py:196
  63.8 3.5 %copy-done.1 = bf16[1024,4096]{1,0:T(8,128)(2,1)S(1)} copy-done((bf16[1024,4096]{1,0:T(8,128)(2,1)S(1)}, bf16[1024,4096]{1,0:T(8,128)(2,1)}, u32[]{:S(2)}) %copy-start.1) | copy-done | bytes 8388632
  67.9 1.8 %row_sweep.3 = f32[16,2,1024]{2,1,0:T(2,128)S(1)} custom-call(f32[8,1,4096]{2,1,0:T(1,128)S(1)} %all-to-all-done.2.refs_0_, bf16[1024,4096]{1,0:T(8,128)(2,1)S(1)} %copy-done.1, f32[1,1024]{1,0:T(1,128)S(1)} %copy-done.10), custom_call_target="tpu_custom_call" | custom-call | flops 8388608 | bytes 8388608 | tf_op jit(solution)/shard_map/row_sweep/pallas_call | solution.py:277
  69.8 10.7 %all_to_all.37.refs_0_ = f32[16,2,1024]{2,1,0:T(2,128)S(1)} all-to-all(f32[16,2,1024]{2,1,0:T(2,128)S(1)} %row_sweep.3), channel_id=1, replica_groups=mesh['x'=4,'zl'=2,'c'=2,'zh'=2,'y'=4] {'c','zh','y'}, dimensions={0} | all-to-all | bytes 262144 | tf_op jit(solution)/shard_map/all_to_all | solution.py:562
  80.6 2.5 %col_sweep.3 = f32[8,1,5120]{2,1,0:T(1,128)S(1)} custom-call(f32[16,2,1024]{2,1,0:T(2,128)S(1)} %all_to_all.37.refs_0_, bf16[1024,4096]{1,0:T(8,128)(2,1)S(1)} %copy-done.1), custom_call_target="tpu_custom_call" | custom-call | flops 8388608 | bytes 8388608 | tf_op jit(solution)/shard_map/col_sweep/pallas_call | solution.py:317
  83.0 10.5 %all_to_all.38.refs_1_.totals = f32[8,1,5120]{2,1,0:T(1,128)S(1)} all-to-all(f32[8,1,5120]{2,1,0:T(1,128)S(1)} %col_sweep.3), channel_id=1, replica_groups=mesh['x'=4,'zl'=2,'c'=2,'zh'=2,'y'=4] {'x','zl'}, dimensions={0} | all-to-all | bytes 327680 | tf_op jit(solution)/shard_map/all_to_all | solution.py:562
  93.5 5.6 %last_sweep.1 = (f32[64,2,1024]{2,1,0:T(2,128)}, f32[512,512]{1,0:T(8,128)S(1)}, f32[512,512]{1,0:T(8,128)S(1)}, f32[8,4096]{1,0:T(8,128)S(1)}) custom-call(s32[7]{0:T(128)S(1)} %copy-done.12, f32[8,1,5120]{2,1,0:T(1,128)S(1)} %all_to_all.38.refs_1_.totals, bf16[1024,4096]{1,0:T(8,128)(2,1)S(1)} %bitcast.27, bf16[256,4096]{1,0:T(8,128)(2,1)S(1)} %copy-done.2, ...), custom_call_target="tpu_custom_call" | custom-call | flops 2155872256 | bytes 10485760 | tf_op jit(solution)/shard_map/last_sweep/pallas_call | solution.py:361
  99.8 1.7 %collective-permute-start.2 = (f32[512,512]{1,0:T(8,128)S(1)}, f32[512,512]{1,0:T(8,128)}, u32[]{:S(2)}, u32[]{:S(2)}) collective-permute-start(f32[512,512]{1,0:T(8,128)S(1)} %get-tuple-element.35), channel_id=1, source_target_pairs={{0,8},{8,0},{1,9},{9,1},{2,10},{10,2},{3,11},{11,3},{4,12},{12,4},... | collective-permute-start | bytes 3145736 | tf_op jit(solution)/shard_map/ppermute | solution.py:566
  101.5 4.9 %all-to-all-start.5 = ((f32[64,2,1024]{2,1,0:T(2,128)}), f32[64,2,1024]{2,1,0:T(2,128)S(1)}, u32[]{:S(2)}, u32[]{:S(2)}) async-start(f32[64,2,1024]{2,1,0:T(2,128)} %get-tuple-element.40), calls=%async_computation.5 | async-start | bytes 1048576 | tf_op jit(solution)/shard_map/all_to_all | solution.py:562
  106.4 11.9 %wide_products.1 = (bf16[4096,1024]{1,0:T(8,128)(2,1)}, bf16[256,4096]{1,0:T(8,128)(2,1)}, bf16[256,1024]{1,0:T(8,128)(2,1)}, f32[1,1024]{1,0:T(1,128)}, f32[256,1024]{1,0:T(8,128)}) custom-call(s32[7]{0:T(128)} %copy-done.11, f32[4096,512]{1,0:T(8,128)} %all-gather.2.cloned.1.call-done.both, f32[8,1,5120]{2,1,0:T(1,128)} %copy-done.3, ...), custom_call_target="tpu_custom_call" | custom-call | flops 6442450944 | bytes 16777216 | tf_op jit(solution)/shard_map/wide_products/pallas_call | solution.py:412
  118.3 1.5 add.111
  120.6 2.9 %collective-permute-start.3 = (f32[4,64,512]{2,1,0:T(8,128)}, f32[4,64,512]{2,1,0:T(8,128)}, u32[]{:S(2)}, u32[]{:S(2)}) collective-permute-start(f32[4,64,512]{2,1,0:T(8,128)} %dynamic-slice_bitcast_fusion), channel_id=1, source_target_pairs={{0,4},{4,0},{1,5},{5,1},{2,6},{6,2},{3,7},{7,3},{8,12},{12,8},{9,1... | collective-permute-start | bytes 1572872 | tf_op jit(solution)/shard_map/ppermute | solution.py:566
  125.9 7.9 %finish_protos.1 = (f32[16,16,1024]{2,1,0:T(8,128)}, f32[1,128]{1,0:T(1,128)}) custom-call(s32[7]{0:T(128)} %copy-done.11, f32[64,2,1024]{2,1,0:T(2,128)} %copy-done.14, f32[8,1,5120]{2,1,0:T(1,128)} %copy-done.3, bf16[256,4096]{1,0:T(8,128)(2,1)} %get-tuple-element.41.turned, bf16[4096,1024]{1,0:T(8,128)(2,1)} %get-tuple-element.42.expo, ...), custom_call_target="tpu_custom_call" | custom-call | flops 2147483648 | bytes 10485760 | tf_op jit(solution)/shard_map/finish_protos/pallas_call | solution.py:513
  133.9 4.7 %all-to-all-start.6 = ((f32[16,16,1024]{2,1,0:T(8,128)}), f32[16,16,1024]{2,1,0:T(8,128)S(1)}, u32[]{:S(2)}, u32[]{:S(2)}) async-start(f32[16,16,1024]{2,1,0:T(8,128)} %get-tuple-element.45), calls=%async_computation.6 | async-start | bytes 2097152 | tf_op jit(solution)/shard_map/all_to_all | solution.py:562
  138.6 1.1 bitcast_add_fusion
  139.8 1.3 collective-permute-start.4
  141.1 2.4 %collective-permute-start.5 = (f32[64,512]{1,0:T(8,128)S(1)}, f32[64,512]{1,0:T(8,128)S(1)}, u32[]{:S(2)}, u32[]{:S(2)}) collective-permute-start(f32[64,512]{1,0:T(8,128)S(1)} %get-tuple-element.51), channel_id=1, source_target_pairs={{0,2},{1,3},{2,0},{3,1},{4,6},{5,7},{6,4},{7,5},{8,10},{9,11},{10,... | collective-permute-start | bytes 393224 | tf_op jit(solution)/shard_map/ppermute | solution.py:580
  143.5 1.2 collective-permute-start.6
  145.4 1.4 collective-permute-start.8
  148.1 1.8 %collective-permute-done.5 = f32[64,512]{1,0:T(8,128)S(1)} collective-permute-done((f32[64,512]{1,0:T(8,128)S(1)}, f32[64,512]{1,0:T(8,128)S(1)}, u32[]{:S(2)}, u32[]{:S(2)}) %collective-permute-start.5) | collective-permute-done | bytes 131104 | tf_op jit(solution)/shard_map/ppermute | solution.py:580
  150.9 1.5 fusion.7
  152.4 1.9 %all-to-all-done.6 = f32[16,16,1024]{2,1,0:T(8,128)S(1)} async-done(((f32[16,16,1024]{2,1,0:T(8,128)}), f32[16,16,1024]{2,1,0:T(8,128)S(1)}, u32[]{:S(2)}, u32[]{:S(2)}) %all-to-all-start.6) | async-done | bytes 1048608 | tf_op jit(solution)/shard_map/all_to_all | solution.py:562
  154.8 1.2 reshape.33
  (66 shorter events, 11.1 us)
Async XLA Ops:
  7.2 99.2 %all-gather.2.cloned.1.call-start = ((), (), s32[]{:S(2)}) async-start(), calls=%async_computation.7 | async-start | bytes 9437184 | tf_op jit(solution)/shard_map/all_gather | solution.py:600
  7.2 1.0 copy-start.6
  8.2 0.9 copy-start.7
  10.5 7.1 %copy-start.11 = (s32[7]{0:T(128)}, s32[7]{0:T(128)S(1)}, u32[]{:S(2)}) copy-start(s32[7]{0:T(128)S(1)} %get-tuple-element.25.place.refs_0_) | copy-start | bytes 88
  10.5 7.1 %copy-start.13 = (f32[512,256]{1,0:T(8,128)}, f32[512,256]{1,0:T(8,128)S(1)}, u32[]{:S(2)}) copy-start(f32[512,256]{1,0:T(8,128)S(1)} %get-tuple-element.29.own) | copy-start | bytes 1572868
  10.5 3.4 %collective-permute-start = (f32[512,256]{1,0:T(8,128)S(1)}, f32[512,256]{1,0:T(8,128)S(1)}, u32[]{:S(2)}, u32[]{:S(2)}) collective-permute-start(f32[512,256]{1,0:T(8,128)S(1)} %get-tuple-element.26.own), channel_id=1, source_target_pairs={{0,8},{8,0},{1,9},{9,1},{2,10},{10,2},{3,11},{11,3},{4,12},{12,4},... | collective-permute-start | bytes 1572872 | tf_op jit(solution)/shard_map/ppermute | solution.py:566
  12.0 41.4 %collective-permute-start.1 = (f32[512,256]{1,0:T(8,128)S(1)}, f32[512,256]{1,0:T(8,128)S(1)}, u32[]{:S(2)}, u32[]{:S(2)}) collective-permute-start(f32[512,256]{1,0:T(8,128)S(1)} %get-tuple-element.29.own), channel_id=1, source_target_pairs={{0,8},{8,0},{1,9},{9,1},{2,10},{10,2},{3,11},{11,3},{4,12},{12,4},... | collective-permute-start | bytes 1572872 | tf_op jit(solution)/shard_map/ppermute | solution.py:566
  17.6 29.5 %copy-start = (bf16[1024,4096]{1,0:T(8,128)(2,1)}, bf16[1024,4096]{1,0:T(8,128)(2,1)S(1)}, u32[]{:S(2)}) copy-start(bf16[1024,4096]{1,0:T(8,128)(2,1)S(1)} %get-tuple-element.28.refs_1_.refs_2_) | copy-start | bytes 25165828
  49.9 13.9 %all-to-all-start.2 = ((f32[8,1,4096]{2,1,0:T(1,128)}), f32[8,1,4096]{2,1,0:T(1,128)S(1)}, u32[]{:S(2)}, u32[]{:S(2)}) async-start(f32[8,1,4096]{2,1,0:T(1,128)} %col_sweep.2), calls=%async_computation.2 | async-start | bytes 262144 | tf_op jit(solution)/shard_map/all_to_all | solution.py:562
  53.4 0.8 copy-start.16
  63.8 3.5 %copy-start.1 = (bf16[1024,4096]{1,0:T(8,128)(2,1)S(1)}, bf16[1024,4096]{1,0:T(8,128)(2,1)}, u32[]{:S(2)}) copy-start(bf16[1024,4096]{1,0:T(8,128)(2,1)} %copy-done) | copy-start | bytes 25165828
  67.2 0.7 copy-start.10
  67.9 25.6 %slice-start = ((s8[8388608]{0:T(1024)(128)(4,1)}), s8[4194304]{0:T(1024)(128)(4,1)S(1)}, s32[]{:S(2)}) async-start(s8[8388608]{0:T(1024)(128)(4,1)} %bitcast.26), calls=%async_computation.8 | async-start | bytes 8388608
  80.5 13.0 %slice-start.1 = ((s8[8388608]{0:T(1024)(128)(4,1)}), s8[4194304]{0:T(1024)(128)(4,1)S(1)}, s32[]{:S(2)}) async-start(s8[8388608]{0:T(1024)(128)(4,1)} %bitcast.26), calls=%async_computation.9 | async-start | bytes 8388608
  80.5 13.0 %copy-start.2 = (bf16[256,4096]{1,0:T(8,128)(2,1)S(1)}, bf16[256,4096]{1,0:T(8,128)(2,1)}, u32[]{:S(2)}) copy-start(bf16[256,4096]{1,0:T(8,128)(2,1)} %get-tuple-element.31.refs_3_) | copy-start | bytes 6291460
  80.5 13.0 %copy-start.4 = (f32[1024,256]{1,0:T(8,128)S(1)}, f32[1024,256]{1,0:T(8,128)}, u32[]{:S(2)}) copy-start(f32[1024,256]{1,0:T(8,128)} %get-tuple-element.33.refs_5_) | copy-start | bytes 3145732
  80.5 13.0 %copy-start.5 = (bf16[1024,256]{1,0:T(8,128)(2,1)S(1)}, bf16[1024,256]{1,0:T(8,128)(2,1)}, u32[]{:S(2)}) copy-start(bf16[1024,256]{1,0:T(8,128)(2,1)} %get-tuple-element.32.refs_4_) | copy-start | bytes 1572868
  80.5 13.0 %copy-start.12 = (s32[7]{0:T(128)S(1)}, s32[7]{0:T(128)}, u32[]{:S(2)}) copy-start(s32[7]{0:T(128)} %copy-done.11) | copy-start | bytes 88
  93.5 5.6 %copy-start.3 = (f32[8,1,5120]{2,1,0:T(1,128)}, f32[8,1,5120]{2,1,0:T(1,128)S(1)}, u32[]{:S(2)}) copy-start(f32[8,1,5120]{2,1,0:T(1,128)S(1)} %all_to_all.38.refs_1_.totals) | copy-start | bytes 491524
  99.1 0.7 copy-start.8
  99.8 18.5 %collective-permute-start.2 = (f32[512,512]{1,0:T(8,128)S(1)}, f32[512,512]{1,0:T(8,128)}, u32[]{:S(2)}, u32[]{:S(2)}) collective-permute-start(f32[512,512]{1,0:T(8,128)S(1)} %get-tuple-element.35), channel_id=1, source_target_pairs={{0,8},{8,0},{1,9},{9,1},{2,10},{10,2},{3,11},{11,3},{4,12},{12,4},... | collective-permute-start | bytes 3145736 | tf_op jit(solution)/shard_map/ppermute | solution.py:566
  101.5 23.7 %all-to-all-start.5 = ((f32[64,2,1024]{2,1,0:T(2,128)}), f32[64,2,1024]{2,1,0:T(2,128)S(1)}, u32[]{:S(2)}, u32[]{:S(2)}) async-start(f32[64,2,1024]{2,1,0:T(2,128)} %get-tuple-element.40), calls=%async_computation.5 | async-start | bytes 1048576 | tf_op jit(solution)/shard_map/all_to_all | solution.py:562
  118.3 5.2 %copy-start.9 = (f32[8,4096]{1,0:T(8,128)S(1)}, f32[8,4096]{1,0:T(8,128)}, u32[]{:S(2)}) copy-start(f32[8,4096]{1,0:T(8,128)} %copy-done.8) | copy-start | bytes 393220
  120.6 18.0 %collective-permute-start.3 = (f32[4,64,512]{2,1,0:T(8,128)}, f32[4,64,512]{2,1,0:T(8,128)}, u32[]{:S(2)}, u32[]{:S(2)}) collective-permute-start(f32[4,64,512]{2,1,0:T(8,128)} %dynamic-slice_bitcast_fusion), channel_id=1, source_target_pairs={{0,4},{4,0},{1,5},{5,1},{2,6},{6,2},{3,7},{7,3},{8,12},{12,8},{9,1... | collective-permute-start | bytes 1572872 | tf_op jit(solution)/shard_map/ppermute | solution.py:566
  123.5 1.6 collective-permute-start.7
  125.1 0.8 copy-start.14
  133.8 11.5 %copy-start.17 = (f32[1,128]{1,0:T(1,128)S(1)}, f32[1,128]{1,0:T(1,128)}, u32[]{:S(2)}) copy-start(f32[1,128]{1,0:T(1,128)} %get-tuple-element.46) | copy-start | bytes 1540
  133.9 20.5 %all-to-all-start.6 = ((f32[16,16,1024]{2,1,0:T(8,128)}), f32[16,16,1024]{2,1,0:T(8,128)S(1)}, u32[]{:S(2)}, u32[]{:S(2)}) async-start(f32[16,16,1024]{2,1,0:T(8,128)} %get-tuple-element.45), calls=%async_computation.6 | async-start | bytes 2097152 | tf_op jit(solution)/shard_map/all_to_all | solution.py:562
  139.8 8.3 %collective-permute-start.4 = (f32[64,512]{1,0:T(8,128)S(1)}, f32[64,512]{1,0:T(8,128)S(1)}, u32[]{:S(2)}, u32[]{:S(2)}) collective-permute-start(f32[64,512]{1,0:T(8,128)S(1)} %get-tuple-element.49), channel_id=1, source_target_pairs={{0,1},{1,2},{2,3},{3,0},{4,5},{5,6},{6,7},{7,4},{8,9},{9,10},{10,1... | collective-permute-start | bytes 393224 | tf_op jit(solution)/shard_map/ppermute | solution.py:580
  141.1 8.8 %collective-permute-start.5 = (f32[64,512]{1,0:T(8,128)S(1)}, f32[64,512]{1,0:T(8,128)S(1)}, u32[]{:S(2)}, u32[]{:S(2)}) collective-permute-start(f32[64,512]{1,0:T(8,128)S(1)} %get-tuple-element.51), channel_id=1, source_target_pairs={{0,2},{1,3},{2,0},{3,1},{4,6},{5,7},{6,4},{7,5},{8,10},{9,11},{10,... | collective-permute-start | bytes 393224 | tf_op jit(solution)/shard_map/ppermute | solution.py:580
  143.5 6.4 %collective-permute-start.6 = (f32[64,512]{1,0:T(8,128)S(1)}, f32[64,512]{1,0:T(8,128)S(1)}, u32[]{:S(2)}, u32[]{:S(2)}) collective-permute-start(f32[64,512]{1,0:T(8,128)S(1)} %get-tuple-element.50), channel_id=1, source_target_pairs={{0,3},{1,0},{2,1},{3,2},{4,7},{5,4},{6,5},{7,6},{8,11},{9,8},{10,9... | collective-permute-start | bytes 393224 | tf_op jit(solution)/shard_map/ppermute | solution.py:580
  145.4 2.7 %collective-permute-start.8 = (f32[1,128]{1,0:T(1,128)S(1)}, f32[1,128]{1,0:T(1,128)S(1)}, u32[]{:S(2)}, u32[]{:S(2)}) collective-permute-start(f32[1,128]{1,0:T(1,128)S(1)} %copy-done.17), channel_id=1, source_target_pairs={{0,16},{16,0},{1,17},{17,1},{2,18},{18,2},{3,19},{19,3},{4,20},{20... | collective-permute-start | bytes 1544 | tf_op jit(solution)/shard_map/ppermute | solution.py:566
  (1 other events, 0.7 us)
Sparse Core Ops, SparseCore 0:
  10.6 55.2 all-gather.1

commit v4 on v3

--- a/solution.py
+++ b/solution.py
@@ -24,6 +24,7 @@
 
 PARAMS = pltpu.CompilerParams(vmem_limit_bytes=61 * MIB)
 HELD = pltpu.CompilerParams(vmem_limit_bytes=20 * MIB)
+TIGHT = pltpu.CompilerParams(vmem_limit_bytes=48 * MIB)
 
 
 def unit_rows(wide):
@@ -66,7 +67,6 @@
 VMEM = pl.BlockSpec(memory_space=pltpu.VMEM)
 SMEM = pl.BlockSpec(memory_space=pltpu.SMEM)
 HBM = pl.BlockSpec(memory_space=pltpu.HBM)
-TOKEN = (8, LANES)
 
 
 def whole(shape):
@@ -85,10 +85,10 @@
     student_unit[...] = second
     both[:, :width] = first
     both[:, width:] = second
-    core, x, near = (lax.axis_index(axis) for axis in ("c", "x", "zl"))
+    core, x, near, far = (lax.axis_index(axis) for axis in ("c", "x", "zl", "zh"))
     share = 2 * x + core
     here = (share // 4 == core).astype(jnp.int32)
-    for i, value in enumerate((core, 2 * x + near, share, share % 4, near, x, here)):
+    for i, value in enumerate((core, 2 * x + near, share, share % 4, near, x, here, far)):
         place[i] = value.astype(jnp.int32)
 
 
@@ -103,7 +103,7 @@
             jax.ShapeDtypeStruct((rows, width), F32),
             jax.ShapeDtypeStruct((rows, width), F32),
             jax.ShapeDtypeStruct((rows, 2 * width), F32),
-            jax.ShapeDtypeStruct((7,), jnp.int32),
+            jax.ShapeDtypeStruct((8,), jnp.int32),
         ],
         compiler_params=HELD,
         name="unit_rows",
@@ -124,10 +124,10 @@
         directions, _ = unit_cols(protos[:, here].astype(F32))
         values = jnp.exp2(dot(unit[...], directions) * teacher_rate)
         expo[:, here] = values.astype(BF16)
-        col_part[:, :, here] = tall(jnp.sum(values, axis=0, keepdims=True), col_part.shape[0])
-
-
-def teacher_call(place, own, other, protos, copies):
+        col_part[:, here] = jnp.sum(values, axis=0, keepdims=True)
+
+
+def teacher_call(place, own, other, protos):
     rows, width = own.shape
     cols = protos.shape[1]
     return pl.pallas_call(
@@ -136,7 +136,7 @@
         out_specs=[VMEM, VMEM],
         out_shape=[
             jax.ShapeDtypeStruct((2 * rows, cols), BF16),
-            jax.ShapeDtypeStruct((copies, 1, cols), F32),
+            jax.ShapeDtypeStruct((1, cols), F32),
         ],
         scratch_shapes=[pltpu.VMEM((2 * rows, width), BF16)],
         compiler_params=HELD,
@@ -149,106 +149,79 @@
     )(place, own, other, protos)
 
 
-def student_kernel(
-    place, own, other, protos, mixed, total_part, dirs, unit, own_v, other_v, store, dirs_v, unit_v, sums, in_sems, out_sems
-):
-    half = store.shape[1]
-    pair = [
-        pltpu.make_async_copy(own, own_v, in_sems.at[0]),
-        pltpu.make_async_copy(other, other_v, in_sems.at[1]),
-    ]
-    incoming, outgoing = [], []
-    for j in range(half // BLOCK):
-        there = pl.ds(pl.multiple_of(place[0] * half + j * BLOCK, BLOCK), BLOCK)
+def add_kernel(one, two, out):
+    out[...] = one[...] + two[...]
+
+
+def add_call(one, two):
+    return pl.pallas_call(
+        add_kernel,
+        in_specs=[VMEM] * 2,
+        out_specs=VMEM,
+        out_shape=jax.ShapeDtypeStruct(one.shape, F32),
+        compiler_params=HELD,
+        name="add_parts",
+    )(one, two)
+
+
+def student_kernel(part, place, one, two, sums_in, protos, mixed, sums, dirs, unit, store, sems):
+    cols = dirs.shape[1]
+    copies = []
+    for j in range(cols // BLOCK):
+        first = (2 * place[0] + part) * cols + j * BLOCK
+        there = pl.ds(pl.multiple_of(first, BLOCK), BLOCK)
         here = pl.ds(j * BLOCK, BLOCK)
-        incoming.append(
-            pltpu.make_async_copy(protos.at[:, there], store.at[:, here], in_sems.at[2 + j])
-        )
-        outgoing.append(
-            pltpu.make_async_copy(dirs_v.at[:, here], dirs.at[:, here], out_sems.at[1 + j])
-        )
-    for copy in pair + incoming:
+        copies.append(pltpu.make_async_copy(protos.at[:, there], store.at[:, here], sems.at[j]))
+    for copy in copies:
         copy.start()
-    for copy in pair:
+    if part == 0:
+        unit[...] = pair_rows(place[0], one[...], two[...])
+        mixed[...] = jnp.zeros_like(mixed)
+    else:
+        unit[...] = one[...]
+        mixed[...] = two[...]
+    total = sums_in[...]
+    for j, copy in enumerate(copies):
+        here = slice(j * BLOCK, (j + 1) * BLOCK)
         copy.wait()
-    unit_v[...] = pair_rows(place[0], own_v[...], other_v[...])
-    unit_out = pltpu.make_async_copy(unit_v, unit, out_sems.at[0])
-    unit_out.start()
-    for j in range(half // BLOCK):
-        here = slice(j * BLOCK, (j + 1) * BLOCK)
-        incoming[j].wait()
         directions, _ = unit_cols(store[:, here].astype(F32))
-        dirs_v[:, here] = directions
-        outgoing[j].start()
-        values = jnp.exp2(dot(unit_v[...], directions) * student_rate)
-        part = fold_lanes(values)
-        product = dot_rows(values.astype(BF16), directions)
-        sums[...] = part if j == 0 else sums[...] + part
-        mixed[...] = product if j == 0 else mixed[...] + product
-    total_part[...] = row_to_lanes(sums[...])
-    for copy in [unit_out] + outgoing:
-        copy.wait()
-
-
-def student_call(place, own, other, protos):
-    rows, width = own.shape
-    cols = protos.shape[1] // 2
-    return pl.pallas_call(
-        student_kernel,
-        in_specs=[SMEM, HBM, HBM, HBM],
-        out_specs=[VMEM, VMEM, HBM, HBM],
+        dirs[:, here] = directions
+        values = jnp.exp2(dot(unit[...], directions) * student_rate)
+        total = total + row_to_lanes(fold_lanes(values))
+        mixed[...] += dot_rows(values.astype(BF16), directions)
+    sums[...] = total
+
+
+def student_call(part, place, one, two, sums, protos):
+    width = protos.shape[0]
+    rows = sums.shape[1]
+    cols = protos.shape[1] // 4
+    return pl.pallas_call(
+        lambda *refs: student_kernel(part, *refs),
+        in_specs=[SMEM, VMEM, VMEM, VMEM, HBM],
+        out_specs=[VMEM] * 4,
         out_shape=[
-            jax.ShapeDtypeStruct((2 * rows, width), F32),
-            jax.ShapeDtypeStruct((1, 2 * rows), F32),
+            jax.ShapeDtypeStruct((rows, width), F32),
+            jax.ShapeDtypeStruct((1, rows), F32),
             jax.ShapeDtypeStruct((width, cols), BF16),
-            jax.ShapeDtypeStruct((2 * rows, width), BF16),
+            jax.ShapeDtypeStruct((rows, width), BF16),
         ],
         scratch_shapes=[
-            pltpu.VMEM((rows, width), F32),
-            pltpu.VMEM((rows, width), F32),
             pltpu.VMEM((width, cols), BF16),
-            pltpu.VMEM((width, cols), BF16),
-            pltpu.VMEM((2 * rows, width), BF16),
-            pltpu.VMEM((2 * rows, LANES), F32),
-            pltpu.SemaphoreType.DMA((2 + cols // BLOCK,)),
-            pltpu.SemaphoreType.DMA((1 + cols // BLOCK,)),
+            pltpu.SemaphoreType.DMA((cols // BLOCK,)),
         ],
-        compiler_params=PARAMS,
+        compiler_params=TIGHT,
         cost_estimate=pl.CostEstimate(
-            flops=8 * rows * cols * width,
+            flops=4 * rows * cols * width,
             bytes_accessed=4 * width * cols + 8 * rows * width,
-            transcendentals=2 * rows * cols,
+            transcendentals=rows * cols,
         ),
         name="student_totals",
-    )(place, own, other, protos)
+    )(place, one, two, sums, protos)
 
 
 def row_slices(expo):
     return [slice(first, first + LANES) for first in range(0, expo.shape[0], LANES)]
-
-
-class Stream:
-    def __init__(self, expo, scratch):
-        self.rows = row_slices(expo)
-        self.values, self.copies = expo, []
-        if scratch:
-            self.values, sems = scratch
-            for i, here in enumerate(self.rows):
-                copy = pltpu.make_async_copy(expo.at[here, :], self.values.at[here, :], sems.at[i])
-                copy.start()
-                self.copies.append(copy)
-
-    def __iter__(self):
-        for i, here in enumerate(self.rows):
-            if self.copies:
-                self.copies[i].wait()
-            yield here
-
-
-def stream_scratch(expo, held):
-    if held:
-        return []
-    return [pltpu.VMEM(expo.shape, BF16), pltpu.SemaphoreType.DMA((expo.shape[0] // LANES,))]
 
 
 def scaled_row_sums(values, here, scale):
@@ -259,68 +232,58 @@
     return row_to_lanes(total)
 
 
-def row_sweep_kernel(proto_total, extra, col_parts, expo, *rest):
-    row_part, scale = rest[extra], rest[extra + 1]
-    stream = Stream(expo, rest[extra + 2 :])
+def row_sweep_kernel(proto_total, extra, expo, *rest):
+    parts, (row_part, scale) = rest[extra:-2], rest[-2:]
     copies = row_part.shape[0]
-    sums = jnp.sum(col_parts[...], axis=0)
+    sums = 0.0
+    for part in parts:
+        sums = sums + (jnp.sum(part[...], axis=0) if len(part.shape) == 3 else part[...])
     scale[...] = jnp.broadcast_to(1.0 / (proto_total * sums), scale.shape)
     if extra:
         row_part[:, 1:2, :] = tall(rest[0][...], copies)
-    for here in stream:
-        row_part[:, 0:1, here] = tall(scaled_row_sums(stream.values, here, scale), copies)
-
-
-def row_sweep(proto_total, col_parts, expo, copies, held, extra=()):
+    for here in row_slices(expo):
+        row_part[:, 0:1, here] = tall(scaled_row_sums(expo, here, scale), copies)
+
+
+def row_sweep(proto_total, parts, expo, copies, extra=()):
     rows, cols = expo.shape
     kinds = 1 + len(extra)
     return pl.pallas_call(
         lambda *refs: row_sweep_kernel(proto_total, len(extra), *refs),
-        in_specs=[VMEM, VMEM if held else HBM] + [VMEM] * len(extra),
+        in_specs=[VMEM] * (1 + len(extra) + len(parts)),
         out_specs=VMEM,
         out_shape=jax.ShapeDtypeStruct((copies, kinds, rows), F32),
-        scratch_shapes=[pltpu.VMEM((8, cols), F32)] + stream_scratch(expo, held),
-        compiler_params=HELD if held else PARAMS,
+        scratch_shapes=[pltpu.VMEM((8, cols), F32)],
+        compiler_params=HELD,
         cost_estimate=pl.CostEstimate(
             flops=2 * rows * cols, bytes_accessed=2 * rows * cols, transcendentals=0
         ),
         name="row_sweep",
-    )(col_parts, expo, *extra)
-
-
-def col_sweep_kernel(batch_total, row_parts, expo, col_part, scale, *scratch):
-    stream = Stream(expo, scratch)
+    )(expo, *extra, *parts)
+
+
+def col_sweep_kernel(batch_total, row_parts, expo, col_part, scale):
     copies = col_part.shape[0]
     cols = expo.shape[1]
     sums = jnp.sum(row_parts[...], axis=0)
     scale[...] = lanes_to_rows(1.0 / (batch_total * sums[0:1]))
     if sums.shape[0] > 1:
         col_part[:, :, cols:] = tall(sums[1:2], copies)
-    if stream.copies:
-        total = [jnp.zeros((8, LANES), F32)] * (cols // LANES)
-        for here in stream:
-            for j in range(cols // LANES):
-                block = stream.values[here, j * LANES : (j + 1) * LANES].astype(F32) * scale[here, :]
-                total[j] = total[j] + jnp.sum(block.reshape(LANES // 8, 8, LANES), axis=0)
-        for j, part in enumerate(total):
-            part = jnp.sum(part, axis=0, keepdims=True)
-            col_part[:, :, j * LANES : (j + 1) * LANES] = tall(part, copies)
-    else:
-        for at in range(0, cols, LANES):
-            block = expo[:, at : at + LANES].astype(F32) * scale[...]
-            col_part[:, :, at : at + LANES] = tall(jnp.sum(block, axis=0, keepdims=True), copies)
-
-
-def col_sweep(batch_total, row_parts, expo, copies, held):
+    for at in range(0, cols, LANES):
+        block = expo[:, at : at + LANES].astype(F32) * scale[...]
+        col_part[:, :, at : at + LANES] = tall(jnp.sum(block, axis=0, keepdims=True), copies)
+
+
+def col_sweep(batch_total, row_parts, expo, copies):
     rows, cols = expo.shape
-    extra = row_parts.shape[1] - 1
+    extra = rows * (row_parts.shape[1] - 1)
     return pl.pallas_call(
         lambda *refs: col_sweep_kernel(batch_total, *refs),
-        in_specs=[VMEM, VMEM if held else HBM],
+        in_specs=[VMEM] * 2,
         out_specs=VMEM,
-        out_shape=jax.ShapeDtypeStruct((copies, 1, cols + extra * rows), F32),
-        scratch_shapes=[pltpu.VMEM((rows, LANES), F32)] + stream_scratch(expo, held),
-        compiler_params=HELD if held else PARAMS,
+        out_shape=jax.ShapeDtypeStruct((copies, 1, cols + extra), F32),
+        scratch_shapes=[pltpu.VMEM((rows, LANES), F32)],
+        compiler_params=HELD,
         cost_estimate=pl.CostEstimate(
             flops=2 * rows * cols, bytes_accessed=2 * rows * cols, transcendentals=0
         ),
@@ -329,16 +292,19 @@
 
 
 def last_sweep_kernel(
-    proto_total, place, col_parts, expo, dirs, unit, student, row_part, own, other, scale, scaled
+    proto_total, place, col_parts, expo, dirs, far_dirs, unit, student, row_part, own, other,
+    scale_out, scale, scaled,
 ):
     rows, cols = expo.shape
     width = dirs.shape[0]
     copies = row_part.shape[0]
-    half = rows // 2
+    half, quarter = rows // 2, rows // 4
     wide = 1.0 / (proto_total * jnp.sum(col_parts[:, :, :cols], axis=0))
+    scale_out[...] = wide
     scale[...] = jnp.broadcast_to(wide, scale.shape)
-    scaled[...] = (dirs[...].astype(F32) * wide).astype(BF16)
-    second = place[0] == 1
+    part = dirs.shape[1]
+    scaled[:, :part] = (dirs[...].astype(F32) * wide[:, :part]).astype(BF16)
+    scaled[:, part:] = (far_dirs[...].astype(F32) * wide[:, part:]).astype(BF16)
     products = []
     for first in range(0, rows, half):
         here = slice(first, first + half)
@@ -348,27 +314,33 @@
         row_part[:, 1:2, here] = tall(row_to_lanes(meet), copies)
     for here in row_slices(expo):
         row_part[:, 0:1, here] = tall(scaled_row_sums(expo, here, scale), copies)
-    own[:, :width] = jnp.where(second, student[half:, :], student[:half, :])
-    other[:, :width] = jnp.where(second, student[:half, :], student[half:, :])
-    own[:, width:] = jnp.where(second, products[1], products[0])
-    other[:, width:] = jnp.where(second, products[0], products[1])
-
-
-def last_sweep(proto_total, place, col_parts, expo, dirs, unit, student, copies):
+    core, far = place[0] == 1, place[7] == 1
+
+    def choose(where, one, two):
+        return jnp.where(where, two, one), jnp.where(where, one, two)
+
+    for at, kind in ((0, [student[:half, :], student[half:, :]]), (width, products)):
+        for out, values in zip((own, other), choose(core, *kind)):
+            stay, go = choose(far, values[:quarter], values[quarter:])
+            out[0, :, at : at + width] = stay
+            out[1, :, at : at + width] = go
+
+
+def last_sweep(proto_total, place, col_parts, expo, dirs, far_dirs, unit, student, copies):
     rows, cols = expo.shape
     width = dirs.shape[0]
-    half = (rows // 2, 2 * width)
+    half = (2, rows // 4, 2 * width)
     return pl.pallas_call(
         lambda *refs: last_sweep_kernel(proto_total, *refs),
-        in_specs=[SMEM] + [VMEM] * 5,
+        in_specs=[SMEM] + [VMEM] * 6,
         out_specs=[VMEM] * 4,
         out_shape=[
             jax.ShapeDtypeStruct((copies, 2, rows), F32),
             jax.ShapeDtypeStruct(half, F32),
             jax.ShapeDtypeStruct(half, F32),
-            jax.ShapeDtypeStruct((8, cols), F32),
+            jax.ShapeDtypeStruct((1, cols), F32),
         ],
-        scratch_shapes=[pltpu.VMEM((width, cols), BF16)],
+        scratch_shapes=[pltpu.VMEM((8, cols), F32), pltpu.VMEM((width, cols), BF16)],
         compiler_params=HELD,
         cost_estimate=pl.CostEstimate(
             flops=2 * rows * cols * (width + 1),
@@ -376,11 +348,11 @@
             transcendentals=0,
         ),
         name="last_sweep",
-    )(place, col_parts, expo, dirs, unit, student)
+    )(place, col_parts, expo, dirs, far_dirs, unit, student)
 
 
 def wide_kernel(
-    place, both, totals, t_protos, s_protos, after, expo, turned, dirs, inverse, mixed, t_dirs
+    place, both, totals, t_protos, s_protos, expo, turned, dirs, inverse, mixed, t_dirs
 ):
     @pl.when(pl.program_id(0) == 0)
     def _():
@@ -403,7 +375,7 @@
         mixed[:, here] += dot(across, chance)
 
 
-def wide_call(place, gathered, col_parts, t_protos, s_protos, after, shares, blocks):
+def wide_call(place, gathered, col_parts, t_protos, s_protos, shares, blocks):
     crops, double = gathered.shape
     width = double // 2
     rows = crops // blocks
@@ -419,7 +391,6 @@
                 pl.BlockSpec((1, 1, rows), lambda i, place: (2 * i + place[4], 0, last)),
                 pl.BlockSpec((width, cols), lambda i, place: (0, place[2])),
                 pl.BlockSpec((width, cols), lambda i, place: (0, place[2])),
-                whole(TOKEN),
             ],
             out_specs=[
                 pl.BlockSpec((rows, cols), lambda i, place: (i, 0)),
@@ -444,7 +415,7 @@
             transcendentals=2 * crops * cols,
         ),
         name="wide_products",
-    )(place, gathered, col_parts, t_protos, s_protos, after)
+    )(place, gathered, col_parts, t_protos, s_protos)
 
 
 def finish_kernel(
@@ -492,7 +463,7 @@
             done += 1
     for copy in late:
         copy.wait()
-    factor = jnp.where(place[6] == 1, scale[0:1], far_scale[0:1])
+    factor = jnp.where(place[6] == 1, scale[...], far_scale[...])
     values = mixed_v[...] - factor * total[...]
     wide = dirs_v[...].astype(F32)
     dots = jnp.sum(values * wide, axis=0, keepdims=True)
@@ -520,8 +491,8 @@
                 pl.BlockSpec((chips, 1, rows), lambda i, place: (0, 0, last)),
                 HBM,
                 HBM,
-                pl.BlockSpec((8, cols), lambda i, place: (0, place[3])),
-                pl.BlockSpec((8, cols), lambda i, place: (0, place[3])),
+                pl.BlockSpec((1, cols), lambda i, place: (0, place[3])),
+                pl.BlockSpec((1, cols), lambda i, place: (0, place[3])),
                 HBM,
                 whole((1, cols)),
                 HBM,
@@ -570,10 +541,10 @@
     return lax.dynamic_index_in_dim(values, index, 0, keepdims=False)
 
 
-def sum_scatter(values):
-    near, along = lax.axis_index("zh"), lax.axis_index("y")
-    count = values.shape[1]
-    half = pick(values, near) + swap(pick(values, 1 - near), "zh")
+def sum_scatter(stay, go):
+    along = lax.axis_index("y")
+    half = stay + swap(go, "zh")
+    count = half.shape[0]
     total = pick(half, along)
     for step in range(1, count):
         ring = [(i, (i + step) % count) for i in range(count)]
@@ -602,26 +573,39 @@
     half = teacher_protos.shape[1] // 2
     half_protos = lax.dynamic_slice_in_dim(teacher_protos, core * half, half, 1)
 
-    expo, col_part = teacher_call(place, teacher_unit, teacher_other, half_protos, chips)
-    student_mixed, total_part, dirs, unit = student_call(
-        place, student_unit, student_other, student_protos
+    expo, col_part = teacher_call(place, teacher_unit, teacher_other, half_protos)
+
+    near_part = swap(col_part, "zl")
+    no_sums = jnp.zeros((1, 2 * crops), F32)
+    mixed, sums, dirs, unit = student_call(
+        0, place, student_unit, student_other, no_sums, student_protos
     )
-
+    near_part, mixed = lax.optimization_barrier((near_part, mixed))
+    col_part = add_call(col_part, near_part)
+    col_parts = [
+        lax.ppermute(col_part, "x", [(i, (i + step) % blocks) for i in range(blocks)])
+        for step in range(1, blocks)
+    ]
+    student_mixed, total_part, far_dirs, unit = student_call(
+        1, place, unit, mixed, sums, student_protos
+    )
+    col_parts, total_part = lax.optimization_barrier((col_parts, total_part))
+    row_part = row_sweep(proto_total, [col_part] + col_parts, expo, row_copies)
+    row_parts = exchange(row_part, ROW_AXES)
+    col_part = col_sweep(batch_total, row_parts, expo, chips)
     col_parts = exchange(col_part, COL_AXES)
-    row_part = row_sweep(proto_total, col_parts, expo, row_copies, True)
+    row_part = row_sweep(proto_total, [col_parts], expo, row_copies, (total_part,))
     row_parts = exchange(row_part, ROW_AXES)
-    col_part = col_sweep(batch_total, row_parts, expo, chips, True)
-    col_parts = exchange(col_part, COL_AXES)
-    row_part = row_sweep(proto_total, col_parts, expo, row_copies, True, (total_part,))
-    row_parts = exchange(row_part, ROW_AXES)
-    col_part = col_sweep(batch_total, row_parts, expo, chips, True)
+    col_part = col_sweep(batch_total, row_parts, expo, chips)
     col_parts = exchange(col_part, COL_AXES)
     row_part, own_part, other_part, scale = last_sweep(
-        proto_total, place, col_parts, expo, dirs, unit, student_mixed, blocks * row_copies
+        proto_total, place, col_parts, expo, dirs, far_dirs, unit, student_mixed,
+        blocks * row_copies,
     )
     row_parts = exchange(row_part, LAST_AXES)
+    gathered, scale = lax.optimization_barrier((gathered, scale))
     wide_expo, turned, wide_dirs, inverse, wide_mixed = wide_call(
-        place, gathered, col_parts, teacher_protos, student_protos, scale, shares, blocks
+        place, gathered, col_parts, teacher_protos, student_protos, shares, blocks
     )
     far_scale = swap(scale, "c")
 
@@ -638,11 +622,9 @@
 
     rows = crops // groups
     far_part, wide_mixed = lax.optimization_barrier((swap(other_part, "c"), wide_mixed))
-    summed = sum_scatter(
-        (own_part + far_part).reshape(
-            lax.axis_size("zh"), lax.axis_size("y"), rows, 2 * width
-        )
-    )
+    pieces = (2, lax.axis_size("y"), rows, 2 * width)
+    own_part, far_part = own_part.reshape(pieces), far_part.reshape(pieces)
+    summed = sum_scatter(own_part[0] + far_part[0], own_part[1] + far_part[1])
     first = core * crops + group * rows
     sources = lax.dynamic_slice(
         row_parts, (lax.axis_index("x") * row_copies, 0, first), (row_copies, 1, rows)

time: 165 us -> 158 us (0.958)
  local copies, waits for them, and re-layouts: 13.4 us -> 6.9 us
  blocking collectives: 49 us -> 45.5 us
  starting transfers between devices: 26.2 us -> 28.5 us
    unnamed x40 -> x16, local copies, waits for them, and re-layouts: 8.41 us -> 2.68 us
    ppermute x0 -> x3, starting transfers between devices: none -> 4.87 us  [on_device(): lax.ppermute(col_part, 'x', [(i, (i + step) % blocks) for i in range(bloc...]
    all_to_all x3 -> x2, starting transfers between devices: 13.2 us -> 9.4 us  [exchange(): return lax.all_to_all(values, axes, 0, 0, tiled=True)]
    all_to_all x4, blocking collectives: 49 us -> 45.5 us  [exchange(): return lax.all_to_all(values, axes, 0, 0, tiled=True)]
    ppermute x6 -> x7, starting transfers between devices: 8.14 us -> 9.97 us  [swap(): return lax.ppermute(values, axis, SWAP)]
    ppermute x3, waiting for transfers between devices: 1.76 us -> 3.45 us  [sum_scatter(): total = total + lax.ppermute(pick(half, (along + step) % count), 'y', ring)]
    pallas_call x1 -> x3, Pallas kernels: 9.5 us -> 9.86 us  [the longest x2 9.85 us: student_call(): pl.pallas_call(lambda *refs: student_kernel(part, *refs), in_specs=[SMEM,...]
  transfers between devices with their start and end apart: 13 -> 16, of which waited for: 4 -> 3; matrix products, arithmetic and copies ran while one was open for 6% -> 6% of each run, Pallas kernels for 29% -> 30%
where the time goes in v4:
time: 158 us; the launch traced here: 157 us
  Pallas kernels  48.4 us (31%)
  blocking collectives  45.5 us (29%)
  starting transfers between devices  28.5 us (18%)
  between operations  15.5 us (10%)
  local copies, waits for them, and re-layouts  6.9 us (4%)
  other arithmetic  6.55 us (4%)
  waiting for transfers between devices  5.86 us (4%)
    all_to_all x4, blocking collectives, exchange(): return lax.all_to_all(values, axes, 0, 0, tiled=True)  45.5 us
    pallas_call x1, Pallas kernels, wide_call(): pl.pallas_call(wide_kernel, grid_spec=pltpu.PrefetchScalarGridSpec(num_sc...  12 us
    ppermute x7, starting transfers between devices, swap(): return lax.ppermute(values, axis, SWAP)  9.97 us
    pallas_call x2, Pallas kernels, student_call(): pl.pallas_call(lambda *refs: student_kernel(part, *refs), in_specs=[SMEM,...  9.85 us
    all_to_all x2, starting transfers between devices, exchange(): return lax.all_to_all(values, axes, 0, 0, tiled=True)  9.4 us
    pallas_call x1, Pallas kernels, finish_call(): pl.pallas_call(finish_kernel, grid_spec=pltpu.PrefetchScalarGridSpec(num_...  7.95 us
    pallas_call x1, Pallas kernels, last_sweep(): pl.pallas_call(lambda *refs: last_sweep_kernel(proto_total, *refs), in_sp...  5.96 us
    ppermute x3, starting transfers between devices, on_device(): lax.ppermute(col_part, 'x', [(i, (i + step) % blocks) for i in range(bloc...  4.87 us
  transfers between devices with their start and end apart: 16, of which 3 were waited for; matrix products, arithmetic and copies ran while one was open for 6% of the time, Pallas kernels for 30%

profile of v4, /device:TPU:1, one launch (start us, length us, event | category | flops | bytes accessed | tf_op | source)
XLA Modules:
  0.0 157.2 jit_solution(6488282448437053609)
XLA Ops:
  9.1 1.4 unit_rows.1
  10.5 1.5 collective-permute-start
  12.1 1.8 %constant_dynamic-slice_fusion.1.protos = bf16[256,4096]{1,0:T(8,128)(2,1)S(1)} fusion(bf16[256,8192]{1,0:T(8,128)(2,1)} %t_protos.1, s32[]{:T(128)S(6)} %select_n.46), kind=kLoop, calls=%fused_computation.24 | loop fusion | bytes 4194308 | tf_op jit(solution)/shard_map/dynamic_slice | solution.py:574
  13.9 3.7 %teacher_expo.1 = (bf16[1024,4096]{1,0:T(8,128)(2,1)S(1)}, f32[1,4096]{1,0:T(1,128)S(1)}) custom-call(s32[8]{0:T(128)S(1)} %get-tuple-element.37.place.refs_0_, f32[512,256]{1,0:T(8,128)S(1)} %get-tuple-element.38.own, f32[512,256]{1,0:T(8,128)S(1)} %collective-permute-done.other, bf16[256,4096]{1,0:T(8,128)(2,1)S(1)} %constant_dynamic-slice_fusion.1.protos), custom_call_target="tpu_custom_call" | custom-call | flops 2147483648 | bytes 10485760 | tf_op jit(solution)/shard_map/teacher_expo/pallas_call | solution.py:133
  17.6 1.8 %collective-permute-start.1 = (f32[1,4096]{1,0:T(1,128)S(1)}, f32[1,4096]{1,0:T(1,128)S(1)}, u32[]{:S(2)}, u32[]{:S(2)}) collective-permute-start(f32[1,4096]{1,0:T(1,128)S(1)} %get-tuple-element.40.one), channel_id=1, source_target_pairs={{0,16},{16,0},{1,17},{17,1},{2,18},{18,2},{3,19},{19,3},{4,20},{20... | collective-permute-start | bytes 49160 | tf_op jit(solution)/shard_map/ppermute | solution.py:537
  19.4 5.0 %student_totals.2 = (f32[1024,256]{1,0:T(8,128)S(1)}, f32[1,1024]{1,0:T(1,128)S(1)}, bf16[256,2048]{1,0:T(8,128)(2,1)S(1)}, bf16[1024,256]{1,0:T(8,128)(2,1)S(1)}) custom-call(s32[8]{0:T(128)S(1)} %get-tuple-element.37.place.refs_0_, f32[512,256]{1,0:T(8,128)S(1)} %get-tuple-element.41.refs_1_, f32[512,256]{1,0:T(8,128)S(1)} %collective-permute-done.2.refs_2_, ...), custom_call_target="tpu_custom_call" | custom-call | flops 2147483648 | bytes 4194304 | tf_op jit(solution)/shard_map/student_totals/pallas_call | solution.py:199
  24.4 1.3 collective-permute-start.3
  25.7 2.4 %collective-permute-start.4 = (f32[1,4096]{1,0:T(1,128)S(1)}, f32[1,4096]{1,0:T(1,128)S(1)}, u32[]{:S(2)}, u32[]{:S(2)}) collective-permute-start(f32[1,4096]{1,0:T(1,128)S(1)} %add_parts.1.refs_1_), channel_id=1, source_target_pairs={{0,64},{32,96},{64,0},{96,32},{1,65},{33,97},{65,1},{97,33},{2,66}... | collective-permute-start | bytes 49160 | tf_op jit(solution)/shard_map/ppermute | solution.py:586
  29.3 4.9 %student_totals.3 = (f32[1024,256]{1,0:T(8,128)S(1)}, f32[1,1024]{1,0:T(1,128)S(1)}, bf16[256,2048]{1,0:T(8,128)(2,1)S(1)}, bf16[1024,256]{1,0:T(8,128)(2,1)S(1)}) custom-call(s32[8]{0:T(128)S(1)} %get-tuple-element.37.place.refs_0_, bf16[1024,256]{1,0:T(8,128)(2,1)S(1)} %get-tuple-element.44.refs_1_, f32[1024,256]{1,0:T(8,128)S(1)} %get-tuple-element.45.refs_2_, ...), custom_call_target="tpu_custom_call" | custom-call | flops 2147483648 | bytes 4194304 | tf_op jit(solution)/shard_map/student_totals/pallas_call | solution.py:199
  34.2 1.7 %row_sweep.2 = f32[16,1,1024]{2,1,0:T(1,128)S(1)} custom-call(bf16[1024,4096]{1,0:T(8,128)(2,1)S(1)} %get-tuple-element.39.refs_0_.refs_1_.refs_2_, f32[1,4096]{1,0:T(1,128)S(1)} %add_parts.1.refs_1_, f32[1,4096]{1,0:T(1,128)S(1)} %collective-permute-done.3.refs_2_, f32[1,4096]{1,0:T(1,128)S(1)} %collective-permute-done.4.refs_3_, ...), custom_call_target="tpu_custom_call" | custom-call | flops 8388608 | bytes 8388608 | tf_op jit(solution)/shard_map/row_sweep/pallas_call | solution.py:251
  35.9 16.2 %all_to_all.30.refs_0_ = f32[16,1,1024]{2,1,0:T(1,128)S(1)} all-to-all(f32[16,1,1024]{2,1,0:T(1,128)S(1)} %row_sweep.2), channel_id=1, replica_groups=mesh['x'=4,'zl'=2,'c'=2,'zh'=2,'y'=4] {'c','zh','y'}, dimensions={0} | all-to-all | bytes 131072 | tf_op jit(solution)/shard_map/all_to_all | solution.py:533
  52.1 2.0 %col_sweep.2 = f32[8,1,4096]{2,1,0:T(1,128)S(1)} custom-call(f32[16,1,1024]{2,1,0:T(1,128)S(1)} %all_to_all.30.refs_0_, bf16[1024,4096]{1,0:T(8,128)(2,1)S(1)} %get-tuple-element.39.refs_0_.refs_1_.refs_2_), custom_call_target="tpu_custom_call" | custom-call | flops 8388608 | bytes 8388608 | tf_op jit(solution)/shard_map/col_sweep/pallas_call | solution.py:280
  54.2 9.3 %all_to_all.31.refs_2_ = f32[8,1,4096]{2,1,0:T(1,128)S(1)} all-to-all(f32[8,1,4096]{2,1,0:T(1,128)S(1)} %col_sweep.2), channel_id=1, replica_groups=mesh['x'=4,'zl'=2,'c'=2,'zh'=2,'y'=4] {'x','zl'}, dimensions={0} | all-to-all | bytes 262144 | tf_op jit(solution)/shard_map/all_to_all | solution.py:533
  63.5 1.8 %row_sweep.3 = f32[16,2,1024]{2,1,0:T(2,128)S(1)} custom-call(bf16[1024,4096]{1,0:T(8,128)(2,1)S(1)} %get-tuple-element.39.refs_0_.refs_1_.refs_2_, f32[1,1024]{1,0:T(1,128)S(1)} %get-tuple-element.48.refs_1_, f32[8,1,4096]{2,1,0:T(1,128)S(1)} %all_to_all.31.refs_2_), custom_call_target="tpu_custom_call" | custom-call | flops 8388608 | bytes 8388608 | tf_op jit(solution)/shard_map/row_sweep/pallas_call | solution.py:251
  65.3 11.6 %all_to_all.32.refs_0_ = f32[16,2,1024]{2,1,0:T(2,128)S(1)} all-to-all(f32[16,2,1024]{2,1,0:T(2,128)S(1)} %row_sweep.3), channel_id=1, replica_groups=mesh['x'=4,'zl'=2,'c'=2,'zh'=2,'y'=4] {'c','zh','y'}, dimensions={0} | all-to-all | bytes 262144 | tf_op jit(solution)/shard_map/all_to_all | solution.py:533
  76.8 2.1 %col_sweep.3 = f32[8,1,5120]{2,1,0:T(1,128)S(1)} custom-call(f32[16,2,1024]{2,1,0:T(2,128)S(1)} %all_to_all.32.refs_0_, bf16[1024,4096]{1,0:T(8,128)(2,1)S(1)} %get-tuple-element.39.refs_0_.refs_1_.refs_2_), custom_call_target="tpu_custom_call" | custom-call | flops 8388608 | bytes 8388608 | tf_op jit(solution)/shard_map/col_sweep/pallas_call | solution.py:280
  78.9 8.4 %all_to_all.33.refs_1_.totals = f32[8,1,5120]{2,1,0:T(1,128)S(1)} all-to-all(f32[8,1,5120]{2,1,0:T(1,128)S(1)} %col_sweep.3), channel_id=1, replica_groups=mesh['x'=4,'zl'=2,'c'=2,'zh'=2,'y'=4] {'x','zl'}, dimensions={0} | all-to-all | bytes 327680 | tf_op jit(solution)/shard_map/all_to_all | solution.py:533
  87.3 6.0 %last_sweep.1 = (f32[64,2,1024]{2,1,0:T(2,128)}, f32[2,256,512]{2,1,0:T(8,128)S(1)}, f32[2,256,512]{2,1,0:T(8,128)}, f32[1,4096]{1,0:T(1,128)S(1)}) custom-call(s32[8]{0:T(128)S(1)} %get-tuple-element.37.place.refs_0_, f32[8,1,5120]{2,1,0:T(1,128)S(1)} %all_to_all.33.refs_1_.totals, bf16[1024,4096]{1,0:T(8,128)(2,1)S(1)} %get-tuple-element.39.refs_0_.refs_1_.refs_2_, ...), custom_call_target="tpu_custom_call" | custom-call | flops 2155872256 | bytes 10485760 | tf_op jit(solution)/shard_map/last_sweep/pallas_call | solution.py:333
  93.3 1.6 %collective-permute-start.6 = (f32[2,256,512]{2,1,0:T(8,128)}, f32[2,256,512]{2,1,0:T(8,128)}, u32[]{:S(2)}, u32[]{:S(2)}) collective-permute-start(f32[2,256,512]{2,1,0:T(8,128)} %get-tuple-element.57), channel_id=1, source_target_pairs={{0,8},{8,0},{1,9},{9,1},{2,10},{10,2},{3,11},{11,3},{4,12},{12,4},... | collective-permute-start | bytes 3145736 | tf_op jit(solution)/shard_map/ppermute | solution.py:537
  94.9 4.9 %all-to-all-start.4 = ((f32[64,2,1024]{2,1,0:T(2,128)}), f32[64,2,1024]{2,1,0:T(2,128)S(1)}, u32[]{:S(2)}, u32[]{:S(2)}) async-start(f32[64,2,1024]{2,1,0:T(2,128)} %get-tuple-element.63), calls=%async_computation.4 | async-start | bytes 1048576 | tf_op jit(solution)/shard_map/all_to_all | solution.py:533
  99.8 12.0 %wide_products.1 = (bf16[4096,1024]{1,0:T(8,128)(2,1)}, bf16[256,4096]{1,0:T(8,128)(2,1)}, bf16[256,1024]{1,0:T(8,128)(2,1)}, f32[1,1024]{1,0:T(1,128)}, f32[256,1024]{1,0:T(8,128)}) custom-call(s32[8]{0:T(128)} %copy-done.4, f32[4096,512]{1,0:T(8,128)} %all-gather.2.cloned.1.call-done.both, f32[8,1,5120]{2,1,0:T(1,128)} %copy-done, ...), custom_call_target="tpu_custom_call" | custom-call | flops 6442450944 | bytes 16777216 | tf_op jit(solution)/shard_map/wide_products/pallas_call | solution.py:384
  111.9 2.2 %slice_add_fusion.1 = (f32[1,256,512]{2,1,0:T(8,128)}, f32[1,256,512]{2,1,0:T(8,128)S(1)}) fusion(f32[2,256,512]{2,1,0:T(8,128)} %collective-permute-done.6, f32[2,256,512]{2,1,0:T(8,128)S(1)} %get-tuple-element.56), kind=kLoop, calls=%fused_computation.2 | loop fusion | flops 262144 | bytes 3145728 | tf_op jit(solution)/shard_map/add | solution.py:627
  114.1 2.9 %collective-permute-start.7 = (f32[4,64,512]{2,1,0:T(8,128)}, f32[4,64,512]{2,1,0:T(8,128)S(1)}, u32[]{:S(2)}, u32[]{:S(2)}) collective-permute-start(f32[4,64,512]{2,1,0:T(8,128)} %bitcast.1), channel_id=1, source_target_pairs={{0,4},{4,0},{1,5},{5,1},{2,6},{6,2},{3,7},{7,3},{8,12},{12,8},{9,1... | collective-permute-start | bytes 1572872 | tf_op jit(solution)/shard_map/ppermute | solution.py:537
  119.3 8.0 %finish_protos.1 = (f32[16,16,1024]{2,1,0:T(8,128)}, f32[1,128]{1,0:T(1,128)}) custom-call(s32[8]{0:T(128)} %copy-done.4, f32[64,2,1024]{2,1,0:T(2,128)} %copy-done.5, f32[8,1,5120]{2,1,0:T(1,128)} %copy-done, bf16[256,4096]{1,0:T(8,128)(2,1)} %get-tuple-element.64.turned, bf16[4096,1024]{1,0:T(8,128)(2,1)} %get-tuple-element.65.expo, f32[1,4096]{1,0:T(1,128)} %copy-done.3, ...), custom_call_target="tpu_custom_call" | custom-call | flops 2147483648 | bytes 10485760 | tf_op jit(solution)/shard_map/finish_protos/pallas_call | solution.py:484
  127.3 4.5 %all-to-all-start.5 = ((f32[16,16,1024]{2,1,0:T(8,128)}), f32[16,16,1024]{2,1,0:T(8,128)S(1)}, u32[]{:S(2)}, u32[]{:S(2)}) async-start(f32[16,16,1024]{2,1,0:T(8,128)} %get-tuple-element.69), calls=%async_computation.5 | async-start | bytes 2097152 | tf_op jit(solution)/shard_map/all_to_all | solution.py:533
  131.9 2.5 %collective-permute-start.10 = (f32[64,512]{1,0:T(8,128)S(1)}, f32[64,512]{1,0:T(8,128)S(1)}, u32[]{:S(2)}, u32[]{:S(2)}) collective-permute-start(f32[64,512]{1,0:T(8,128)S(1)} %get-tuple-element.76), channel_id=1, source_target_pairs={{0,3},{1,0},{2,1},{3,2},{4,7},{5,4},{6,5},{7,6},{8,11},{9,8},{10,9... | collective-permute-start | bytes 393224 | tf_op jit(solution)/shard_map/ppermute | solution.py:551
  134.4 1.8 %collective-permute-start.9 = (f32[64,512]{1,0:T(8,128)S(1)}, f32[64,512]{1,0:T(8,128)S(1)}, u32[]{:S(2)}, u32[]{:S(2)}) collective-permute-start(f32[64,512]{1,0:T(8,128)S(1)} %get-tuple-element.77), channel_id=1, source_target_pairs={{0,2},{1,3},{2,0},{3,1},{4,6},{5,7},{6,4},{7,5},{8,10},{9,11},{10,... | collective-permute-start | bytes 393224 | tf_op jit(solution)/shard_map/ppermute | solution.py:551
  136.9 1.4 collective-permute-start.12
  139.7 3.4 %collective-permute-done.8 = f32[64,512]{1,0:T(8,128)S(1)} collective-permute-done((f32[64,512]{1,0:T(8,128)S(1)}, f32[64,512]{1,0:T(8,128)S(1)}, u32[]{:S(2)}, u32[]{:S(2)}) %collective-permute-start.8) | collective-permute-done | bytes 131104 | tf_op jit(solution)/shard_map/ppermute | solution.py:551
  144.2 1.5 fusion.7
  145.7 1.8 %all-to-all-done.5 = f32[16,16,1024]{2,1,0:T(8,128)S(1)} async-done(((f32[16,16,1024]{2,1,0:T(8,128)}), f32[16,16,1024]{2,1,0:T(8,128)S(1)}, u32[]{:S(2)}, u32[]{:S(2)}) %all-to-all-start.5) | async-done | bytes 1048608 | tf_op jit(solution)/shard_map/all_to_all | solution.py:533
  148.0 1.2 reshape.41
  (49 shorter events, 9.2 us)
Async XLA Ops:
  7.2 92.7 %all-gather.2.cloned.1.call-start = ((), (), s32[]{:S(2)}) async-start(), calls=%async_computation.6 | async-start | bytes 9437184 | tf_op jit(solution)/shard_map/all_gather | solution.py:571
  7.2 1.0 copy-start.1
  8.2 0.9 copy-start.2
  10.5 76.8 %copy-start.4 = (s32[8]{0:T(128)}, s32[8]{0:T(128)S(1)}, u32[]{:S(2)}) copy-start(s32[8]{0:T(128)S(1)} %get-tuple-element.37.place.refs_0_) | copy-start | bytes 100
  10.5 3.4 %collective-permute-start = (f32[512,256]{1,0:T(8,128)S(1)}, f32[512,256]{1,0:T(8,128)S(1)}, u32[]{:S(2)}, u32[]{:S(2)}) collective-permute-start(f32[512,256]{1,0:T(8,128)S(1)} %get-tuple-element.38.own), channel_id=1, source_target_pairs={{0,8},{8,0},{1,9},{9,1},{2,10},{10,2},{3,11},{11,3},{4,12},{12,4},... | collective-permute-start | bytes 1572872 | tf_op jit(solution)/shard_map/ppermute | solution.py:537
  12.0 7.4 %collective-permute-start.2 = (f32[512,256]{1,0:T(8,128)S(1)}, f32[512,256]{1,0:T(8,128)S(1)}, u32[]{:S(2)}, u32[]{:S(2)}) collective-permute-start(f32[512,256]{1,0:T(8,128)S(1)} %get-tuple-element.41.refs_1_), channel_id=1, source_target_pairs={{0,8},{8,0},{1,9},{9,1},{2,10},{10,2},{3,11},{11,3},{4,12},{12,4},... | collective-permute-start | bytes 1572872 | tf_op jit(solution)/shard_map/ppermute | solution.py:537
  17.6 6.8 %collective-permute-start.1 = (f32[1,4096]{1,0:T(1,128)S(1)}, f32[1,4096]{1,0:T(1,128)S(1)}, u32[]{:S(2)}, u32[]{:S(2)}) collective-permute-start(f32[1,4096]{1,0:T(1,128)S(1)} %get-tuple-element.40.one), channel_id=1, source_target_pairs={{0,16},{16,0},{1,17},{17,1},{2,18},{18,2},{3,19},{19,3},{4,20},{20... | collective-permute-start | bytes 49160 | tf_op jit(solution)/shard_map/ppermute | solution.py:537
  24.4 9.8 %collective-permute-start.3 = (f32[1,4096]{1,0:T(1,128)S(1)}, f32[1,4096]{1,0:T(1,128)S(1)}, u32[]{:S(2)}, u32[]{:S(2)}) collective-permute-start(f32[1,4096]{1,0:T(1,128)S(1)} %add_parts.1.refs_1_), channel_id=1, source_target_pairs={{0,32},{32,64},{64,96},{96,0},{1,33},{33,65},{65,97},{97,1},{2,34}... | collective-permute-start | bytes 49160 | tf_op jit(solution)/shard_map/ppermute | solution.py:586
  25.7 8.5 %collective-permute-start.4 = (f32[1,4096]{1,0:T(1,128)S(1)}, f32[1,4096]{1,0:T(1,128)S(1)}, u32[]{:S(2)}, u32[]{:S(2)}) collective-permute-start(f32[1,4096]{1,0:T(1,128)S(1)} %add_parts.1.refs_1_), channel_id=1, source_target_pairs={{0,64},{32,96},{64,0},{96,32},{1,65},{33,97},{65,1},{97,33},{2,66}... | collective-permute-start | bytes 49160 | tf_op jit(solution)/shard_map/ppermute | solution.py:586
  28.1 6.1 %collective-permute-start.5 = (f32[1,4096]{1,0:T(1,128)S(1)}, f32[1,4096]{1,0:T(1,128)S(1)}, u32[]{:S(2)}, u32[]{:S(2)}) collective-permute-start(f32[1,4096]{1,0:T(1,128)S(1)} %add_parts.1.refs_1_), channel_id=1, source_target_pairs={{0,96},{32,0},{64,32},{96,64},{1,97},{33,1},{65,33},{97,65},{2,98}... | collective-permute-start | bytes 49160 | tf_op jit(solution)/shard_map/ppermute | solution.py:586
  87.3 6.0 %copy-start = (f32[8,1,5120]{2,1,0:T(1,128)}, f32[8,1,5120]{2,1,0:T(1,128)S(1)}, u32[]{:S(2)}) copy-start(f32[8,1,5120]{2,1,0:T(1,128)S(1)} %all_to_all.33.refs_1_.totals) | copy-start | bytes 491524
  93.3 23.7 %copy-start.3 = (f32[1,4096]{1,0:T(1,128)}, f32[1,4096]{1,0:T(1,128)S(1)}, u32[]{:S(2)}) copy-start(f32[1,4096]{1,0:T(1,128)S(1)} %get-tuple-element.66.scale) | copy-start | bytes 49156
  93.3 18.5 %collective-permute-start.6 = (f32[2,256,512]{2,1,0:T(8,128)}, f32[2,256,512]{2,1,0:T(8,128)}, u32[]{:S(2)}, u32[]{:S(2)}) collective-permute-start(f32[2,256,512]{2,1,0:T(8,128)} %get-tuple-element.57), channel_id=1, source_target_pairs={{0,8},{8,0},{1,9},{9,1},{2,10},{10,2},{3,11},{11,3},{4,12},{12,4},... | collective-permute-start | bytes 3145736 | tf_op jit(solution)/shard_map/ppermute | solution.py:537
  94.9 23.5 %all-to-all-start.4 = ((f32[64,2,1024]{2,1,0:T(2,128)}), f32[64,2,1024]{2,1,0:T(2,128)S(1)}, u32[]{:S(2)}, u32[]{:S(2)}) async-start(f32[64,2,1024]{2,1,0:T(2,128)} %get-tuple-element.63), calls=%async_computation.4 | async-start | bytes 1048576 | tf_op jit(solution)/shard_map/all_to_all | solution.py:533
  114.1 17.7 %collective-permute-start.7 = (f32[4,64,512]{2,1,0:T(8,128)}, f32[4,64,512]{2,1,0:T(8,128)S(1)}, u32[]{:S(2)}, u32[]{:S(2)}) collective-permute-start(f32[4,64,512]{2,1,0:T(8,128)} %bitcast.1), channel_id=1, source_target_pairs={{0,4},{4,0},{1,5},{5,1},{2,6},{6,2},{3,7},{7,3},{8,12},{12,8},{9,1... | collective-permute-start | bytes 1572872 | tf_op jit(solution)/shard_map/ppermute | solution.py:537
  117.0 1.5 collective-permute-start.11
  118.5 0.8 copy-start.5
  118.5 0.8 copy-start.6
  127.3 9.7 %copy-start.7 = (f32[1,128]{1,0:T(1,128)S(1)}, f32[1,128]{1,0:T(1,128)}, u32[]{:S(2)}) copy-start(f32[1,128]{1,0:T(1,128)} %get-tuple-element.70) | copy-start | bytes 1540
  127.3 20.2 %all-to-all-start.5 = ((f32[16,16,1024]{2,1,0:T(8,128)}), f32[16,16,1024]{2,1,0:T(8,128)S(1)}, u32[]{:S(2)}, u32[]{:S(2)}) async-start(f32[16,16,1024]{2,1,0:T(8,128)} %get-tuple-element.69), calls=%async_computation.5 | async-start | bytes 2097152 | tf_op jit(solution)/shard_map/all_to_all | solution.py:533
  131.9 7.8 %collective-permute-start.10 = (f32[64,512]{1,0:T(8,128)S(1)}, f32[64,512]{1,0:T(8,128)S(1)}, u32[]{:S(2)}, u32[]{:S(2)}) collective-permute-start(f32[64,512]{1,0:T(8,128)S(1)} %get-tuple-element.76), channel_id=1, source_target_pairs={{0,3},{1,0},{2,1},{3,2},{4,7},{5,4},{6,5},{7,6},{8,11},{9,8},{10,9... | collective-permute-start | bytes 393224 | tf_op jit(solution)/shard_map/ppermute | solution.py:551
  134.4 8.7 %collective-permute-start.8 = (f32[64,512]{1,0:T(8,128)S(1)}, f32[64,512]{1,0:T(8,128)S(1)}, u32[]{:S(2)}, u32[]{:S(2)}) collective-permute-start(f32[64,512]{1,0:T(8,128)S(1)} %get-tuple-element.75), channel_id=1, source_target_pairs={{0,1},{1,2},{2,3},{3,0},{4,5},{5,6},{6,7},{7,4},{8,9},{9,10},{10,1... | collective-permute-start | bytes 393224 | tf_op jit(solution)/shard_map/ppermute | solution.py:551
  134.4 8.7 %collective-permute-start.9 = (f32[64,512]{1,0:T(8,128)S(1)}, f32[64,512]{1,0:T(8,128)S(1)}, u32[]{:S(2)}, u32[]{:S(2)}) collective-permute-start(f32[64,512]{1,0:T(8,128)S(1)} %get-tuple-element.77), channel_id=1, source_target_pairs={{0,2},{1,3},{2,0},{3,1},{4,6},{5,7},{6,4},{7,5},{8,10},{9,11},{10,... | collective-permute-start | bytes 393224 | tf_op jit(solution)/shard_map/ppermute | solution.py:551
  136.9 2.7 %collective-permute-start.12 = (f32[1,128]{1,0:T(1,128)S(1)}, f32[1,128]{1,0:T(1,128)S(1)}, u32[]{:S(2)}, u32[]{:S(2)}) collective-permute-start(f32[1,128]{1,0:T(1,128)S(1)} %copy-done.7), channel_id=1, source_target_pairs={{0,16},{16,0},{1,17},{17,1},{2,18},{18,2},{3,19},{19,3},{4,20},{20... | collective-permute-start | bytes 1544 | tf_op jit(solution)/shard_map/ppermute | solution.py:537
Sparse Core Ops, SparseCore 0:
  10.6 55.3 all-gather.1

commit v5 on v4

--- a/solution.py
+++ b/solution.py
@@ -181,9 +181,10 @@
         unit[...] = one[...]
         mixed[...] = two[...]
     total = sums_in[...]
-    for j, copy in enumerate(copies):
+    for copy in copies:
+        copy.wait()
+    for j in range(cols // BLOCK):
         here = slice(j * BLOCK, (j + 1) * BLOCK)
-        copy.wait()
         directions, _ = unit_cols(store[:, here].astype(F32))
         dirs[:, here] = directions
         values = jnp.exp2(dot(unit[...], directions) * student_rate)
@@ -521,6 +522,25 @@
     )(place, row_parts, col_parts, turned, expo, scale, far_scale, dirs, inverse, mixed)
 
 
+def join_kernel(pieces, out):
+    count, rows, cols = pieces.shape
+    for share in range(count // 2):
+        first = 4 * (share // 2) + share % 2
+        out[:, share * cols : (share + 1) * cols] = pieces[first] + pieces[first + 2]
+
+
+def join_call(pieces):
+    count, rows, cols = pieces.shape
+    return pl.pallas_call(
+        join_kernel,
+        in_specs=[VMEM],
+        out_specs=VMEM,
+        out_shape=jax.ShapeDtypeStruct((rows, count // 2 * cols), F32),
+        compiler_params=HELD,
+        name="join_pieces",
+    )(pieces)
+
+
 COL_AXES = ("x", "zl")
 ROW_AXES = ("c", "zh", "y")
 CROP_AXES = ("x", "zl", "c")
@@ -615,10 +635,7 @@
     )
     loss = (terms + swap(terms, "zl"))[0, 0] / batch_total
     grad_rows = exchange(grad_rows, CROP_AXES)
-    own_rows, cols = grad_rows.shape[1:]
-    grad_rows = grad_rows.reshape(blocks, 2, 2, own_rows, cols)
-    grad_rows = grad_rows[:, 0] + grad_rows[:, 1]
-    grad_prototypes = jnp.moveaxis(grad_rows, 2, 0).reshape(own_rows, shares * cols)
+    grad_prototypes = join_call(grad_rows)
 
     rows = crops // groups
     far_part, wide_mixed = lax.optimization_barrier((swap(other_part, "c"), wide_mixed))

time: 158 us -> 156 us (0.987)
  local copies, waits for them, and re-layouts: 6.9 us -> 5.1 us
  transfers between devices with their start and end apart: 16 -> 16, of which waited for: 3 -> 3; matrix products, arithmetic and copies ran while one was open for 6% -> 5% of each run, Pallas kernels for 30% -> 30%
where the time goes in v5:
time: 156 us; the launch traced here: 155 us
  Pallas kernels  48.9 us (31%)
  blocking collectives  45.5 us (29%)
  starting transfers between devices  28.6 us (18%)
  between operations  15.4 us (10%)
  waiting for transfers between devices  5.94 us (4%)
  other arithmetic  5.67 us (4%)
  local copies, waits for them, and re-layouts  5.1 us (3%)
    all_to_all x4, blocking collectives, exchange(): return lax.all_to_all(values, axes, 0, 0, tiled=True)  45.5 us
    pallas_call x1, Pallas kernels, wide_call(): pl.pallas_call(wide_kernel, grid_spec=pltpu.PrefetchScalarGridSpec(num_sc...  12 us
    ppermute x7, starting transfers between devices, swap(): return lax.ppermute(values, axis, SWAP)  10 us
    all_to_all x2, starting transfers between devices, exchange(): return lax.all_to_all(values, axes, 0, 0, tiled=True)  9.42 us
    pallas_call x2, Pallas kernels, student_call(): pl.pallas_call(lambda *refs: student_kernel(part, *refs), in_specs=[SMEM,...  8.8 us
    pallas_call x1, Pallas kernels, finish_call(): pl.pallas_call(finish_kernel, grid_spec=pltpu.PrefetchScalarGridSpec(num_...  7.95 us
    pallas_call x1, Pallas kernels, last_sweep(): pl.pallas_call(lambda *refs: last_sweep_kernel(proto_total, *refs), in_sp...  5.67 us
    pallas_call x2, Pallas kernels, col_sweep(): pl.pallas_call(lambda *refs: col_sweep_kernel(batch_total, *refs), in_spe...  4.92 us
  transfers between devices with their start and end apart: 16, of which 3 were waited for; matrix products, arithmetic and copies ran while one was open for 5% of the time, Pallas kernels for 30%

profile of v5, /device:TPU:1, one launch (start us, length us, event | category | flops | bytes accessed | tf_op | source)
XLA Modules:
  0.0 155.2 jit_solution(7099881718515876290)
XLA Ops:
  9.1 1.4 unit_rows.1
  10.5 1.5 collective-permute-start
  12.1 1.7 %constant_dynamic-slice_fusion.1.protos = bf16[256,4096]{1,0:T(8,128)(2,1)S(1)} fusion(bf16[256,8192]{1,0:T(8,128)(2,1)} %t_protos.1, s32[]{:T(128)S(6)} %select_n.46), kind=kLoop, calls=%fused_computation.22 | loop fusion | bytes 4194308 | tf_op jit(solution)/shard_map/dynamic_slice | solution.py:594
  13.9 3.7 %teacher_expo.1 = (bf16[1024,4096]{1,0:T(8,128)(2,1)S(1)}, f32[1,4096]{1,0:T(1,128)S(1)}) custom-call(s32[8]{0:T(128)S(1)} %get-tuple-element.37.place.refs_0_, f32[512,256]{1,0:T(8,128)S(1)} %get-tuple-element.38.own, f32[512,256]{1,0:T(8,128)S(1)} %collective-permute-done.other, bf16[256,4096]{1,0:T(8,128)(2,1)S(1)} %constant_dynamic-slice_fusion.1.protos), custom_call_target="tpu_custom_call" | custom-call | flops 2147483648 | bytes 10485760 | tf_op jit(solution)/shard_map/teacher_expo/pallas_call | solution.py:133
  17.5 1.8 %collective-permute-start.1 = (f32[1,4096]{1,0:T(1,128)S(1)}, f32[1,4096]{1,0:T(1,128)S(1)}, u32[]{:S(2)}, u32[]{:S(2)}) collective-permute-start(f32[1,4096]{1,0:T(1,128)S(1)} %get-tuple-element.40.one), channel_id=1, source_target_pairs={{0,16},{16,0},{1,17},{17,1},{2,18},{18,2},{3,19},{19,3},{4,20},{20... | collective-permute-start | bytes 49160 | tf_op jit(solution)/shard_map/ppermute | solution.py:557
  19.4 4.4 %student_totals.2 = (f32[1024,256]{1,0:T(8,128)S(1)}, f32[1,1024]{1,0:T(1,128)S(1)}, bf16[256,2048]{1,0:T(8,128)(2,1)S(1)}, bf16[1024,256]{1,0:T(8,128)(2,1)S(1)}) custom-call(s32[8]{0:T(128)S(1)} %get-tuple-element.37.place.refs_0_, f32[512,256]{1,0:T(8,128)S(1)} %get-tuple-element.41.refs_1_, f32[512,256]{1,0:T(8,128)S(1)} %collective-permute-done.2.refs_2_, ...), custom_call_target="tpu_custom_call" | custom-call | flops 2147483648 | bytes 4194304 | tf_op jit(solution)/shard_map/student_totals/pallas_call | solution.py:200
  23.8 1.3 collective-permute-start.3
  25.1 2.4 %collective-permute-start.4 = (f32[1,4096]{1,0:T(1,128)S(1)}, f32[1,4096]{1,0:T(1,128)S(1)}, u32[]{:S(2)}, u32[]{:S(2)}) collective-permute-start(f32[1,4096]{1,0:T(1,128)S(1)} %add_parts.1.refs_1_), channel_id=1, source_target_pairs={{0,64},{32,96},{64,0},{96,32},{1,65},{33,97},{65,1},{97,33},{2,66}... | collective-permute-start | bytes 49160 | tf_op jit(solution)/shard_map/ppermute | solution.py:606
  27.6 1.2 collective-permute-start.5
  28.7 4.4 %student_totals.3 = (f32[1024,256]{1,0:T(8,128)S(1)}, f32[1,1024]{1,0:T(1,128)S(1)}, bf16[256,2048]{1,0:T(8,128)(2,1)S(1)}, bf16[1024,256]{1,0:T(8,128)(2,1)S(1)}) custom-call(s32[8]{0:T(128)S(1)} %get-tuple-element.37.place.refs_0_, bf16[1024,256]{1,0:T(8,128)(2,1)S(1)} %get-tuple-element.44.refs_1_, f32[1024,256]{1,0:T(8,128)S(1)} %get-tuple-element.45.refs_2_, ...), custom_call_target="tpu_custom_call" | custom-call | flops 2147483648 | bytes 4194304 | tf_op jit(solution)/shard_map/student_totals/pallas_call | solution.py:200
  33.1 1.8 %row_sweep.2 = f32[16,1,1024]{2,1,0:T(1,128)S(1)} custom-call(bf16[1024,4096]{1,0:T(8,128)(2,1)S(1)} %get-tuple-element.39.refs_0_.refs_1_.refs_2_, f32[1,4096]{1,0:T(1,128)S(1)} %add_parts.1.refs_1_, f32[1,4096]{1,0:T(1,128)S(1)} %collective-permute-done.3.refs_2_, f32[1,4096]{1,0:T(1,128)S(1)} %collective-permute-done.4.refs_3_, ...), custom_call_target="tpu_custom_call" | custom-call | flops 8388608 | bytes 8388608 | tf_op jit(solution)/shard_map/row_sweep/pallas_call | solution.py:252
  34.9 16.2 %all_to_all.30.refs_0_ = f32[16,1,1024]{2,1,0:T(1,128)S(1)} all-to-all(f32[16,1,1024]{2,1,0:T(1,128)S(1)} %row_sweep.2), channel_id=1, replica_groups=mesh['x'=4,'zl'=2,'c'=2,'zh'=2,'y'=4] {'c','zh','y'}, dimensions={0} | all-to-all | bytes 131072 | tf_op jit(solution)/shard_map/all_to_all | solution.py:553
  51.1 2.4 %col_sweep.2 = f32[8,1,4096]{2,1,0:T(1,128)S(1)} custom-call(f32[16,1,1024]{2,1,0:T(1,128)S(1)} %all_to_all.30.refs_0_, bf16[1024,4096]{1,0:T(8,128)(2,1)S(1)} %get-tuple-element.39.refs_0_.refs_1_.refs_2_), custom_call_target="tpu_custom_call" | custom-call | flops 8388608 | bytes 8388608 | tf_op jit(solution)/shard_map/col_sweep/pallas_call | solution.py:281
  53.6 9.3 %all_to_all.31.refs_2_ = f32[8,1,4096]{2,1,0:T(1,128)S(1)} all-to-all(f32[8,1,4096]{2,1,0:T(1,128)S(1)} %col_sweep.2), channel_id=1, replica_groups=mesh['x'=4,'zl'=2,'c'=2,'zh'=2,'y'=4] {'x','zl'}, dimensions={0} | all-to-all | bytes 262144 | tf_op jit(solution)/shard_map/all_to_all | solution.py:553
  62.9 1.8 %row_sweep.3 = f32[16,2,1024]{2,1,0:T(2,128)S(1)} custom-call(bf16[1024,4096]{1,0:T(8,128)(2,1)S(1)} %get-tuple-element.39.refs_0_.refs_1_.refs_2_, f32[1,1024]{1,0:T(1,128)S(1)} %get-tuple-element.48.refs_1_, f32[8,1,4096]{2,1,0:T(1,128)S(1)} %all_to_all.31.refs_2_), custom_call_target="tpu_custom_call" | custom-call | flops 8388608 | bytes 8388608 | tf_op jit(solution)/shard_map/row_sweep/pallas_call | solution.py:252
  64.7 11.6 %all_to_all.32.refs_0_ = f32[16,2,1024]{2,1,0:T(2,128)S(1)} all-to-all(f32[16,2,1024]{2,1,0:T(2,128)S(1)} %row_sweep.3), channel_id=1, replica_groups=mesh['x'=4,'zl'=2,'c'=2,'zh'=2,'y'=4] {'c','zh','y'}, dimensions={0} | all-to-all | bytes 262144 | tf_op jit(solution)/shard_map/all_to_all | solution.py:553
  76.2 2.5 %col_sweep.3 = f32[8,1,5120]{2,1,0:T(1,128)S(1)} custom-call(f32[16,2,1024]{2,1,0:T(2,128)S(1)} %all_to_all.32.refs_0_, bf16[1024,4096]{1,0:T(8,128)(2,1)S(1)} %get-tuple-element.39.refs_0_.refs_1_.refs_2_), custom_call_target="tpu_custom_call" | custom-call | flops 8388608 | bytes 8388608 | tf_op jit(solution)/shard_map/col_sweep/pallas_call | solution.py:281
  78.7 8.4 %all_to_all.33.refs_1_.totals = f32[8,1,5120]{2,1,0:T(1,128)S(1)} all-to-all(f32[8,1,5120]{2,1,0:T(1,128)S(1)} %col_sweep.3), channel_id=1, replica_groups=mesh['x'=4,'zl'=2,'c'=2,'zh'=2,'y'=4] {'x','zl'}, dimensions={0} | all-to-all | bytes 327680 | tf_op jit(solution)/shard_map/all_to_all | solution.py:553
  87.2 5.7 %last_sweep.1 = (f32[64,2,1024]{2,1,0:T(2,128)}, f32[2,256,512]{2,1,0:T(8,128)S(1)}, f32[2,256,512]{2,1,0:T(8,128)S(1)}, f32[1,4096]{1,0:T(1,128)S(1)}) custom-call(s32[8]{0:T(128)S(1)} %get-tuple-element.37.place.refs_0_, f32[8,1,5120]{2,1,0:T(1,128)S(1)} %all_to_all.33.refs_1_.totals, bf16[1024,4096]{1,0:T(8,128)(2,1)S(1)} %get-tuple-element.39.refs_0_.refs_1_.refs_2_, ...), custom_call_target="tpu_custom_call" | custom-call | flops 2155872256 | bytes 10485760 | tf_op jit(solution)/shard_map/last_sweep/pallas_call | solution.py:334
  92.9 1.6 %collective-permute-start.6 = (f32[2,256,512]{2,1,0:T(8,128)S(1)}, f32[2,256,512]{2,1,0:T(8,128)}, u32[]{:S(2)}, u32[]{:S(2)}) collective-permute-start(f32[2,256,512]{2,1,0:T(8,128)S(1)} %get-tuple-element.57), channel_id=1, source_target_pairs={{0,8},{8,0},{1,9},{9,1},{2,10},{10,2},{3,11},{11,3},{4,12},{12,4},... | collective-permute-start | bytes 3145736 | tf_op jit(solution)/shard_map/ppermute | solution.py:557
  94.5 4.9 %all-to-all-start.4 = ((f32[64,2,1024]{2,1,0:T(2,128)}), f32[64,2,1024]{2,1,0:T(2,128)S(1)}, u32[]{:S(2)}, u32[]{:S(2)}) async-start(f32[64,2,1024]{2,1,0:T(2,128)} %get-tuple-element.63), calls=%async_computation.4 | async-start | bytes 1048576 | tf_op jit(solution)/shard_map/all_to_all | solution.py:553
  99.4 12.0 %wide_products.1 = (bf16[4096,1024]{1,0:T(8,128)(2,1)}, bf16[256,4096]{1,0:T(8,128)(2,1)}, bf16[256,1024]{1,0:T(8,128)(2,1)}, f32[1,1024]{1,0:T(1,128)}, f32[256,1024]{1,0:T(8,128)}) custom-call(s32[8]{0:T(128)} %copy-done.4, f32[4096,512]{1,0:T(8,128)} %all-gather.2.cloned.1.call-done.both, f32[8,1,5120]{2,1,0:T(1,128)} %copy-done, ...), custom_call_target="tpu_custom_call" | custom-call | flops 6442450944 | bytes 16777216 | tf_op jit(solution)/shard_map/wide_products/pallas_call | solution.py:385
  111.4 1.4 slice_add_fusion
  112.8 3.0 %collective-permute-start.7 = (f32[4,64,512]{2,1,0:T(8,128)S(1)}, f32[4,64,512]{2,1,0:T(8,128)S(1)}, u32[]{:S(2)}, u32[]{:S(2)}) collective-permute-start(f32[4,64,512]{2,1,0:T(8,128)S(1)} %bitcast.19), channel_id=1, source_target_pairs={{0,4},{4,0},{1,5},{5,1},{2,6},{6,2},{3,7},{7,3},{8,12},{12,8},{9,1... | collective-permute-start | bytes 1572872 | tf_op jit(solution)/shard_map/ppermute | solution.py:557
  118.1 8.0 %finish_protos.1 = (f32[16,16,1024]{2,1,0:T(8,128)}, f32[1,128]{1,0:T(1,128)}) custom-call(s32[8]{0:T(128)} %copy-done.4, f32[64,2,1024]{2,1,0:T(2,128)} %copy-done.5, f32[8,1,5120]{2,1,0:T(1,128)} %copy-done, bf16[256,4096]{1,0:T(8,128)(2,1)} %get-tuple-element.64.turned, bf16[4096,1024]{1,0:T(8,128)(2,1)} %get-tuple-element.65.expo, f32[1,4096]{1,0:T(1,128)} %copy-done.3, ...), custom_call_target="tpu_custom_call" | custom-call | flops 2147483648 | bytes 10485760 | tf_op jit(solution)/shard_map/finish_protos/pallas_call | solution.py:485
  126.1 4.5 %all-to-all-start.5 = ((f32[16,16,1024]{2,1,0:T(8,128)}), f32[16,16,1024]{2,1,0:T(8,128)S(1)}, u32[]{:S(2)}, u32[]{:S(2)}) async-start(f32[16,16,1024]{2,1,0:T(8,128)} %get-tuple-element.69), calls=%async_computation.5 | async-start | bytes 2097152 | tf_op jit(solution)/shard_map/all_to_all | solution.py:553
  130.8 2.5 %collective-permute-start.10 = (f32[64,512]{1,0:T(8,128)S(1)}, f32[64,512]{1,0:T(8,128)S(1)}, u32[]{:S(2)}, u32[]{:S(2)}) collective-permute-start(f32[64,512]{1,0:T(8,128)S(1)} %get-tuple-element.76), channel_id=1, source_target_pairs={{0,3},{1,0},{2,1},{3,2},{4,7},{5,4},{6,5},{7,6},{8,11},{9,8},{10,9... | collective-permute-start | bytes 393224 | tf_op jit(solution)/shard_map/ppermute | solution.py:571
  133.3 1.7 %collective-permute-start.9 = (f32[64,512]{1,0:T(8,128)S(1)}, f32[64,512]{1,0:T(8,128)S(1)}, u32[]{:S(2)}, u32[]{:S(2)}) collective-permute-start(f32[64,512]{1,0:T(8,128)S(1)} %get-tuple-element.77), channel_id=1, source_target_pairs={{0,2},{1,3},{2,0},{3,1},{4,6},{5,7},{6,4},{7,5},{8,10},{9,11},{10,... | collective-permute-start | bytes 393224 | tf_op jit(solution)/shard_map/ppermute | solution.py:571
  135.7 1.4 collective-permute-start.12
  138.5 3.5 %collective-permute-done.8 = f32[64,512]{1,0:T(8,128)S(1)} collective-permute-done((f32[64,512]{1,0:T(8,128)S(1)}, f32[64,512]{1,0:T(8,128)S(1)}, u32[]{:S(2)}, u32[]{:S(2)}) %collective-permute-start.8) | collective-permute-done | bytes 131104 | tf_op jit(solution)/shard_map/ppermute | solution.py:571
  143.0 1.5 fusion.6
  144.5 1.8 %all-to-all-done.5.pieces = f32[16,16,1024]{2,1,0:T(8,128)S(1)} async-done(((f32[16,16,1024]{2,1,0:T(8,128)}), f32[16,16,1024]{2,1,0:T(8,128)S(1)}, u32[]{:S(2)}, u32[]{:S(2)}) %all-to-all-start.5) | async-done | bytes 1048608 | tf_op jit(solution)/shard_map/all_to_all | solution.py:553
  (47 shorter events, 8.4 us)
Async XLA Ops:
  7.2 92.2 %all-gather.2.cloned.1.call-start = ((), (), s32[]{:S(2)}) async-start(), calls=%async_computation.6 | async-start | bytes 9437184 | tf_op jit(solution)/shard_map/all_gather | solution.py:591
  7.2 1.0 copy-start.1
  8.2 0.9 copy-start.2
  10.5 76.7 %copy-start.4 = (s32[8]{0:T(128)}, s32[8]{0:T(128)S(1)}, u32[]{:S(2)}) copy-start(s32[8]{0:T(128)S(1)} %get-tuple-element.37.place.refs_0_) | copy-start | bytes 100
  10.5 3.3 %collective-permute-start = (f32[512,256]{1,0:T(8,128)S(1)}, f32[512,256]{1,0:T(8,128)S(1)}, u32[]{:S(2)}, u32[]{:S(2)}) collective-permute-start(f32[512,256]{1,0:T(8,128)S(1)} %get-tuple-element.38.own), channel_id=1, source_target_pairs={{0,8},{8,0},{1,9},{9,1},{2,10},{10,2},{3,11},{11,3},{4,12},{12,4},... | collective-permute-start | bytes 1572872 | tf_op jit(solution)/shard_map/ppermute | solution.py:557
  12.0 7.3 %collective-permute-start.2 = (f32[512,256]{1,0:T(8,128)S(1)}, f32[512,256]{1,0:T(8,128)S(1)}, u32[]{:S(2)}, u32[]{:S(2)}) collective-permute-start(f32[512,256]{1,0:T(8,128)S(1)} %get-tuple-element.41.refs_1_), channel_id=1, source_target_pairs={{0,8},{8,0},{1,9},{9,1},{2,10},{10,2},{3,11},{11,3},{4,12},{12,4},... | collective-permute-start | bytes 1572872 | tf_op jit(solution)/shard_map/ppermute | solution.py:557
  17.5 6.3 %collective-permute-start.1 = (f32[1,4096]{1,0:T(1,128)S(1)}, f32[1,4096]{1,0:T(1,128)S(1)}, u32[]{:S(2)}, u32[]{:S(2)}) collective-permute-start(f32[1,4096]{1,0:T(1,128)S(1)} %get-tuple-element.40.one), channel_id=1, source_target_pairs={{0,16},{16,0},{1,17},{17,1},{2,18},{18,2},{3,19},{19,3},{4,20},{20... | collective-permute-start | bytes 49160 | tf_op jit(solution)/shard_map/ppermute | solution.py:557
  23.8 9.3 %collective-permute-start.3 = (f32[1,4096]{1,0:T(1,128)S(1)}, f32[1,4096]{1,0:T(1,128)S(1)}, u32[]{:S(2)}, u32[]{:S(2)}) collective-permute-start(f32[1,4096]{1,0:T(1,128)S(1)} %add_parts.1.refs_1_), channel_id=1, source_target_pairs={{0,32},{32,64},{64,96},{96,0},{1,33},{33,65},{65,97},{97,1},{2,34}... | collective-permute-start | bytes 49160 | tf_op jit(solution)/shard_map/ppermute | solution.py:606
  25.1 8.0 %collective-permute-start.4 = (f32[1,4096]{1,0:T(1,128)S(1)}, f32[1,4096]{1,0:T(1,128)S(1)}, u32[]{:S(2)}, u32[]{:S(2)}) collective-permute-start(f32[1,4096]{1,0:T(1,128)S(1)} %add_parts.1.refs_1_), channel_id=1, source_target_pairs={{0,64},{32,96},{64,0},{96,32},{1,65},{33,97},{65,1},{97,33},{2,66}... | collective-permute-start | bytes 49160 | tf_op jit(solution)/shard_map/ppermute | solution.py:606
  27.6 5.5 %collective-permute-start.5 = (f32[1,4096]{1,0:T(1,128)S(1)}, f32[1,4096]{1,0:T(1,128)S(1)}, u32[]{:S(2)}, u32[]{:S(2)}) collective-permute-start(f32[1,4096]{1,0:T(1,128)S(1)} %add_parts.1.refs_1_), channel_id=1, source_target_pairs={{0,96},{32,0},{64,32},{96,64},{1,97},{33,1},{65,33},{97,65},{2,98}... | collective-permute-start | bytes 49160 | tf_op jit(solution)/shard_map/ppermute | solution.py:606
  87.2 5.7 %copy-start = (f32[8,1,5120]{2,1,0:T(1,128)}, f32[8,1,5120]{2,1,0:T(1,128)S(1)}, u32[]{:S(2)}) copy-start(f32[8,1,5120]{2,1,0:T(1,128)S(1)} %all_to_all.33.refs_1_.totals) | copy-start | bytes 491524
  92.8 22.9 %copy-start.3 = (f32[1,4096]{1,0:T(1,128)}, f32[1,4096]{1,0:T(1,128)S(1)}, u32[]{:S(2)}) copy-start(f32[1,4096]{1,0:T(1,128)S(1)} %get-tuple-element.66.scale) | copy-start | bytes 49156
  92.9 18.6 %collective-permute-start.6 = (f32[2,256,512]{2,1,0:T(8,128)S(1)}, f32[2,256,512]{2,1,0:T(8,128)}, u32[]{:S(2)}, u32[]{:S(2)}) collective-permute-start(f32[2,256,512]{2,1,0:T(8,128)S(1)} %get-tuple-element.57), channel_id=1, source_target_pairs={{0,8},{8,0},{1,9},{9,1},{2,10},{10,2},{3,11},{11,3},{4,12},{12,4},... | collective-permute-start | bytes 3145736 | tf_op jit(solution)/shard_map/ppermute | solution.py:557
  94.5 22.8 %all-to-all-start.4 = ((f32[64,2,1024]{2,1,0:T(2,128)}), f32[64,2,1024]{2,1,0:T(2,128)S(1)}, u32[]{:S(2)}, u32[]{:S(2)}) async-start(f32[64,2,1024]{2,1,0:T(2,128)} %get-tuple-element.63), calls=%async_computation.4 | async-start | bytes 1048576 | tf_op jit(solution)/shard_map/all_to_all | solution.py:553
  112.8 17.8 %collective-permute-start.7 = (f32[4,64,512]{2,1,0:T(8,128)S(1)}, f32[4,64,512]{2,1,0:T(8,128)S(1)}, u32[]{:S(2)}, u32[]{:S(2)}) collective-permute-start(f32[4,64,512]{2,1,0:T(8,128)S(1)} %bitcast.19), channel_id=1, source_target_pairs={{0,4},{4,0},{1,5},{5,1},{2,6},{6,2},{3,7},{7,3},{8,12},{12,8},{9,1... | collective-permute-start | bytes 1572872 | tf_op jit(solution)/shard_map/ppermute | solution.py:557
  115.8 1.5 collective-permute-start.11
  117.3 0.8 copy-start.5
  117.3 0.8 copy-start.6
  126.1 9.6 %copy-start.7 = (f32[1,128]{1,0:T(1,128)S(1)}, f32[1,128]{1,0:T(1,128)}, u32[]{:S(2)}) copy-start(f32[1,128]{1,0:T(1,128)} %get-tuple-element.70) | copy-start | bytes 1540
  126.1 20.2 %all-to-all-start.5 = ((f32[16,16,1024]{2,1,0:T(8,128)}), f32[16,16,1024]{2,1,0:T(8,128)S(1)}, u32[]{:S(2)}, u32[]{:S(2)}) async-start(f32[16,16,1024]{2,1,0:T(8,128)} %get-tuple-element.69), calls=%async_computation.5 | async-start | bytes 2097152 | tf_op jit(solution)/shard_map/all_to_all | solution.py:553
  130.8 7.7 %collective-permute-start.10 = (f32[64,512]{1,0:T(8,128)S(1)}, f32[64,512]{1,0:T(8,128)S(1)}, u32[]{:S(2)}, u32[]{:S(2)}) collective-permute-start(f32[64,512]{1,0:T(8,128)S(1)} %get-tuple-element.76), channel_id=1, source_target_pairs={{0,3},{1,0},{2,1},{3,2},{4,7},{5,4},{6,5},{7,6},{8,11},{9,8},{10,9... | collective-permute-start | bytes 393224 | tf_op jit(solution)/shard_map/ppermute | solution.py:571
  133.3 8.7 %collective-permute-start.8 = (f32[64,512]{1,0:T(8,128)S(1)}, f32[64,512]{1,0:T(8,128)S(1)}, u32[]{:S(2)}, u32[]{:S(2)}) collective-permute-start(f32[64,512]{1,0:T(8,128)S(1)} %get-tuple-element.75), channel_id=1, source_target_pairs={{0,1},{1,2},{2,3},{3,0},{4,5},{5,6},{6,7},{7,4},{8,9},{9,10},{10,1... | collective-permute-start | bytes 393224 | tf_op jit(solution)/shard_map/ppermute | solution.py:571
  133.3 8.7 %collective-permute-start.9 = (f32[64,512]{1,0:T(8,128)S(1)}, f32[64,512]{1,0:T(8,128)S(1)}, u32[]{:S(2)}, u32[]{:S(2)}) collective-permute-start(f32[64,512]{1,0:T(8,128)S(1)} %get-tuple-element.77), channel_id=1, source_target_pairs={{0,2},{1,3},{2,0},{3,1},{4,6},{5,7},{6,4},{7,5},{8,10},{9,11},{10,... | collective-permute-start | bytes 393224 | tf_op jit(solution)/shard_map/ppermute | solution.py:571
  135.7 2.7 %collective-permute-start.12 = (f32[1,128]{1,0:T(1,128)S(1)}, f32[1,128]{1,0:T(1,128)S(1)}, u32[]{:S(2)}, u32[]{:S(2)}) collective-permute-start(f32[1,128]{1,0:T(1,128)S(1)} %copy-done.7), channel_id=1, source_target_pairs={{0,16},{16,0},{1,17},{17,1},{2,18},{18,2},{3,19},{19,3},{4,20},{20... | collective-permute-start | bytes 1544 | tf_op jit(solution)/shard_map/ppermute | solution.py:557
Sparse Core Ops, SparseCore 0:
  10.6 55.2 all-gather.1

commit v6 on v5

--- a/solution.py
+++ b/solution.py
@@ -117,11 +117,16 @@
     return jnp.concatenate([first, second], axis=0)
 
 
-def teacher_kernel(place, own, other, protos, expo, col_part, unit):
+def teacher_kernel(place, own, other, protos, expo, col_part, unit, store, sem):
+    half = store.shape[1]
+    there = pl.ds(pl.multiple_of(place[0] * half, half), half)
+    copy = pltpu.make_async_copy(protos.at[:, there], store, sem)
+    copy.start()
     unit[...] = pair_rows(place[0], own[...], other[...])
-    for first in range(0, protos.shape[1], BLOCK):
+    copy.wait()
+    for first in range(0, half, BLOCK):
         here = slice(first, first + BLOCK)
-        directions, _ = unit_cols(protos[:, here].astype(F32))
+        directions, _ = unit_cols(store[:, here].astype(F32))
         values = jnp.exp2(dot(unit[...], directions) * teacher_rate)
         expo[:, here] = values.astype(BF16)
         col_part[:, here] = jnp.sum(values, axis=0, keepdims=True)
@@ -129,17 +134,21 @@
 
 def teacher_call(place, own, other, protos):
     rows, width = own.shape
-    cols = protos.shape[1]
+    cols = protos.shape[1] // 2
     return pl.pallas_call(
         teacher_kernel,
-        in_specs=[SMEM, VMEM, VMEM, VMEM],
+        in_specs=[SMEM, VMEM, VMEM, HBM],
         out_specs=[VMEM, VMEM],
         out_shape=[
             jax.ShapeDtypeStruct((2 * rows, cols), BF16),
             jax.ShapeDtypeStruct((1, cols), F32),
         ],
-        scratch_shapes=[pltpu.VMEM((2 * rows, width), BF16)],
-        compiler_params=HELD,
+        scratch_shapes=[
+            pltpu.VMEM((2 * rows, width), BF16),
+            pltpu.VMEM((width, cols), BF16),
+            pltpu.SemaphoreType.DMA,
+        ],
+        compiler_params=TIGHT,
         cost_estimate=pl.CostEstimate(
             flops=4 * rows * cols * width,
             bytes_accessed=2 * 2 * rows * cols + 2 * width * cols,
@@ -590,10 +599,8 @@
     teacher_other = swap(teacher_unit, "c")
     gathered = lax.all_gather(both, GATHER_AXES, axis=0, tiled=True)
     student_other = swap(student_unit, "c")
-    half = teacher_protos.shape[1] // 2
-    half_protos = lax.dynamic_slice_in_dim(teacher_protos, core * half, half, 1)
-
-    expo, col_part = teacher_call(place, teacher_unit, teacher_other, half_protos)
+
+    expo, col_part = teacher_call(place, teacher_unit, teacher_other, teacher_protos)
 
     near_part = swap(col_part, "zl")
     no_sums = jnp.zeros((1, 2 * crops), F32)

time: 156 us -> 161 us (1.032)
  Pallas kernels: 48.9 us -> 52.4 us
    pallas_call x1, Pallas kernels: 3.67 us -> 7.08 us  [teacher_call(): pl.pallas_call(teacher_kernel, in_specs=[SMEM, VMEM, VMEM, HBM], out_spec...]
    unnamed x16 -> x20, local copies, waits for them, and re-layouts: 2.68 us -> 4.88 us
    dynamic_slice x1 -> x0, local copies, waits for them, and re-layouts: 1.73 us -> none  [on_device(): half_protos = lax.dynamic_slice_in_dim(teacher_protos, core * half, half, 1)]
    ppermute x7, waiting for transfers between devices: 0.54 us -> 2.25 us  [swap(): return lax.ppermute(values, axis, SWAP)]
  transfers between devices with their start and end apart: 16 -> 16, of which waited for: 3 -> 4; matrix products, arithmetic and copies ran while one was open for 5% -> 4% of each run, Pallas kernels for 30% -> 31%
where the time goes in v6:
time: 161 us; the launch traced here: 160 us
  Pallas kernels  52.4 us (33%)
  blocking collectives  44.9 us (28%)
  starting transfers between devices  28.3 us (18%)
  between operations  15.5 us (10%)
  waiting for transfers between devices  6.65 us (4%)
  other arithmetic  6.35 us (4%)
  local copies, waits for them, and re-layouts  5.67 us (4%)
    all_to_all x4, blocking collectives, exchange(): return lax.all_to_all(values, axes, 0, 0, tiled=True)  44.9 us
    pallas_call x1, Pallas kernels, wide_call(): pl.pallas_call(wide_kernel, grid_spec=pltpu.PrefetchScalarGridSpec(num_sc...  11.9 us
    ppermute x7, starting transfers between devices, swap(): return lax.ppermute(values, axis, SWAP)  10 us
    pallas_call x2, Pallas kernels, student_call(): pl.pallas_call(lambda *refs: student_kernel(part, *refs), in_specs=[SMEM,...  9.11 us
    all_to_all x2, starting transfers between devices, exchange(): return lax.all_to_all(values, axes, 0, 0, tiled=True)  9.09 us
    pallas_call x1, Pallas kernels, finish_call(): pl.pallas_call(finish_kernel, grid_spec=pltpu.PrefetchScalarGridSpec(num_...  7.89 us
    pallas_call x1, Pallas kernels, teacher_call(): pl.pallas_call(teacher_kernel, in_specs=[SMEM, VMEM, VMEM, HBM], out_spec...  7.08 us
    pallas_call x1, Pallas kernels, last_sweep(): pl.pallas_call(lambda *refs: last_sweep_kernel(proto_total, *refs), in_sp...  5.67 us
  transfers between devices with their start and end apart: 16, of which 4 were waited for; matrix products, arithmetic and copies ran while one was open for 4% of the time, Pallas kernels for 31%

profile of v6, /device:TPU:1, one launch (start us, length us, event | category | flops | bytes accessed | tf_op | source)
XLA Modules:
  0.0 159.7 jit_solution(1184038349906634918)
XLA Ops:
  9.1 1.4 unit_rows.1
  10.5 1.5 collective-permute-start
  12.1 1.4 collective-permute-done.other
  13.6 2.2 %copy-done.5 = bf16[256,8192]{1,0:T(8,128)(2,1)S(1)} copy-done((bf16[256,8192]{1,0:T(8,128)(2,1)S(1)}, bf16[256,8192]{1,0:T(8,128)(2,1)}, u32[]{:S(2)}) %copy-start.5) | copy-done | bytes 4194328
  15.7 7.1 %teacher_expo.1 = (bf16[1024,4096]{1,0:T(8,128)(2,1)}, f32[1,4096]{1,0:T(1,128)S(1)}) custom-call(s32[8]{0:T(128)S(1)} %get-tuple-element.37.place.refs_0_, f32[512,256]{1,0:T(8,128)S(1)} %get-tuple-element.38.own, f32[512,256]{1,0:T(8,128)S(1)} %collective-permute-done.other, bf16[256,8192]{1,0:T(8,128)(2,1)S(1)} %copy-done.5), custom_call_target="tpu_custom_call" | custom-call | flops 2147483648 | bytes 10485760 | tf_op jit(solution)/shard_map/teacher_expo/pallas_call | solution.py:138
  22.8 1.8 %collective-permute-start.1 = (f32[1,4096]{1,0:T(1,128)S(1)}, f32[1,4096]{1,0:T(1,128)S(1)}, u32[]{:S(2)}, u32[]{:S(2)}) collective-permute-start(f32[1,4096]{1,0:T(1,128)S(1)} %get-tuple-element.40.one), channel_id=1, source_target_pairs={{0,16},{16,0},{1,17},{17,1},{2,18},{18,2},{3,19},{19,3},{4,20},{20... | collective-permute-start | bytes 49160 | tf_op jit(solution)/shard_map/ppermute | solution.py:566
  24.6 4.7 %student_totals.2 = (f32[1024,256]{1,0:T(8,128)S(1)}, f32[1,1024]{1,0:T(1,128)S(1)}, bf16[256,2048]{1,0:T(8,128)(2,1)S(1)}, bf16[1024,256]{1,0:T(8,128)(2,1)S(1)}) custom-call(s32[8]{0:T(128)S(1)} %get-tuple-element.37.place.refs_0_, f32[512,256]{1,0:T(8,128)S(1)} %get-tuple-element.41.refs_1_, f32[512,256]{1,0:T(8,128)S(1)} %collective-permute-done.2.refs_2_, ...), custom_call_target="tpu_custom_call" | custom-call | flops 2147483648 | bytes 4194304 | tf_op jit(solution)/shard_map/student_totals/pallas_call | solution.py:209
  29.4 1.3 collective-permute-start.3
  30.7 2.4 %collective-permute-start.4 = (f32[1,4096]{1,0:T(1,128)S(1)}, f32[1,4096]{1,0:T(1,128)S(1)}, u32[]{:S(2)}, u32[]{:S(2)}) collective-permute-start(f32[1,4096]{1,0:T(1,128)S(1)} %add_parts.1.refs_1_), channel_id=1, source_target_pairs={{0,64},{32,96},{64,0},{96,32},{1,65},{33,97},{65,1},{97,33},{2,66}... | collective-permute-start | bytes 49160 | tf_op jit(solution)/shard_map/ppermute | solution.py:613
  34.3 4.4 %student_totals.3 = (f32[1024,256]{1,0:T(8,128)S(1)}, f32[1,1024]{1,0:T(1,128)S(1)}, bf16[256,2048]{1,0:T(8,128)(2,1)S(1)}, bf16[1024,256]{1,0:T(8,128)(2,1)S(1)}) custom-call(s32[8]{0:T(128)S(1)} %get-tuple-element.37.place.refs_0_, bf16[1024,256]{1,0:T(8,128)(2,1)S(1)} %get-tuple-element.44.refs_1_, f32[1024,256]{1,0:T(8,128)S(1)} %get-tuple-element.45.refs_2_, ...), custom_call_target="tpu_custom_call" | custom-call | flops 2147483648 | bytes 4194304 | tf_op jit(solution)/shard_map/student_totals/pallas_call | solution.py:209
  38.8 1.8 %row_sweep.2 = f32[16,1,1024]{2,1,0:T(1,128)S(1)} custom-call(bf16[1024,4096]{1,0:T(8,128)(2,1)S(1)} %bitcast.19, f32[1,4096]{1,0:T(1,128)S(1)} %add_parts.1.refs_1_, f32[1,4096]{1,0:T(1,128)S(1)} %collective-permute-done.3.refs_2_, f32[1,4096]{1,0:T(1,128)S(1)} %collective-permute-done.4.refs_3_, f32[1,4096]{1,0:T(1,128)S(1)} %collective-permute-done.5.refs_4_), custom_call_target="tpu_custom_call" | custom-call | flops 8388608 | bytes 8388608 | tf_op jit(solution)/shard_map/row_sweep/pallas_call | solution.py:261
  40.6 16.1 %all_to_all.30.refs_0_ = f32[16,1,1024]{2,1,0:T(1,128)S(1)} all-to-all(f32[16,1,1024]{2,1,0:T(1,128)S(1)} %row_sweep.2), channel_id=1, replica_groups=mesh['x'=4,'zl'=2,'c'=2,'zh'=2,'y'=4] {'c','zh','y'}, dimensions={0} | all-to-all | bytes 131072 | tf_op jit(solution)/shard_map/all_to_all | solution.py:562
  56.6 2.4 %col_sweep.2 = f32[8,1,4096]{2,1,0:T(1,128)S(1)} custom-call(f32[16,1,1024]{2,1,0:T(1,128)S(1)} %all_to_all.30.refs_0_, bf16[1024,4096]{1,0:T(8,128)(2,1)S(1)} %bitcast.19), custom_call_target="tpu_custom_call" | custom-call | flops 8388608 | bytes 8388608 | tf_op jit(solution)/shard_map/col_sweep/pallas_call | solution.py:290
  59.1 7.6 %all_to_all.31.refs_2_ = f32[8,1,4096]{2,1,0:T(1,128)S(1)} all-to-all(f32[8,1,4096]{2,1,0:T(1,128)S(1)} %col_sweep.2), channel_id=1, replica_groups=mesh['x'=4,'zl'=2,'c'=2,'zh'=2,'y'=4] {'x','zl'}, dimensions={0} | all-to-all | bytes 262144 | tf_op jit(solution)/shard_map/all_to_all | solution.py:562
  66.7 1.8 %row_sweep.3 = f32[16,2,1024]{2,1,0:T(2,128)S(1)} custom-call(bf16[1024,4096]{1,0:T(8,128)(2,1)S(1)} %bitcast.19, f32[1,1024]{1,0:T(1,128)S(1)} %get-tuple-element.48.refs_1_, f32[8,1,4096]{2,1,0:T(1,128)S(1)} %all_to_all.31.refs_2_), custom_call_target="tpu_custom_call" | custom-call | flops 8388608 | bytes 8388608 | tf_op jit(solution)/shard_map/row_sweep/pallas_call | solution.py:261
  68.5 12.7 %all_to_all.32.refs_0_ = f32[16,2,1024]{2,1,0:T(2,128)S(1)} all-to-all(f32[16,2,1024]{2,1,0:T(2,128)S(1)} %row_sweep.3), channel_id=1, replica_groups=mesh['x'=4,'zl'=2,'c'=2,'zh'=2,'y'=4] {'c','zh','y'}, dimensions={0} | all-to-all | bytes 262144 | tf_op jit(solution)/shard_map/all_to_all | solution.py:562
  81.3 2.5 %col_sweep.3 = f32[8,1,5120]{2,1,0:T(1,128)S(1)} custom-call(f32[16,2,1024]{2,1,0:T(2,128)S(1)} %all_to_all.32.refs_0_, bf16[1024,4096]{1,0:T(8,128)(2,1)S(1)} %bitcast.19), custom_call_target="tpu_custom_call" | custom-call | flops 8388608 | bytes 8388608 | tf_op jit(solution)/shard_map/col_sweep/pallas_call | solution.py:290
  83.7 8.5 %all_to_all.33.refs_1_.totals = f32[8,1,5120]{2,1,0:T(1,128)S(1)} all-to-all(f32[8,1,5120]{2,1,0:T(1,128)S(1)} %col_sweep.3), channel_id=1, replica_groups=mesh['x'=4,'zl'=2,'c'=2,'zh'=2,'y'=4] {'x','zl'}, dimensions={0} | all-to-all | bytes 327680 | tf_op jit(solution)/shard_map/all_to_all | solution.py:562
  92.2 5.7 %last_sweep.1 = (f32[64,2,1024]{2,1,0:T(2,128)}, f32[2,256,512]{2,1,0:T(8,128)S(1)}, f32[2,256,512]{2,1,0:T(8,128)S(1)}, f32[1,4096]{1,0:T(1,128)S(1)}) custom-call(s32[8]{0:T(128)S(1)} %get-tuple-element.37.place.refs_0_, f32[8,1,5120]{2,1,0:T(1,128)S(1)} %all_to_all.33.refs_1_.totals, bf16[1024,4096]{1,0:T(8,128)(2,1)S(1)} %bitcast.19, ...), custom_call_target="tpu_custom_call" | custom-call | flops 2155872256 | bytes 10485760 | tf_op jit(solution)/shard_map/last_sweep/pallas_call | solution.py:343
  97.9 1.7 %collective-permute-start.6 = (f32[2,256,512]{2,1,0:T(8,128)S(1)}, f32[2,256,512]{2,1,0:T(8,128)}, u32[]{:S(2)}, u32[]{:S(2)}) collective-permute-start(f32[2,256,512]{2,1,0:T(8,128)S(1)} %get-tuple-element.57), channel_id=1, source_target_pairs={{0,8},{8,0},{1,9},{9,1},{2,10},{10,2},{3,11},{11,3},{4,12},{12,4},... | collective-permute-start | bytes 3145736 | tf_op jit(solution)/shard_map/ppermute | solution.py:566
  99.5 4.6 %all-to-all-start.4 = ((f32[64,2,1024]{2,1,0:T(2,128)}), f32[64,2,1024]{2,1,0:T(2,128)S(1)}, u32[]{:S(2)}, u32[]{:S(2)}) async-start(f32[64,2,1024]{2,1,0:T(2,128)} %get-tuple-element.63), calls=%async_computation.4 | async-start | bytes 1048576 | tf_op jit(solution)/shard_map/all_to_all | solution.py:562
  104.2 11.9 %wide_products.1 = (bf16[4096,1024]{1,0:T(8,128)(2,1)}, bf16[256,4096]{1,0:T(8,128)(2,1)}, bf16[256,1024]{1,0:T(8,128)(2,1)}, f32[1,1024]{1,0:T(1,128)}, f32[256,1024]{1,0:T(8,128)}) custom-call(s32[8]{0:T(128)} %copy-done.4, f32[4096,512]{1,0:T(8,128)} %all-gather.2.cloned.1.call-done.both, f32[8,1,5120]{2,1,0:T(1,128)} %copy-done, ...), custom_call_target="tpu_custom_call" | custom-call | flops 6442450944 | bytes 16777216 | tf_op jit(solution)/shard_map/wide_products/pallas_call | solution.py:394
  116.1 1.4 slice_add_fusion
  117.5 3.0 %collective-permute-start.7 = (f32[4,64,512]{2,1,0:T(8,128)S(1)}, f32[4,64,512]{2,1,0:T(8,128)S(1)}, u32[]{:S(2)}, u32[]{:S(2)}) collective-permute-start(f32[4,64,512]{2,1,0:T(8,128)S(1)} %bitcast.21), channel_id=1, source_target_pairs={{0,4},{4,0},{1,5},{5,1},{2,6},{6,2},{3,7},{7,3},{8,12},{12,8},{9,1... | collective-permute-start | bytes 1572872 | tf_op jit(solution)/shard_map/ppermute | solution.py:566
  122.8 7.9 %finish_protos.1 = (f32[16,16,1024]{2,1,0:T(8,128)}, f32[1,128]{1,0:T(1,128)}) custom-call(s32[8]{0:T(128)} %copy-done.4, f32[64,2,1024]{2,1,0:T(2,128)} %copy-done.6, f32[8,1,5120]{2,1,0:T(1,128)} %copy-done, bf16[256,4096]{1,0:T(8,128)(2,1)} %get-tuple-element.64.turned, bf16[4096,1024]{1,0:T(8,128)(2,1)} %get-tuple-element.65.expo, f32[1,4096]{1,0:T(1,128)} %copy-done.3, ...), custom_call_target="tpu_custom_call" | custom-call | flops 2147483648 | bytes 10485760 | tf_op jit(solution)/shard_map/finish_protos/pallas_call | solution.py:494
  130.7 4.5 %all-to-all-start.5 = ((f32[16,16,1024]{2,1,0:T(8,128)}), f32[16,16,1024]{2,1,0:T(8,128)S(1)}, u32[]{:S(2)}, u32[]{:S(2)}) async-start(f32[16,16,1024]{2,1,0:T(8,128)} %get-tuple-element.69), calls=%async_computation.5 | async-start | bytes 2097152 | tf_op jit(solution)/shard_map/all_to_all | solution.py:562
  135.3 2.5 %collective-permute-start.10 = (f32[64,512]{1,0:T(8,128)S(1)}, f32[64,512]{1,0:T(8,128)S(1)}, u32[]{:S(2)}, u32[]{:S(2)}) collective-permute-start(f32[64,512]{1,0:T(8,128)S(1)} %get-tuple-element.76), channel_id=1, source_target_pairs={{0,3},{1,0},{2,1},{3,2},{4,7},{5,4},{6,5},{7,6},{8,11},{9,8},{10,9... | collective-permute-start | bytes 393224 | tf_op jit(solution)/shard_map/ppermute | solution.py:580
  137.8 1.7 %collective-permute-start.9 = (f32[64,512]{1,0:T(8,128)S(1)}, f32[64,512]{1,0:T(8,128)S(1)}, u32[]{:S(2)}, u32[]{:S(2)}) collective-permute-start(f32[64,512]{1,0:T(8,128)S(1)} %get-tuple-element.77), channel_id=1, source_target_pairs={{0,2},{1,3},{2,0},{3,1},{4,6},{5,7},{6,4},{7,5},{8,10},{9,11},{10,... | collective-permute-start | bytes 393224 | tf_op jit(solution)/shard_map/ppermute | solution.py:580
  140.4 1.3 collective-permute-start.12
  144.1 2.5 %collective-permute-done.8 = f32[64,512]{1,0:T(8,128)S(1)} collective-permute-done((f32[64,512]{1,0:T(8,128)S(1)}, f32[64,512]{1,0:T(8,128)S(1)}, u32[]{:S(2)}, u32[]{:S(2)}) %collective-permute-start.8) | collective-permute-done | bytes 131104 | tf_op jit(solution)/shard_map/ppermute | solution.py:580
  147.6 1.5 fusion.6
  149.1 1.8 %all-to-all-done.5.pieces = f32[16,16,1024]{2,1,0:T(8,128)S(1)} async-done(((f32[16,16,1024]{2,1,0:T(8,128)}), f32[16,16,1024]{2,1,0:T(8,128)S(1)}, u32[]{:S(2)}, u32[]{:S(2)}) %all-to-all-start.5) | async-done | bytes 1048608 | tf_op jit(solution)/shard_map/all_to_all | solution.py:562
  (51 shorter events, 10.6 us)
Async XLA Ops:
  7.2 97.0 %all-gather.2.cloned.1.call-start = ((), (), s32[]{:S(2)}) async-start(), calls=%async_computation.6 | async-start | bytes 9437184 | tf_op jit(solution)/shard_map/all_gather | solution.py:600
  7.2 1.0 copy-start.1
  8.2 0.9 copy-start.2
  10.5 81.7 %copy-start.4 = (s32[8]{0:T(128)}, s32[8]{0:T(128)S(1)}, u32[]{:S(2)}) copy-start(s32[8]{0:T(128)S(1)} %get-tuple-element.37.place.refs_0_) | copy-start | bytes 100
  10.5 3.0 %collective-permute-start = (f32[512,256]{1,0:T(8,128)S(1)}, f32[512,256]{1,0:T(8,128)S(1)}, u32[]{:S(2)}, u32[]{:S(2)}) collective-permute-start(f32[512,256]{1,0:T(8,128)S(1)} %get-tuple-element.38.own), channel_id=1, source_target_pairs={{0,8},{8,0},{1,9},{9,1},{2,10},{10,2},{3,11},{11,3},{4,12},{12,4},... | collective-permute-start | bytes 1572872 | tf_op jit(solution)/shard_map/ppermute | solution.py:566
  12.0 12.6 %collective-permute-start.2 = (f32[512,256]{1,0:T(8,128)S(1)}, f32[512,256]{1,0:T(8,128)S(1)}, u32[]{:S(2)}, u32[]{:S(2)}) collective-permute-start(f32[512,256]{1,0:T(8,128)S(1)} %get-tuple-element.41.refs_1_), channel_id=1, source_target_pairs={{0,8},{8,0},{1,9},{9,1},{2,10},{10,2},{3,11},{11,3},{4,12},{12,4},... | collective-permute-start | bytes 1572872 | tf_op jit(solution)/shard_map/ppermute | solution.py:566
  13.6 2.2 %copy-start.5 = (bf16[256,8192]{1,0:T(8,128)(2,1)S(1)}, bf16[256,8192]{1,0:T(8,128)(2,1)}, u32[]{:S(2)}) copy-start(bf16[256,8192]{1,0:T(8,128)(2,1)} %t_protos.1) | copy-start | bytes 12582916
  22.8 15.9 %slice-start = ((s8[8388608]{0:T(1024)(128)(4,1)}), s8[4194304]{0:T(1024)(128)(4,1)S(1)}, s32[]{:S(2)}) async-start(s8[8388608]{0:T(1024)(128)(4,1)} %bitcast.18), calls=%async_computation.7 | async-start | bytes 8388608
  22.8 6.5 %collective-permute-start.1 = (f32[1,4096]{1,0:T(1,128)S(1)}, f32[1,4096]{1,0:T(1,128)S(1)}, u32[]{:S(2)}, u32[]{:S(2)}) collective-permute-start(f32[1,4096]{1,0:T(1,128)S(1)} %get-tuple-element.40.one), channel_id=1, source_target_pairs={{0,16},{16,0},{1,17},{17,1},{2,18},{18,2},{3,19},{19,3},{4,20},{20... | collective-permute-start | bytes 49160 | tf_op jit(solution)/shard_map/ppermute | solution.py:566
  29.4 9.4 %slice-start.1 = ((s8[8388608]{0:T(1024)(128)(4,1)}), s8[4194304]{0:T(1024)(128)(4,1)S(1)}, s32[]{:S(2)}) async-start(s8[8388608]{0:T(1024)(128)(4,1)} %bitcast.18), calls=%async_computation.8 | async-start | bytes 8388608
  29.4 9.3 %collective-permute-start.3 = (f32[1,4096]{1,0:T(1,128)S(1)}, f32[1,4096]{1,0:T(1,128)S(1)}, u32[]{:S(2)}, u32[]{:S(2)}) collective-permute-start(f32[1,4096]{1,0:T(1,128)S(1)} %add_parts.1.refs_1_), channel_id=1, source_target_pairs={{0,32},{32,64},{64,96},{96,0},{1,33},{33,65},{65,97},{97,1},{2,34}... | collective-permute-start | bytes 49160 | tf_op jit(solution)/shard_map/ppermute | solution.py:613
  30.7 8.0 %collective-permute-start.4 = (f32[1,4096]{1,0:T(1,128)S(1)}, f32[1,4096]{1,0:T(1,128)S(1)}, u32[]{:S(2)}, u32[]{:S(2)}) collective-permute-start(f32[1,4096]{1,0:T(1,128)S(1)} %add_parts.1.refs_1_), channel_id=1, source_target_pairs={{0,64},{32,96},{64,0},{96,32},{1,65},{33,97},{65,1},{97,33},{2,66}... | collective-permute-start | bytes 49160 | tf_op jit(solution)/shard_map/ppermute | solution.py:613
  33.2 5.6 %collective-permute-start.5 = (f32[1,4096]{1,0:T(1,128)S(1)}, f32[1,4096]{1,0:T(1,128)S(1)}, u32[]{:S(2)}, u32[]{:S(2)}) collective-permute-start(f32[1,4096]{1,0:T(1,128)S(1)} %add_parts.1.refs_1_), channel_id=1, source_target_pairs={{0,96},{32,0},{64,32},{96,64},{1,97},{33,1},{65,33},{97,65},{2,98}... | collective-permute-start | bytes 49160 | tf_op jit(solution)/shard_map/ppermute | solution.py:613
  92.2 11.9 %copy-start = (f32[8,1,5120]{2,1,0:T(1,128)}, f32[8,1,5120]{2,1,0:T(1,128)S(1)}, u32[]{:S(2)}) copy-start(f32[8,1,5120]{2,1,0:T(1,128)S(1)} %all_to_all.33.refs_1_.totals) | copy-start | bytes 491524
  97.9 22.6 %copy-start.3 = (f32[1,4096]{1,0:T(1,128)}, f32[1,4096]{1,0:T(1,128)S(1)}, u32[]{:S(2)}) copy-start(f32[1,4096]{1,0:T(1,128)S(1)} %get-tuple-element.66.scale) | copy-start | bytes 49156
  97.9 18.2 %collective-permute-start.6 = (f32[2,256,512]{2,1,0:T(8,128)S(1)}, f32[2,256,512]{2,1,0:T(8,128)}, u32[]{:S(2)}, u32[]{:S(2)}) collective-permute-start(f32[2,256,512]{2,1,0:T(8,128)S(1)} %get-tuple-element.57), channel_id=1, source_target_pairs={{0,8},{8,0},{1,9},{9,1},{2,10},{10,2},{3,11},{11,3},{4,12},{12,4},... | collective-permute-start | bytes 3145736 | tf_op jit(solution)/shard_map/ppermute | solution.py:566
  99.5 22.4 %all-to-all-start.4 = ((f32[64,2,1024]{2,1,0:T(2,128)}), f32[64,2,1024]{2,1,0:T(2,128)S(1)}, u32[]{:S(2)}, u32[]{:S(2)}) async-start(f32[64,2,1024]{2,1,0:T(2,128)} %get-tuple-element.63), calls=%async_computation.4 | async-start | bytes 1048576 | tf_op jit(solution)/shard_map/all_to_all | solution.py:562
  117.5 17.7 %collective-permute-start.7 = (f32[4,64,512]{2,1,0:T(8,128)S(1)}, f32[4,64,512]{2,1,0:T(8,128)S(1)}, u32[]{:S(2)}, u32[]{:S(2)}) collective-permute-start(f32[4,64,512]{2,1,0:T(8,128)S(1)} %bitcast.21), channel_id=1, source_target_pairs={{0,4},{4,0},{1,5},{5,1},{2,6},{6,2},{3,7},{7,3},{8,12},{12,8},{9,1... | collective-permute-start | bytes 1572872 | tf_op jit(solution)/shard_map/ppermute | solution.py:566
  120.4 1.5 collective-permute-start.11
  122.0 0.8 copy-start.6
  122.0 0.8 copy-start.7
  130.7 20.2 %all-to-all-start.5 = ((f32[16,16,1024]{2,1,0:T(8,128)}), f32[16,16,1024]{2,1,0:T(8,128)S(1)}, u32[]{:S(2)}, u32[]{:S(2)}) async-start(f32[16,16,1024]{2,1,0:T(8,128)} %get-tuple-element.69), calls=%async_computation.5 | async-start | bytes 2097152 | tf_op jit(solution)/shard_map/all_to_all | solution.py:562
  135.3 8.7 %collective-permute-start.10 = (f32[64,512]{1,0:T(8,128)S(1)}, f32[64,512]{1,0:T(8,128)S(1)}, u32[]{:S(2)}, u32[]{:S(2)}) collective-permute-start(f32[64,512]{1,0:T(8,128)S(1)} %get-tuple-element.76), channel_id=1, source_target_pairs={{0,3},{1,0},{2,1},{3,2},{4,7},{5,4},{6,5},{7,6},{8,11},{9,8},{10,9... | collective-permute-start | bytes 393224 | tf_op jit(solution)/shard_map/ppermute | solution.py:580
  137.8 8.7 %collective-permute-start.8 = (f32[64,512]{1,0:T(8,128)S(1)}, f32[64,512]{1,0:T(8,128)S(1)}, u32[]{:S(2)}, u32[]{:S(2)}) collective-permute-start(f32[64,512]{1,0:T(8,128)S(1)} %get-tuple-element.75), channel_id=1, source_target_pairs={{0,1},{1,2},{2,3},{3,0},{4,5},{5,6},{6,7},{7,4},{8,9},{9,10},{10,1... | collective-permute-start | bytes 393224 | tf_op jit(solution)/shard_map/ppermute | solution.py:580
  137.8 8.7 %collective-permute-start.9 = (f32[64,512]{1,0:T(8,128)S(1)}, f32[64,512]{1,0:T(8,128)S(1)}, u32[]{:S(2)}, u32[]{:S(2)}) collective-permute-start(f32[64,512]{1,0:T(8,128)S(1)} %get-tuple-element.77), channel_id=1, source_target_pairs={{0,2},{1,3},{2,0},{3,1},{4,6},{5,7},{6,4},{7,5},{8,10},{9,11},{10,... | collective-permute-start | bytes 393224 | tf_op jit(solution)/shard_map/ppermute | solution.py:580
  140.4 3.0 %collective-permute-start.12 = (f32[1,128]{1,0:T(1,128)}, f32[1,128]{1,0:T(1,128)S(1)}, u32[]{:S(2)}, u32[]{:S(2)}) collective-permute-start(f32[1,128]{1,0:T(1,128)} %get-tuple-element.70), channel_id=1, source_target_pairs={{0,16},{16,0},{1,17},{17,1},{2,18},{18,2},{3,19},{19,3},{4,20},{20... | collective-permute-start | bytes 1544 | tf_op jit(solution)/shard_map/ppermute | solution.py:566
Sparse Core Ops, SparseCore 0:
  10.6 54.0 all-gather.1
